TPU v7x, 128 devices: a whole 4x4x4 slice. The times are simulated.
128 devices in a mesh: ctx: 16 (over x, y), head: 8 (over z, core).
Axes of the slice: x: 4, y: 4, z: 4, core: 2. Of those that a mesh axis runs over, the one named last changes fastest.
Arguments:
- queries: bfloat16 [16384, 4096], P(('ctx', 'head')), may hold values from -12 to 12
- keys: bfloat16 [16384, 4096], P(('ctx', 'head')), may hold values from -6 to 6
- values: bfloat16 [16384, 4096], P(('ctx', 'head')), may hold values from -6 to 6
- grad_out: bfloat16 [16384, 4096], P(('ctx', 'head')), may hold values from -6 to 6
- local_blocks: int32 [128, 4], P('ctx'), may hold values from 0 to 7, as said below
- summary_blocks: int32 [16, 1], P('ctx'), may hold values from 0 to 7, as said below
Outputs:
- attended: bfloat16 [16384, 4096], P(('ctx', 'head'))
- grad_queries: bfloat16 [16384, 4096], P(('ctx', 'head'))
- grad_keys: bfloat16 [16384, 4096], P(('ctx', 'head'))
- grad_values: bfloat16 [16384, 4096], P(('ctx', 'head'))
Inputs may be any that keep to these rules, and one draw needn't show every extreme that they name: `local_blocks`: each row names 4 different blocks, numbered within the query block's own span; its first entry is the query block itself. `summary_blocks`: each row names the one block of that span that serves as its summary, numbered within that span.
All inputs are finite; a program needn't handle non-finite values.
Results may differ from a plain program's by a relative error of at most 0.015.
Values may be sent and summed in bfloat16 or wider, within the bound.
No kernel may reach another device: no remote copies, remote signals or barrier semaphores. Data moves between devices by JAX's collectives and lax.ppermute only.
A program may use at most 128 MiB of HBM per device.

v0:
```python
from functools import partial

import jax
import jax.numpy as jnp
from jax import lax
from jax.sharding import PartitionSpec as P

DH = 128
BLK = 128


NEGATIVE_PADDING = -1e30


def split_heads(matrix, head_count):
    return matrix.reshape(matrix.shape[0], head_count, -1).transpose(1, 0, 2)


def join_heads(stacked):
    return stacked.transpose(1, 0, 2).reshape(stacked.shape[1], -1)


def score_pair(head_queries, nearby_keys, distant_keys, valid_mask, logit_scale):
    nearby_logits = (
        jnp.einsum("cgu,cfu->cgf", head_queries, nearby_keys, preferred_element_type=jnp.float32)
        * logit_scale
    )
    distant_logits = (
        jnp.einsum("xra,ga->xrg", head_queries, distant_keys, preferred_element_type=jnp.float32)
        * logit_scale
    )
    return (nearby_logits, jnp.where(valid_mask, distant_logits, NEGATIVE_PADDING))


def forward_head(inputs, valid_mask, logit_scale):
    head_queries, nearby_keys, nearby_values, distant_keys, distant_values = inputs
    nearby_logits, distant_logits = score_pair(
        head_queries, nearby_keys, distant_keys, valid_mask, logit_scale
    )
    row_top = jnp.maximum(nearby_logits.max(-1), distant_logits.max(-1))
    row_total = jnp.exp(nearby_logits - row_top[..., None]).sum(-1) + jnp.exp(
        distant_logits - row_top[..., None]
    ).sum(-1)
    log_total = row_top + jnp.log(row_total)
    nearby_probs = jnp.exp(nearby_logits - log_total[..., None]).astype(jnp.bfloat16)
    distant_probs = jnp.exp(distant_logits - log_total[..., None]).astype(jnp.bfloat16)
    combined_output = jnp.einsum(
        "ufm,umo->ufo", nearby_probs, nearby_values, preferred_element_type=jnp.float32
    )
    combined_output = combined_output + jnp.einsum(
        "egz,zy->egy", distant_probs, distant_values, preferred_element_type=jnp.float32
    )
    return (combined_output.astype(jnp.bfloat16), log_total)


def backward_head(inputs, valid_mask, logit_scale):
    (
        head_queries,
        nearby_keys,
        nearby_values,
        distant_keys,
        distant_values,
        upstream_gradient,
        attended,
        log_total,
    ) = inputs
    nearby_logits, distant_logits = score_pair(
        head_queries, nearby_keys, distant_keys, valid_mask, logit_scale
    )
    near_p = jnp.exp(nearby_logits - log_total[..., None])
    far_p = jnp.exp(distant_logits - log_total[..., None])
    delta = jnp.sum(upstream_gradient.astype(jnp.float32) * attended.astype(jnp.float32), -1)
    nearby_prob_gradient = jnp.einsum(
        "cgu,cfu->cgf", upstream_gradient, nearby_values, preferred_element_type=jnp.float32
    )
    distant_prob_gradient = jnp.einsum(
        "xra,ga->xrg", upstream_gradient, distant_values, preferred_element_type=jnp.float32
    )
    nearby_score_gradient = (
        near_p * (nearby_prob_gradient - delta[..., None]) * logit_scale
    ).astype(jnp.bfloat16)
    distant_score_gradient = (
        far_p * (distant_prob_gradient - delta[..., None]) * logit_scale
    ).astype(jnp.bfloat16)
    query_gradient = jnp.einsum(
        "ufm,umo->ufo", nearby_score_gradient, nearby_keys, preferred_element_type=jnp.float32
    )
    query_gradient = (
        query_gradient
        + jnp.einsum(
            "egz,zy->egy", distant_score_gradient, distant_keys, preferred_element_type=jnp.float32
        )
    ).astype(jnp.bfloat16)
    nearby_probs = near_p.astype(jnp.bfloat16)
    distant_probs = far_p.astype(jnp.bfloat16)
    nearby_key_gradient = jnp.einsum(
        "enp,ens->eps", nearby_score_gradient, head_queries, preferred_element_type=jnp.float32
    )
    nearby_value_gradient = jnp.einsum(
        "enp,ens->eps", nearby_probs, upstream_gradient, preferred_element_type=jnp.float32
    )
    distant_key_gradient = jnp.einsum(
        "fce,fcx->ex", distant_score_gradient, head_queries, preferred_element_type=jnp.float32
    )
    distant_value_gradient = jnp.einsum(
        "fce,fcx->ex", distant_probs, upstream_gradient, preferred_element_type=jnp.float32
    )
    return (
        query_gradient,
        nearby_key_gradient,
        nearby_value_gradient,
        distant_key_gradient,
        distant_value_gradient,
    )


def local(queries, keys, values, grad_out, local_blocks, summary_blocks):
    groups = lax.axis_size("head")
    head_count = queries.shape[1] // DH // groups
    span_index = lax.axis_index("ctx")
    logit_scale = DH ** (-0.5)
    query_rows, key_rows, value_rows, cot_rows = (
        lax.all_to_all(queries, "head", split_axis=1, concat_axis=0, tiled=True),
        lax.all_to_all(keys, "head", split_axis=1, concat_axis=0, tiled=True),
        lax.all_to_all(values, "head", split_axis=1, concat_axis=0, tiled=True),
        lax.all_to_all(grad_out, "head", split_axis=1, concat_axis=0, tiled=True),
    )
    span_len = query_rows.shape[0]
    features = query_rows.shape[1]
    nblocks = span_len // BLK
    near_len = local_blocks.shape[1] * BLK
    key_blocks = key_rows.reshape(nblocks, BLK, features)
    value_blocks = value_rows.reshape(nblocks, BLK, features)
    own_k = key_blocks[summary_blocks[0]].reshape(-1, features)
    own_v = value_blocks[summary_blocks[0]].reshape(-1, features)
    summary_len = own_k.shape[0]
    sum_k, sum_v = (
        lax.all_gather(own_k, "ctx", axis=0, tiled=True),
        lax.all_gather(own_v, "ctx", axis=0, tiled=True),
    )
    valid_mask = jnp.arange(sum_k.shape[0], dtype=jnp.int32) // summary_len < span_index

    def per_head(matrix, block_len):
        return split_heads(matrix, head_count).reshape(head_count, -1, block_len, DH)

    head_queries = per_head(query_rows, BLK)
    nearby_keys = per_head(key_blocks[local_blocks].reshape(-1, features), near_len)
    nearby_values = per_head(value_blocks[local_blocks].reshape(-1, features), near_len)
    distant_keys = split_heads(sum_k, head_count)
    distant_values = split_heads(sum_v, head_count)
    attended_h, log_total = lax.map(
        partial(forward_head, valid_mask=valid_mask, logit_scale=logit_scale),
        (head_queries, nearby_keys, nearby_values, distant_keys, distant_values),
    )
    attended_rows = join_heads(attended_h.reshape(head_count, span_len, DH))
    upstream_gradient = per_head(cot_rows, BLK)
    (
        query_gradient,
        nearby_key_gradient,
        nearby_value_gradient,
        distant_key_gradient,
        distant_value_gradient,
    ) = lax.map(
        partial(backward_head, valid_mask=valid_mask, logit_scale=logit_scale),
        (
            head_queries,
            nearby_keys,
            nearby_values,
            distant_keys,
            distant_values,
            upstream_gradient,
            attended_h,
            log_total,
        ),
    )
    block_ids = jnp.arange(nblocks, dtype=jnp.int32)[:, None]
    placing = (local_blocks.reshape(-1)[None, :] == block_ids).astype(jnp.float32)
    dk_local = jnp.einsum(
        "tj,hjx->htx",
        placing,
        nearby_key_gradient.reshape(head_count, -1, BLK * DH),
        precision=lax.Precision.HIGHEST,
    )
    dv_local = jnp.einsum(
        "tj,hjx->htx",
        placing,
        nearby_value_gradient.reshape(head_count, -1, BLK * DH),
        precision=lax.Precision.HIGHEST,
    )
    own_dk, own_dv = (
        lax.psum_scatter(
            join_heads(distant_key_gradient).astype(jnp.bfloat16),
            "ctx",
            scatter_dimension=0,
            tiled=True,
        ).astype(jnp.float32),
        lax.psum_scatter(
            join_heads(distant_value_gradient).astype(jnp.bfloat16),
            "ctx",
            scatter_dimension=0,
            tiled=True,
        ).astype(jnp.float32),
    )
    owning = (summary_blocks[0][None, :] == block_ids).astype(jnp.float32)
    add_k = jnp.dot(
        owning, own_dk.reshape(-1, BLK * features), precision=lax.Precision.HIGHEST
    ).reshape(span_len, features)
    add_v = jnp.dot(
        owning, own_dv.reshape(-1, BLK * features), precision=lax.Precision.HIGHEST
    ).reshape(span_len, features)
    grad_k_rows = (join_heads(dk_local.reshape(head_count, span_len, DH)) + add_k).astype(
        jnp.bfloat16
    )
    grad_v_rows = (join_heads(dv_local.reshape(head_count, span_len, DH)) + add_v).astype(
        jnp.bfloat16
    )
    grad_q_rows = join_heads(query_gradient.reshape(head_count, span_len, DH))
    attended_tok, grad_q_tok, grad_k_tok, grad_v_tok = (
        lax.all_to_all(attended_rows, "head", split_axis=0, concat_axis=1, tiled=True),
        lax.all_to_all(grad_q_rows, "head", split_axis=0, concat_axis=1, tiled=True),
        lax.all_to_all(grad_k_rows, "head", split_axis=0, concat_axis=1, tiled=True),
        lax.all_to_all(grad_v_rows, "head", split_axis=0, concat_axis=1, tiled=True),
    )
    return (attended_tok, grad_q_tok, grad_k_tok, grad_v_tok)


def solution(mesh):
    placed = (
        P(("ctx", "head"), None),
        P(("ctx", "head"), None),
        P(("ctx", "head"), None),
        P(("ctx", "head"), None),
        P("ctx", None),
        P("ctx", None),
    )
    return jax.shard_map(
        local,
        mesh=mesh,
        in_specs=placed,
        out_specs=(
            P(("ctx", "head"), None),
            P(("ctx", "head"), None),
            P(("ctx", "head"), None),
            P(("ctx", "head"), None),
        ),
        check_vma=False,
    )
```

profile of v0, /device:TPU:2, one launch (start us, length us, event | category | flops | bytes accessed | tf_op | source)
XLA Modules:
  0.0 465.5 jit_solution(17480612421457703559)
XLA Ops:
  10.2 5.3 %all-to-all-start.1 = ((bf16[128,8,512]{2,0,1:T(8,128)(2,1)}), bf16[128,8,512]{2,0,1:T(8,128)(2,1)S(1)}, u32[]{:S(2)}, u32[]{:S(2)}) async-start(bf16[128,8,512]{2,0,1:T(8,128)(2,1)} %copy.93), calls=%async_computation.1 | async-start | bytes 2097152 | tf_op jit(solution)/shard_map/all_to_all | solution.py:124
  16.2 15.3 %all-to-all-done.1 = bf16[128,8,512]{2,0,1:T(8,128)(2,1)S(1)} async-done(((bf16[128,8,512]{2,0,1:T(8,128)(2,1)}), bf16[128,8,512]{2,0,1:T(8,128)(2,1)S(1)}, u32[]{:S(2)}, u32[]{:S(2)}) %all-to-all-start.1) | async-done | bytes 1048608 | tf_op jit(solution)/shard_map/all_to_all | solution.py:124
  33.4 18.5 %all_to_all.134 = bf16[128,8,512]{2,0,1:T(8,128)(2,1)S(1)} all-to-all(bf16[128,8,512]{2,0,1:T(8,128)(2,1)S(1)} %copy.98), channel_id=1, replica_groups=mesh['ctx'=16,'head'=8] {'head'}, dimensions={1} | all-to-all | bytes 2097152 | tf_op jit(solution)/shard_map/all_to_all | solution.py:125
  60.7 13.6 %all-to-all-done = bf16[128,8,512]{0,2,1:T(8,128)(2,1)S(1)} async-done(((bf16[128,8,512]{0,2,1:T(8,128)(2,1)}), bf16[128,8,512]{0,2,1:T(8,128)(2,1)S(1)}, u32[]{:S(2)}, u32[]{:S(2)}) %all-to-all-start) | async-done | bytes 1048608 | tf_op jit(solution)/shard_map/all_to_all | solution.py:123
  74.4 4.2 all-to-all-start.4
  82.1 7.0 %reshape.288 = bf16[4096,4,128]{2,1,0:T(4,128)(2,1)} reshape(bf16[32,128,512]{2,1,0:T(8,128)(2,1)} %gather_fusion) | data formatting | bytes 8388608 | tf_op jit(solution)/shard_map/reshape;reshape | solution.py:16
  89.1 4.7 %copy.143 = bf16[4096,4,128]{2,0,1:T(8,128)(2,1)} copy(bf16[4096,4,128]{2,1,0:T(4,128)(2,1)} %reshape.288) | data formatting | bytes 8388608 | tf_op jit(solution)/shard_map/transpose | solution.py:16
  96.6 6.9 %reshape.289 = bf16[4096,4,128]{2,1,0:T(4,128)(2,1)} reshape(bf16[32,128,512]{2,1,0:T(8,128)(2,1)} %gather_fusion.1) | data formatting | bytes 8388608 | tf_op jit(solution)/shard_map/reshape;reshape | solution.py:16
  103.5 4.7 %copy.144 = bf16[4096,4,128]{2,0,1:T(8,128)(2,1)} copy(bf16[4096,4,128]{2,1,0:T(4,128)(2,1)} %reshape.289) | data formatting | bytes 8388608 | tf_op jit(solution)/shard_map/transpose | solution.py:16
  113.8 3.9 copy.96
  122.7 3.9 copy.100
  126.6 4.0 copy.105
  131.8 44.5 %while.34 = (s32[]{:T(128)}, bf16[4,8,128,128]{3,2,1,0:T(8,128)(2,1)}, f32[4,8,128]{2,1,0:T(8,128)S(1)}, bf16[4,8,128,128]{3,2,1,0:T(8,128)(2,1)S(1)}, bf16[4,8,...) while((s32[]{:T(128)}, ...), condition=%wide.region_5.6_spmd.clone, body=%wide.region_0.5_spmd.clone.sunk | while | flops 1369719808 | bytes 36515436 | solution.py:151
  177.5 79.5 %while.35 = (s32[]{:T(128)}, bf16[4,8,128,128]{3,2,1,0:T(8,128)(2,1)}, f32[4,8,512,128]{3,2,1,0:T(8,128)}, f32[4,8,512,128]{3,2,1,0:T(8,128)}, bf16[4,2048,128]{...) while((s32[]{:T(128)}, ...), condition=%wide.region_8.9_spmd.clone, body=%wide.region_6.8_spmd.clone.sunk | while | flops 3384034304 | bytes 116706640 | solution.py:163
  180.1 4.1 multiply_convert_fusion.5
  200.1 4.1 multiply_convert_fusion.5
  219.9 4.1 multiply_convert_fusion.5
  239.6 4.1 multiply_convert_fusion.5
  256.9 4.1 copy.136
  265.7 4.4 all-to-all-start.5
  270.3 9.5 %reshape.200 = f32[4,32,16384]{2,1,0:T(8,128)} reshape(f32[4,8,512,128]{3,2,1,0:T(8,128)} %get-tuple-element.136) | data formatting | bytes 16777216 | tf_op jit(solution)/shard_map/reshape | solution.py:181
  281.8 4.3 all-to-all-done.5
  286.1 4.5 all-to-all-start.3
  290.5 7.6 %convolution_bitcast_fusion.2 = f32[4,8,16384]{2,1,0:T(8,128)} fusion(f32[4,32,16384]{2,1,0:T(8,128)} %reshape.200, s32[32]{0:T(128)S(1)} %eq.39), kind=kOutput, calls=%fused_computation.126 | convolution fusion | flops 201326848 | bytes 10485888 | tf_op jit(solution)/shard_map/tj,hjx->htx/dot_general | solution.py:178
  303.8 9.5 %reshape.203 = f32[4,32,16384]{2,1,0:T(8,128)} reshape(f32[4,8,512,128]{3,2,1,0:T(8,128)} %get-tuple-element.138) | data formatting | bytes 16777216 | tf_op jit(solution)/shard_map/reshape | solution.py:187
  313.3 7.5 %convolution_bitcast_fusion.1 = f32[4,8,16384]{2,1,0:T(8,128)} fusion(f32[4,32,16384]{2,1,0:T(8,128)} %reshape.203, s32[32]{0:T(128)S(1)} %eq.39), kind=kOutput, calls=%fused_computation.125 | convolution fusion | flops 201326848 | bytes 10485888 | tf_op jit(solution)/shard_map/tj,hjx->htx/dot_general | solution.py:184
  329.8 5.3 %reduce-scatter.7.cloned.1.call-done = bf16[128,512]{1,0:T(8,128)(2,1)} async-done(((bf16[2048,512]{1,0:T(8,128)(2,1)}), bf16[128,512]{1,0:T(8,128)(2,1)}) %reduce-scatter.7.cloned.1.call-update) | async-done | bytes 131088
  336.2 76.1 %reduce-scatter.9.cloned.1.call-done = bf16[128,512]{1,0:T(8,128)(2,1)} async-done(((bf16[2048,512]{1,0:T(8,128)(2,1)}), bf16[128,512]{1,0:T(8,128)(2,1)}) %reduce-scatter.9.cloned.1.call-update) | async-done | bytes 131088
  417.6 4.4 all-to-all-start.6
  423.1 14.8 %all-to-all-done.6 = bf16[8,128,512]{1,2,0:T(8,128)(2,1)S(1)} async-done(((bf16[8,128,512]{1,2,0:T(8,128)(2,1)}), bf16[8,128,512]{1,2,0:T(8,128)(2,1)S(1)}, u32[]{:S(2)}, u32[]{:S(2)}) %all-to-all-start.6) | async-done | bytes 1048608 | tf_op jit(solution)/shard_map/all_to_all | solution.py:221
  438.0 3.6 all-to-all-start.7
  446.4 11.0 %all-to-all-done.7 = bf16[8,128,512]{1,2,0:T(8,128)(2,1)S(1)} async-done(((bf16[8,128,512]{1,2,0:T(8,128)(2,1)}), bf16[8,128,512]{1,2,0:T(8,128)(2,1)S(1)}, u32[]{:S(2)}, u32[]{:S(2)}) %all-to-all-start.7) | async-done | bytes 1048608 | tf_op jit(solution)/shard_map/all_to_all | solution.py:222
  (214 shorter events, 174.5 us)
Async XLA Ops:
  7.2 25.1 %copy-start.10 = (bf16[128,4096]{1,0:T(8,128)(2,1)S(1)}, bf16[128,4096]{1,0:T(8,128)(2,1)}, u32[]{:S(2)}) copy-start(bf16[128,4096]{1,0:T(8,128)(2,1)} %param.12) | copy-start | bytes 3145732
  10.2 21.3 %all-to-all-start.1 = ((bf16[128,8,512]{2,0,1:T(8,128)(2,1)}), bf16[128,8,512]{2,0,1:T(8,128)(2,1)S(1)}, u32[]{:S(2)}, u32[]{:S(2)}) async-start(bf16[128,8,512]{2,0,1:T(8,128)(2,1)} %copy.93), calls=%async_computation.1 | async-start | bytes 2097152 | tf_op jit(solution)/shard_map/all_to_all | solution.py:124
  15.5 98.3 %all-gather.5.cloned.1.call-start = ((), (), s32[]{:S(2)}) async-start(), calls=%async_computation.10 | async-start | bytes 2228224 | tf_op jit(solution)/shard_map/all_gather | solution.py:138
  32.2 90.5 %all-gather.7.cloned.1.call-start = ((), (), s32[]{:S(2)}) async-start(), calls=%async_computation.11 | async-start | bytes 2228224 | tf_op jit(solution)/shard_map/all_gather | solution.py:139
  52.6 26.5 %copy-start.11 = (s32[8,4]{0,1:T(4,128)S(1)}, s32[8,4]{0,1:T(4,128)}, u32[]{:S(2)}) copy-start(s32[8,4]{0,1:T(4,128)} %param.14) | copy-start | bytes 388
  54.9 19.5 %all-to-all-start = ((bf16[128,8,512]{0,2,1:T(8,128)(2,1)}), bf16[128,8,512]{0,2,1:T(8,128)(2,1)S(1)}, u32[]{:S(2)}, u32[]{:S(2)}) async-start(bf16[128,8,512]{0,2,1:T(8,128)(2,1)} %bitcast.287), calls=%async_computation | async-start | bytes 2097152 | tf_op jit(solution)/shard_map/all_to_all | solution.py:123
  74.4 35.7 %all-to-all-start.4 = ((bf16[128,8,512]{0,2,1:T(8,128)(2,1)}), bf16[128,8,512]{0,2,1:T(8,128)(2,1)}, u32[]{:S(2)}, u32[]{:S(2)}) async-start(bf16[128,8,512]{0,2,1:T(8,128)(2,1)} %bitcast.283), calls=%async_computation.4 | async-start | bytes 2097152 | tf_op jit(solution)/shard_map/all_to_all | solution.py:126
  78.6 256.5 %reduce-scatter.7.cloned.1.call-start = ((), (), s32[]{:S(2)}) async-start(), calls=%async_computation.12 | async-start | bytes 2228224
  180.1 4.2 copy-start
  187.1 2.0 copy-start.5
  189.2 2.9 copy-start.7
  190.0 2.1 copy-start.6
  200.1 4.2 copy-start
  207.1 2.0 copy-start.5
  209.1 2.7 copy-start.7
  219.8 4.2 copy-start
  226.9 2.0 copy-start.5
  228.9 2.8 copy-start.7
  239.6 4.2 copy-start
  246.6 2.0 copy-start.5
  248.7 2.8 copy-start.7
  249.5 2.0 copy-start.6
  256.9 4.2 copy-start.9
  261.0 2.7 copy-start.3
  261.1 151.2 %reduce-scatter.9.cloned.1.call-start = ((), (), s32[]{:S(2)}) async-start(), calls=%async_computation.13 | async-start | bytes 2228224
  263.7 6.4 %copy-start.12 = (s32[8,4]{0,1:T(4,128)S(1)}, s32[8,4]{0,1:T(4,128)}, u32[]{:S(2)}) copy-start(s32[8,4]{0,1:T(4,128)} %param.14) | copy-start | bytes 388
  265.7 20.4 %all-to-all-start.5 = ((bf16[8,128,512]{1,2,0:T(8,128)(2,1)}), bf16[8,128,512]{1,2,0:T(8,128)(2,1)S(1)}, u32[]{:S(2)}, u32[]{:S(2)}) async-start(bf16[8,128,512]{1,2,0:T(8,128)(2,1)} %copy.117), calls=%async_computation.5 | async-start | bytes 2097152 | tf_op jit(solution)/shard_map/all_to_all | solution.py:220
  270.3 9.6 %copy-start.2 = (bf16[4,8,128,128]{3,2,1,0:T(8,128)(2,1)S(1)}, bf16[4,8,128,128]{3,2,1,0:T(8,128)(2,1)}, u32[]{:S(2)}) copy-start(bf16[4,8,128,128]{3,2,1,0:T(8,128)(2,1)} %get-tuple-element.597) | copy-start | bytes 3145732
  286.1 131.5 %all-to-all-start.3 = ((bf16[8,128,512]{1,2,0:T(8,128)(2,1)}), bf16[8,128,512]{1,2,0:T(8,128)(2,1)}, u32[]{:S(2)}, u32[]{:S(2)}) async-start(bf16[8,128,512]{1,2,0:T(8,128)(2,1)} %copy.107), calls=%async_computation.3 | async-start | bytes 2097152 | tf_op jit(solution)/shard_map/all_to_all | solution.py:219
  416.5 5.5 %copy-start.4 = (bf16[8,128,512]{1,0,2:T(8,128)(2,1)S(1)}, bf16[8,128,512]{1,0,2:T(8,128)(2,1)}, u32[]{:S(2)}) copy-start(bf16[8,128,512]{1,0,2:T(8,128)(2,1)} %get-tuple-element.350) | copy-start | bytes 3145732
  417.6 20.4 %all-to-all-start.6 = ((bf16[8,128,512]{1,2,0:T(8,128)(2,1)}), bf16[8,128,512]{1,2,0:T(8,128)(2,1)S(1)}, u32[]{:S(2)}, u32[]{:S(2)}) async-start(bf16[8,128,512]{1,2,0:T(8,128)(2,1)} %copy.121), calls=%async_computation.6 | async-start | bytes 2097152 | tf_op jit(solution)/shard_map/all_to_all | solution.py:221
  438.0 19.5 %all-to-all-start.7 = ((bf16[8,128,512]{1,2,0:T(8,128)(2,1)}), bf16[8,128,512]{1,2,0:T(8,128)(2,1)S(1)}, u32[]{:S(2)}, u32[]{:S(2)}) async-start(bf16[8,128,512]{1,2,0:T(8,128)(2,1)} %copy.124), calls=%async_computation.7 | async-start | bytes 2097152 | tf_op jit(solution)/shard_map/all_to_all | solution.py:222
  (10 other events, 14.2 us)
Sparse Core Ops, SparseCore 0:
  32.3 43.9 all-gather.4
  78.4 44.1 all-gather.6
  261.2 73.8 reduce-scatter.6
  338.6 73.6 reduce-scatter.8
where the time goes:
time: 472 us; the launch traced here: 465 us
  waiting for transfers between devices  142 us (30%)
  local copies, waits for them, and re-layouts  122 us (26%)
  matrix products  118 us (25%)
  starting transfers between devices  30.6 us (6%)
  blocking collectives  18.5 us (4%)
  other arithmetic  17.9 us (4%)
  between operations  15 us (3%)
    unnamed x6, waiting for transfers between devices  81.5 us
    unnamed x37, local copies, waits for them, and re-layouts  38.2 us
    all_to_all x1, blocking collectives, local(): lax.all_to_all(values, 'head', split_axis=1, concat_axis=0, tiled=True)  18.5 us
    dot_general x4, matrix products, backward_head(): jnp.einsum('xra,ga->xrg', upstream_gradient, distant_values, preferred_el...  16.5 us
    all_to_all x1, waiting for transfers between devices, local(): lax.all_to_all(keys, 'head', split_axis=1, concat_axis=0, tiled=True)  15.3 us
    all_to_all x1, waiting for transfers between devices, local(): lax.all_to_all(grad_k_rows, 'head', split_axis=0, concat_axis=1, tiled=True)  14.8 us
    another operation x2, local copies, waits for them, and re-layouts, split_heads(): return matrix.reshape(matrix.shape[0], head_count, -1).transpose(1, 0, 2)  13.9 us
    all_to_all x1, waiting for transfers between devices, local(): lax.all_to_all(queries, 'head', split_axis=1, concat_axis=0, tiled=True)  13.6 us
  transfers between devices with their start and end apart: 11, of which 8 were waited for; matrix products, arithmetic and copies ran while one was open for 25% of the time, Pallas kernels for 0%

commit v1 on v0

v1 whole, which is shorter than its diff:
```python
import jax
import jax.numpy as jnp
from jax import lax
from jax.experimental import pallas as pl
from jax.experimental.pallas import tpu as pltpu
from jax.sharding import PartitionSpec as P

BLK = 128
NB = 8
SPAN = 1024
SCALE = 128 ** -0.5
LOG2E = 1.4426950408889634
NEG = -1e30
QT = 256
bf16 = jnp.bfloat16
f32 = jnp.float32


def dot_nt(a, b):
    return lax.dot_general(a, b, (((1,), (1,)), ((), ())), preferred_element_type=f32)


def dot_nn(a, b):
    return lax.dot_general(a, b, (((1,), (0,)), ((), ())), preferred_element_type=f32)


def fold_max(s):
    return s.reshape(s.shape[0] // 8, 8, s.shape[1]).max(0)


def fold_sum(s):
    return s.reshape(s.shape[0] // 8, 8, s.shape[1]).sum(0)


def attention_kernel(
    pos, local, kv, qg, k0, k1, k2, k3, v0, v1, v2, v3,
    ao, dl, dsum, fk, fv,
    kf, vf, kt, vt, kl, vl, klt, vlt, s_ref, p_ref, d_ref, mx, sm, ot, dqt, dk_acc, dv_acc, gs, qs,
):
    x, y, sb = pos[0], pos[1], pos[2]
    ks, vs = (k0, k1, k2, k3), (v0, v1, v2, v3)
    for sx in range(4):
        for sy in range(4):
            kf[sx, sy * BLK:(sy + 1) * BLK, :] = ks[sx][sy]
            vf[sx, sy * BLK:(sy + 1) * BLK, :] = vs[sy][sx]
    mx[...] = jnp.full_like(mx, NEG)
    sm[...] = jnp.zeros_like(sm)
    ot[...] = jnp.zeros_like(ot)
    dqt[...] = jnp.zeros_like(dqt)
    dk_acc[...] = jnp.zeros_like(dk_acc)
    dv_acc[...] = jnp.zeros_like(dv_acc)

    def queries(t, n=2):
        return qg[t * n:(t + 1) * n, 0].reshape(n * BLK, BLK)

    def cots(t, n=2):
        return qg[t * n:(t + 1) * n, 1].reshape(n * BLK, BLK)

    def score_far(sx, first):
        kt[sx] = kf[sx].T
        vt[sx] = vf[sx].T
        for t in range(4):
            cols = slice(t * QT, (t + 1) * QT)
            s = dot_nt(kf[sx], queries(t))
            s_ref[sx, :, cols] = s
            if first:
                top = jnp.full((8, QT), NEG, f32)
                for sy in range(1, 4):
                    top = jnp.maximum(top, jnp.where(sy <= y, fold_max(s[sy * BLK:(sy + 1) * BLK]), NEG))
            else:
                top = fold_max(s)
            mx[:, cols] = jnp.maximum(mx[:, cols], top)

    score_far(0, True)
    pl.loop(1, x + 1)(lambda sx: score_far(sx, False))

    @pl.loop(0, NB)
    def _(b):
        for i in range(4):
            idx = local[b * 4 + i]
            kl[b, i * BLK:(i + 1) * BLK, :] = kv[idx, 0]
            vl[b, i * BLK:(i + 1) * BLK, :] = kv[idx, 1]
        klt[b] = kl[b].T
        vlt[b] = vl[b].T
        cols = pl.ds(pl.multiple_of(b * BLK, BLK), BLK)
        s = dot_nt(kl[b], qg[b, 0])
        s_ref[4, :, cols] = s
        mx[:, cols] = jnp.maximum(mx[:, cols], fold_max(s))

    mc = mx[...].max(0, keepdims=True) * (SCALE * LOG2E)

    def prob_far(sx, first):
        for t in range(4):
            cols = slice(t * QT, (t + 1) * QT)
            total = sm[:, cols]
            for sy in range(4):
                rows = slice(sy * BLK, (sy + 1) * BLK)
                shift = mc[:, cols]
                if first:
                    shift = jnp.where((sy >= 1) & (sy <= y), shift, -NEG)
                p = jnp.exp2(s_ref[sx, rows, cols] * (SCALE * LOG2E) - shift)
                total = total + fold_sum(p)
                p_ref[sx, rows, cols] = p.astype(bf16)
            sm[:, cols] = total
            ot[:, cols] += dot_nn(vt[sx], p_ref[sx, :, cols])

    prob_far(0, True)
    pl.loop(1, x + 1)(lambda sx: prob_far(sx, False))
    for b in range(NB):
        cols = slice(b * BLK, (b + 1) * BLK)
        p = jnp.exp2(s_ref[4, :, cols] * (SCALE * LOG2E) - mc[:, cols])
        sm[:, cols] += fold_sum(p)
        p_ref[4, :, cols] = p.astype(bf16)
        ot[:, cols] += dot_nn(vlt[b], p_ref[4, :, cols])

    inv = 1.0 / sm[...].sum(0, keepdims=True)
    deltas = []
    for b in range(NB):
        cols = slice(b * BLK, (b + 1) * BLK)
        o = (ot[:, cols] * inv[:, cols]).T.astype(bf16)
        ao[b, 0] = o
        g = qg[b, 1].astype(f32)
        column = jnp.broadcast_to(inv[:, cols], (BLK, BLK)).T
        gs[cols, :] = (g * column).astype(bf16)
        qs[cols, :] = (qg[b, 0].astype(f32) * (column * SCALE)).astype(bf16)
        deltas.append((g * o.astype(f32)).T.sum(0, keepdims=True))
    delta = jnp.concatenate(deltas, 1)

    def grad_far(sx):
        for t in range(4):
            cols = slice(t * QT, (t + 1) * QT)
            dp = dot_nt(vf[sx], cots(t))
            for sy in range(4):
                rows = slice(sy * BLK, (sy + 1) * BLK)
                d_ref[sx, rows, cols] = p_ref[sx, rows, cols] * (dp[rows] - delta[:, cols]).astype(bf16)
            dqt[:, cols] += dot_nn(kt[sx], d_ref[sx, :, cols])
        fv[:, sx] = dot_nn(p_ref[sx], gs[...]).reshape(4, BLK, BLK).astype(bf16)
        fk[sx] = dot_nn(d_ref[sx], qs[...]).reshape(4, BLK, BLK).astype(bf16)

    pl.loop(0, x + 1)(grad_far)
    for b in range(NB):
        cols = slice(b * BLK, (b + 1) * BLK)
        dp = dot_nt(vl[b], qg[b, 1])
        d_ref[4, :, cols] = p_ref[4, :, cols] * (dp - delta[:, cols]).astype(bf16)
        dqt[:, cols] += dot_nn(klt[b], d_ref[4, :, cols])
        dv = dot_nn(p_ref[4, :, cols], gs[cols, :])
        dk = dot_nn(d_ref[4, :, cols], qs[cols, :])
        for i in range(4):
            idx = local[b * 4 + i]
            dk_acc[idx] += dk[i * BLK:(i + 1) * BLK]
            dv_acc[idx] += dv[i * BLK:(i + 1) * BLK]
        ao[b, 1] = (dqt[:, cols] * (inv[:, cols] * SCALE)).T.astype(bf16)
    dl[:, 0] = dk_acc[...].astype(bf16)
    dl[:, 1] = dv_acc[...].astype(bf16)
    dsum[0] = dk_acc[sb]
    dsum[1] = dv_acc[sb]


def attention(pos, local, kv, qg, ks, vs):
    width = kv.shape[-1]
    heads = width // BLK
    pair = pl.BlockSpec((NB, 2, BLK, BLK), lambda h: (0, 0, 0, h))
    far = pl.BlockSpec((4, BLK, BLK), lambda h: (0, 0, h))
    smem = pl.BlockSpec(memory_space=pltpu.SMEM)
    return pl.pallas_call(
        attention_kernel,
        grid=(heads,),
        in_specs=[smem, smem, pair, pair] + [far] * 8,
        out_specs=[
            pair, pair,
            pl.BlockSpec((2, BLK, BLK), lambda h: (0, 0, h)),
            pl.BlockSpec((4, 4, BLK, BLK), lambda h: (0, 0, 0, h)),
            pl.BlockSpec((4, 4, BLK, BLK), lambda h: (0, 0, 0, h)),
        ],
        out_shape=[
            jax.ShapeDtypeStruct((NB, 2, BLK, width), bf16),
            jax.ShapeDtypeStruct((NB, 2, BLK, width), bf16),
            jax.ShapeDtypeStruct((2, BLK, width), f32),
            jax.ShapeDtypeStruct((4, 4, BLK, width), bf16),
            jax.ShapeDtypeStruct((4, 4, BLK, width), bf16),
        ],
        scratch_shapes=[
            pltpu.VMEM((4, 512, BLK), bf16), pltpu.VMEM((4, 512, BLK), bf16),
            pltpu.VMEM((4, BLK, 512), bf16), pltpu.VMEM((4, BLK, 512), bf16),
            pltpu.VMEM((NB, 512, BLK), bf16), pltpu.VMEM((NB, 512, BLK), bf16),
            pltpu.VMEM((NB, BLK, 512), bf16), pltpu.VMEM((NB, BLK, 512), bf16),
            pltpu.VMEM((5, 512, SPAN), f32), pltpu.VMEM((5, 512, SPAN), bf16), pltpu.VMEM((5, 512, SPAN), bf16),
            pltpu.VMEM((8, SPAN), f32), pltpu.VMEM((8, SPAN), f32),
            pltpu.VMEM((BLK, SPAN), f32), pltpu.VMEM((BLK, SPAN), f32),
            pltpu.VMEM((NB, BLK, BLK), f32), pltpu.VMEM((NB, BLK, BLK), f32),
            pltpu.VMEM((SPAN, BLK), bf16), pltpu.VMEM((SPAN, BLK), bf16),
        ],
        compiler_params=pltpu.CompilerParams(vmem_limit_bytes=56 << 20),
        cost_estimate=pl.CostEstimate(flops=heads * 12 * SPAN * 2432 * BLK, bytes_accessed=heads * (4 << 20), transcendentals=heads * SPAN * 2432),
    )(pos, local, kv, qg, *ks, *vs)


SIDE = 4


def along_x(array, step, rows=range(SIDE), wrap=False):
    pairs = []
    for x in rows:
        to = x + step
        if wrap:
            to %= SIDE
        if 0 <= to < SIDE:
            pairs += [(x * SIDE + y, to * SIDE + y) for y in range(SIDE)]
    return lax.ppermute(array, "ctx", pairs)


def along_y(array, step):
    return lax.ppermute(
        array, "ctx", [(x * SIDE + y, x * SIDE + (y + step) % SIDE) for x in range(SIDE) for y in range(SIDE)]
    )


def gather_keys(own):
    row = jnp.stack([own] + [along_y(own, s) for s in (1, 2, 3)])
    near = along_x(row, 1)
    last = along_x(row, 3)
    return (row, near, along_x(near, 1, (1, 2)), last)


def gather_values(own):
    column = jnp.stack([own] + [along_x(own, s) for s in (1, 2, 3)])
    near = along_y(column, 1)
    last = along_y(column, -1)
    return (column, near, along_y(near, 1), last)


def plus(*terms):
    total = terms[0].astype(f32)
    for term in terms[1:]:
        total = total + term.astype(f32)
    return total


def scatter_keys(parts):
    passed = along_x(parts[2], -1, (3, 2))
    last = along_x(parts[3], -3)
    near = along_x(plus(parts[1], passed).astype(bf16), -1)
    row = plus(parts[0], near, last).astype(bf16)
    return plus(row[0], *[along_y(row[s], -s) for s in (1, 2, 3)])


def scatter_values(parts):
    passed = along_y(parts[2], -1)
    last = along_y(parts[3], 1)
    near = along_y(plus(parts[1], passed).astype(bf16), -1)
    column = plus(parts[0], near, last).astype(bf16)
    return plus(column[0], *[along_x(column[s], -s) for s in (1, 2, 3)])


def exchange(array):
    return lax.all_to_all(array, "head", split_axis=0, concat_axis=0, tiled=True)


def to_groups(a, b):
    def cut(m):
        return m.reshape(BLK, NB, -1).transpose(1, 0, 2)

    return exchange(jnp.stack([cut(a), cut(b)], 1))


def to_tokens(pair):
    got = exchange(pair)
    return tuple(got[:, i].transpose(1, 0, 2).reshape(BLK, -1) for i in range(2))


def device_step(queries, keys, values, grad_out, local_blocks, summary_blocks):
    j = lax.axis_index("ctx")
    sb = summary_blocks[0, 0]
    kv = to_groups(keys, values)
    qg = to_groups(queries, grad_out)
    own = lax.dynamic_index_in_dim(kv, sb, 0, keepdims=False)
    ks = gather_keys(own[0])
    vs = gather_values(own[1])
    pos = jnp.stack([j // SIDE, j % SIDE, sb]).astype(jnp.int32)
    ao, dl, dsum, fk, fv = attention(pos, local_blocks.reshape(-1), kv, qg, ks, vs)
    attended, grad_q = to_tokens(ao)
    own_grad = (dsum + jnp.stack([scatter_keys(fk), scatter_values(fv)])).astype(bf16)
    dl = lax.dynamic_update_slice(dl, own_grad[None], (sb, 0, 0, 0))
    grad_k, grad_v = to_tokens(dl)
    return attended, grad_q, grad_k, grad_v


def solution(mesh):
    tokens = P(("ctx", "head"), None)
    return jax.shard_map(
        device_step,
        mesh=mesh,
        in_specs=(tokens,) * 4 + (P("ctx", None),) * 2,
        out_specs=(tokens,) * 4,
        check_vma=False,
    )
```

time: 472 us -> 251 us (0.53)
  matrix products: 118 us -> 0 us
  local copies, waits for them, and re-layouts: 122 us -> 24.5 us
  Pallas kernels: 0 us -> 45.7 us
  waiting for transfers between devices: 142 us -> 104 us
  starting transfers between devices: 30.6 us -> 63.1 us
  blocking collectives: 18.5 us -> 0 us
  between operations: 15 us -> 1.68 us
  other arithmetic: 17.9 us -> 9.85 us
    dot_general x58 -> x0, matrix products: 118 us -> none  [the longest x4 16.5 us: backward_head(): jnp.einsum('xra,ga->xrg', upstream_gradient, distant_values, preferred_el...]
    unnamed x6 -> x0, waiting for transfers between devices: 81.5 us -> none
    ppermute x0 -> x24, waiting for transfers between devices: none -> 60.3 us  [the longest x12 55.7 us: along_x(): return lax.ppermute(array, 'ctx', pairs)]
    pallas_call x0 -> x1, Pallas kernels: none -> 45.7 us  [attention(): pl.pallas_call(attention_kernel, grid=(heads,), in_specs=[smem, smem, pai...]
    ppermute x0 -> x24, starting transfers between devices: none -> 45.1 us  [the longest x12 25.5 us: along_x(): return lax.ppermute(array, 'ctx', pairs)]
    reshape x10 -> x5, local copies, waits for them, and re-layouts: 30.2 us -> 2.81 us  [the longest x4 2.13 us: cut(): return m.reshape(BLK, NB, -1).transpose(1, 0, 2)]
    unnamed x37 -> x23, local copies, waits for them, and re-layouts: 38.2 us -> 10.9 us
    all_to_all x1 -> x0, blocking collectives: 18.5 us -> none  [local(): lax.all_to_all(values, 'head', split_axis=1, concat_axis=0, tiled=True)]
  transfers between devices with their start and end apart: 11 -> 28, of which waited for: 8 -> 11; matrix products, arithmetic and copies ran while one was open for 25% -> 8% of each run, Pallas kernels for 0% -> 0%
where the time goes in v1:
time: 251 us; the launch traced here: 249 us
  waiting for transfers between devices  104 us (41%)
  starting transfers between devices  63.1 us (25%)
  Pallas kernels  45.7 us (18%)
  local copies, waits for them, and re-layouts  24.5 us (10%)
  other arithmetic  9.85 us (4%)
    ppermute x12, waiting for transfers between devices, along_x(): return lax.ppermute(array, 'ctx', pairs)  55.7 us
    pallas_call x1, Pallas kernels, attention(): pl.pallas_call(attention_kernel, grid=(heads,), in_specs=[smem, smem, pai...  45.7 us
    all_to_all x4, waiting for transfers between devices, exchange(): lax.all_to_all(array, 'head', split_axis=0, concat_axis=0, tiled=True)  43.7 us
    ppermute x12, starting transfers between devices, along_x(): return lax.ppermute(array, 'ctx', pairs)  25.5 us
    ppermute x12, starting transfers between devices, along_y(): lax.ppermute(array, 'ctx', [(x * SIDE + y, x * SIDE + (y + step) % SIDE)...  19.6 us
    all_to_all x4, starting transfers between devices, exchange(): lax.all_to_all(array, 'head', split_axis=0, concat_axis=0, tiled=True)  17.9 us
    unnamed x23, local copies, waits for them, and re-layouts  10.9 us
    transpose x6, local copies, waits for them, and re-layouts, to_tokens(): got[:, i].transpose(1, 0, 2).reshape(BLK, -1)  6.47 us
  transfers between devices with their start and end apart: 28, of which 11 were waited for; matrix products, arithmetic and copies ran while one was open for 8% of the time, Pallas kernels for 0%

profile of v1, /device:TPU:2, one launch (start us, length us, event | category | flops | bytes accessed | tf_op | source)
XLA Modules:
  0.0 248.8 jit_solution(11437517017775668905)
XLA Ops:
  0.6 1.6 copy.12
  2.8 1.6 copy.14
  6.5 5.4 %all-to-all-start = ((bf16[8,2,128,512]{3,2,1,0:T(8,128)(2,1)}), bf16[8,2,128,512]{3,2,1,0:T(8,128)(2,1)}, u32[]{:S(2)}, u32[]{:S(2)}) async-start(bf16[8,2,128,512]{3,2,1,0:T(8,128)(2,1)} %pad_maximum_fusion), calls=%async_computation | async-start | bytes 4194304 | tf_op jit(solution)/shard_map/all_to_all | solution.py:256
  13.2 1.6 copy.18
  16.9 22.4 %all-to-all-done.kv = bf16[8,2,128,512]{3,2,1,0:T(8,128)(2,1)} async-done(((bf16[8,2,128,512]{3,2,1,0:T(8,128)(2,1)}), bf16[8,2,128,512]{3,2,1,0:T(8,128)(2,1)}, u32[]{:S(2)}, u32[]{:S(2)}) %all-to-all-start) | async-done | bytes 2097184 | tf_op jit(solution)/shard_map/all_to_all | solution.py:256
  39.3 3.6 %all-to-all-start.1 = ((bf16[8,2,128,512]{3,2,1,0:T(8,128)(2,1)}), bf16[8,2,128,512]{3,2,1,0:T(8,128)(2,1)S(1)}, u32[]{:S(2)}, u32[]{:S(2)}) async-start(bf16[8,2,128,512]{3,2,1,0:T(8,128)(2,1)} %pad_maximum_fusion.1), calls=%async_computation.1 | async-start | bytes 4194304 | tf_op jit(solution)/shard_map/all_to_all | solution.py:256
  44.6 3.1 %collective-permute-start.2 = (bf16[128,512]{1,0:T(8,128)(2,1)S(1)}, bf16[128,512]{1,0:T(8,128)(2,1)S(1)}, u32[]{:S(2)}, u32[]{:S(2)}) collective-permute-start(bf16[128,512]{1,0:T(8,128)(2,1)S(1)} %get-tuple-element.28), channel_id=1, source_target_pairs={{0,24},{8,0},{16,8},{24,16},{32,56},{40,32},{48,40},{56,48},{64,88... | collective-permute-start | bytes 393224 | tf_op jit(solution)/shard_map/ppermute | solution.py:213
  49.9 4.7 %collective-permute-start.7 = (bf16[128,512]{1,0:T(8,128)(2,1)S(1)}, bf16[128,512]{1,0:T(8,128)(2,1)S(1)}, u32[]{:S(2)}, u32[]{:S(2)}) collective-permute-start(bf16[128,512]{1,0:T(8,128)(2,1)S(1)} %get-tuple-element.27), channel_id=1, source_target_pairs={{0,64},{8,72},{16,80},{24,88},{32,96},{40,104},{48,112},{56,120},{... | collective-permute-start | bytes 393224 | tf_op jit(solution)/shard_map/ppermute | solution.py:209
  54.6 2.6 %collective-permute-start.6 = (bf16[128,512]{1,0:T(8,128)(2,1)S(1)}, bf16[128,512]{1,0:T(8,128)(2,1)S(1)}, u32[]{:S(2)}, u32[]{:S(2)}) collective-permute-start(bf16[128,512]{1,0:T(8,128)(2,1)S(1)} %get-tuple-element.27), channel_id=1, source_target_pairs={{0,32},{8,40},{16,48},{24,56},{32,64},{40,72},{48,80},{56,88},{64,... | collective-permute-start | bytes 393224 | tf_op jit(solution)/shard_map/ppermute | solution.py:209
  57.6 3.4 %collective-permute-start.3 = (bf16[4,128,512]{2,1,0:T(8,128)(2,1)S(1)}, bf16[4,128,512]{2,1,0:T(8,128)(2,1)}, u32[]{:S(2)}, u32[]{:S(2)}) collective-permute-start(bf16[4,128,512]{2,1,0:T(8,128)(2,1)S(1)} %pad_maximum_fusion.2.k0), channel_id=1, source_target_pairs={{0,32},{8,40},{16,48},{24,56},{32,64},{40,72},{48,80},{56,88},{64,... | collective-permute-start | bytes 1572872 | tf_op jit(solution)/shard_map/ppermute | solution.py:209
  61.6 3.0 %collective-permute-start.9 = (bf16[4,128,512]{2,1,0:T(8,128)(2,1)S(1)}, bf16[4,128,512]{2,1,0:T(8,128)(2,1)}, u32[]{:S(2)}, u32[]{:S(2)}) collective-permute-start(bf16[4,128,512]{2,1,0:T(8,128)(2,1)S(1)} %pad_maximum_fusion.3.v0), channel_id=1, source_target_pairs={{0,8},{8,16},{16,24},{24,0},{32,40},{40,48},{48,56},{56,32},{64,72... | collective-permute-start | bytes 1572872 | tf_op jit(solution)/shard_map/ppermute | solution.py:213
  66.4 7.1 %collective-permute-done.3.k1 = bf16[4,128,512]{2,1,0:T(8,128)(2,1)} collective-permute-done((bf16[4,128,512]{2,1,0:T(8,128)(2,1)S(1)}, bf16[4,128,512]{2,1,0:T(8,128)(2,1)}, u32[]{:S(2)}, u32[]{:S(2)}) %collective-permute-start.3) | collective-permute-done | bytes 524320 | tf_op jit(solution)/shard_map/ppermute | solution.py:209
  73.5 4.2 %collective-permute-start.4 = (bf16[4,128,512]{2,1,0:T(8,128)(2,1)}, bf16[4,128,512]{2,1,0:T(8,128)(2,1)}, u32[]{:S(2)}, u32[]{:S(2)}) collective-permute-start(bf16[4,128,512]{2,1,0:T(8,128)(2,1)} %collective-permute-done.3.k1), channel_id=1, source_target_pairs={{32,64},{40,72},{48,80},{56,88},{64,96},{72,104},{80,112},{88,120}... | collective-permute-start | bytes 1572872 | tf_op jit(solution)/shard_map/ppermute | solution.py:209
  80.3 7.4 %collective-permute-done.4.k2 = bf16[4,128,512]{2,1,0:T(8,128)(2,1)} collective-permute-done((bf16[4,128,512]{2,1,0:T(8,128)(2,1)}, bf16[4,128,512]{2,1,0:T(8,128)(2,1)}, u32[]{:S(2)}, u32[]{:S(2)}) %collective-permute-start.4) | collective-permute-done | bytes 524320 | tf_op jit(solution)/shard_map/ppermute | solution.py:209
  87.7 4.2 %collective-permute-done.10.v2 = bf16[4,128,512]{2,1,0:T(8,128)(2,1)} collective-permute-done((bf16[4,128,512]{2,1,0:T(8,128)(2,1)}, bf16[4,128,512]{2,1,0:T(8,128)(2,1)}, u32[]{:S(2)}, u32[]{:S(2)}) %collective-permute-start.10) | collective-permute-done | bytes 524320 | tf_op jit(solution)/shard_map/ppermute | solution.py:213
  91.9 45.7 %shard_map.93 = (bf16[8,2,128,512]{3,2,1,0:T(8,128)(2,1)}, bf16[8,2,128,512]{3,2,1,0:T(8,128)(2,1)}, f32[2,128,512]{2,1,0:T(8,128)}, bf16[4,4,128,512]{3,2,1,0:T(8,128)(2,1)}, bf16[4,4,128,512]{3,2,1,0:T(8,128)(2,1)}) custom-call(s32[3]{0:T(128)} %pad_add_fusion.pos, s32[32]{0:T(128)} %reshape.51.local, bf16[8,2,128,512]{3,2,1,0:T(8,128)(2,1)} %all-to-all-done.kv, ...), custom_call_target="tpu_custom_call" | custom-call | flops 15300820992 | bytes 16777216 | tf_op jit(solution)/shard_map/pallas_call | solution.py:165
  137.7 2.2 slice_bitcast_fusion.7
  144.3 19.8 %collective-permute-done.12 = bf16[4,128,512]{2,1,0:T(8,128)(2,1)S(1)} collective-permute-done((bf16[4,128,512]{2,1,0:T(8,128)(2,1)S(1)}, bf16[4,128,512]{2,1,0:T(8,128)(2,1)S(1)}, u32[]{:S(2)}, u32[]{:S(2)}) %collective-permute-start.12) | collective-permute-done | bytes 524320 | tf_op jit(solution)/shard_map/ppermute | solution.py:209
  165.2 1.9 collective-permute-start.13
  167.2 4.5 %all-to-all-start.2 = ((bf16[8,2,128,512]{3,2,1,0:T(8,128)(2,1)}), bf16[8,2,128,512]{3,2,1,0:T(8,128)(2,1)S(1)}, u32[]{:S(2)}, u32[]{:S(2)}) async-start(bf16[8,2,128,512]{3,2,1,0:T(8,128)(2,1)} %get-tuple-element.9), calls=%async_computation.2 | async-start | bytes 4194304 | tf_op jit(solution)/shard_map/all_to_all | solution.py:256
  173.1 3.0 %collective-permute-start.19 = (bf16[4,128,512]{2,1,0:T(8,128)(2,1)S(1)}, bf16[4,128,512]{2,1,0:T(8,128)(2,1)S(1)}, u32[]{:S(2)}, u32[]{:S(2)}) collective-permute-start(bf16[4,128,512]{2,1,0:T(8,128)(2,1)S(1)} %fusion), channel_id=1, source_target_pairs={{0,24},{8,0},{16,8},{24,16},{32,56},{40,32},{48,40},{56,48},{64,88... | collective-permute-start | bytes 1572872 | tf_op jit(solution)/shard_map/ppermute | solution.py:213
  176.1 10.5 %collective-permute-done.13 = bf16[4,128,512]{2,1,0:T(8,128)(2,1)} collective-permute-done((bf16[4,128,512]{2,1,0:T(8,128)(2,1)S(1)}, bf16[4,128,512]{2,1,0:T(8,128)(2,1)}, u32[]{:S(2)}, u32[]{:S(2)}) %collective-permute-start.13) | collective-permute-done | bytes 524320 | tf_op jit(solution)/shard_map/ppermute | solution.py:209
  186.6 1.6 fusion.5
  188.2 3.5 %collective-permute-start.15 = (bf16[128,512]{1,0:T(8,128)(2,1)S(1)}, bf16[128,512]{1,0:T(8,128)(2,1)S(1)}, u32[]{:S(2)}, u32[]{:S(2)}) collective-permute-start(bf16[128,512]{1,0:T(8,128)(2,1)S(1)} %get-tuple-element.30), channel_id=1, source_target_pairs={{0,24},{8,0},{16,8},{24,16},{32,56},{40,32},{48,40},{56,48},{64,88... | collective-permute-start | bytes 393224 | tf_op jit(solution)/shard_map/ppermute | solution.py:213
  192.7 2.0 collective-permute-start.16
  196.0 1.9 collective-permute-start.21
  200.0 5.8 %collective-permute-done.21 = bf16[128,512]{1,0:T(8,128)(2,1)S(1)} collective-permute-done((bf16[128,512]{1,0:T(8,128)(2,1)S(1)}, bf16[128,512]{1,0:T(8,128)(2,1)S(1)}, u32[]{:S(2)}, u32[]{:S(2)}) %collective-permute-start.21) | collective-permute-done | bytes 131104 | tf_op jit(solution)/shard_map/ppermute | solution.py:209
  205.8 4.7 %collective-permute-done.22 = bf16[128,512]{1,0:T(8,128)(2,1)S(1)} collective-permute-done((bf16[128,512]{1,0:T(8,128)(2,1)S(1)}, bf16[128,512]{1,0:T(8,128)(2,1)S(1)}, u32[]{:S(2)}, u32[]{:S(2)}) %collective-permute-start.22) | collective-permute-done | bytes 131104 | tf_op jit(solution)/shard_map/ppermute | solution.py:209
  211.4 4.4 %all-to-all-start.3 = ((bf16[8,2,128,512]{3,2,1,0:T(8,128)(2,1)}), bf16[8,2,128,512]{3,2,1,0:T(8,128)(2,1)}, u32[]{:S(2)}, u32[]{:S(2)}) async-start(bf16[8,2,128,512]{3,2,1,0:T(8,128)(2,1)} %fusion.8), calls=%async_computation.3 | async-start | bytes 4194304 | tf_op jit(solution)/shard_map/all_to_all | solution.py:256
  217.0 1.6 copy.21
  221.9 21.2 %all-to-all-done.3 = bf16[8,2,128,512]{3,2,1,0:T(8,128)(2,1)} async-done(((bf16[8,2,128,512]{3,2,1,0:T(8,128)(2,1)}), bf16[8,2,128,512]{3,2,1,0:T(8,128)(2,1)}, u32[]{:S(2)}, u32[]{:S(2)}) %all-to-all-start.3) | async-done | bytes 2097184 | tf_op jit(solution)/shard_map/all_to_all | solution.py:256
  243.1 1.7 slice_bitcast_fusion
  (76 shorter events, 35.1 us)
Async XLA Ops:
  6.5 32.8 %all-to-all-start = ((bf16[8,2,128,512]{3,2,1,0:T(8,128)(2,1)}), bf16[8,2,128,512]{3,2,1,0:T(8,128)(2,1)}, u32[]{:S(2)}, u32[]{:S(2)}) async-start(bf16[8,2,128,512]{3,2,1,0:T(8,128)(2,1)} %pad_maximum_fusion), calls=%async_computation | async-start | bytes 4194304 | tf_op jit(solution)/shard_map/all_to_all | solution.py:256
  39.3 41.0 %all-to-all-start.1 = ((bf16[8,2,128,512]{3,2,1,0:T(8,128)(2,1)}), bf16[8,2,128,512]{3,2,1,0:T(8,128)(2,1)S(1)}, u32[]{:S(2)}, u32[]{:S(2)}) async-start(bf16[8,2,128,512]{3,2,1,0:T(8,128)(2,1)} %pad_maximum_fusion.1), calls=%async_computation.1 | async-start | bytes 4194304 | tf_op jit(solution)/shard_map/all_to_all | solution.py:256
  42.9 36.0 %copy-start.6 = (s32[8,4]{0,1:T(4,128)S(1)}, s32[8,4]{0,1:T(4,128)}, u32[]{:S(2)}) copy-start(s32[8,4]{0,1:T(4,128)} %param.10) | copy-start | bytes 388
  44.6 10.0 %collective-permute-start.2 = (bf16[128,512]{1,0:T(8,128)(2,1)S(1)}, bf16[128,512]{1,0:T(8,128)(2,1)S(1)}, u32[]{:S(2)}, u32[]{:S(2)}) collective-permute-start(bf16[128,512]{1,0:T(8,128)(2,1)S(1)} %get-tuple-element.28), channel_id=1, source_target_pairs={{0,24},{8,0},{16,8},{24,16},{32,56},{40,32},{48,40},{56,48},{64,88... | collective-permute-start | bytes 393224 | tf_op jit(solution)/shard_map/ppermute | solution.py:213
  47.7 9.6 %collective-permute-start.1 = (bf16[128,512]{1,0:T(8,128)(2,1)S(1)}, bf16[128,512]{1,0:T(8,128)(2,1)S(1)}, u32[]{:S(2)}, u32[]{:S(2)}) collective-permute-start(bf16[128,512]{1,0:T(8,128)(2,1)S(1)} %get-tuple-element.28), channel_id=1, source_target_pairs={{0,16},{8,24},{16,0},{24,8},{32,48},{40,56},{48,32},{56,40},{64,80... | collective-permute-start | bytes 393224 | tf_op jit(solution)/shard_map/ppermute | solution.py:213
  48.3 9.2 %collective-permute-start = (bf16[128,512]{1,0:T(8,128)(2,1)S(1)}, bf16[128,512]{1,0:T(8,128)(2,1)S(1)}, u32[]{:S(2)}, u32[]{:S(2)}) collective-permute-start(bf16[128,512]{1,0:T(8,128)(2,1)S(1)} %get-tuple-element.28), channel_id=1, source_target_pairs={{0,8},{8,16},{16,24},{24,0},{32,40},{40,48},{48,56},{56,32},{64,72... | collective-permute-start | bytes 393224 | tf_op jit(solution)/shard_map/ppermute | solution.py:213
  49.3 11.8 %collective-permute-start.8 = (bf16[128,512]{1,0:T(8,128)(2,1)S(1)}, bf16[128,512]{1,0:T(8,128)(2,1)S(1)}, u32[]{:S(2)}, u32[]{:S(2)}) collective-permute-start(bf16[128,512]{1,0:T(8,128)(2,1)S(1)} %get-tuple-element.27), channel_id=1, source_target_pairs={{0,96},{8,104},{16,112},{24,120},{1,97},{9,105},{17,113},{25,121},... | collective-permute-start | bytes 393224 | tf_op jit(solution)/shard_map/ppermute | solution.py:209
  49.9 11.1 %collective-permute-start.7 = (bf16[128,512]{1,0:T(8,128)(2,1)S(1)}, bf16[128,512]{1,0:T(8,128)(2,1)S(1)}, u32[]{:S(2)}, u32[]{:S(2)}) collective-permute-start(bf16[128,512]{1,0:T(8,128)(2,1)S(1)} %get-tuple-element.27), channel_id=1, source_target_pairs={{0,64},{8,72},{16,80},{24,88},{32,96},{40,104},{48,112},{56,120},{... | collective-permute-start | bytes 393224 | tf_op jit(solution)/shard_map/ppermute | solution.py:209
  54.6 6.9 %collective-permute-start.6 = (bf16[128,512]{1,0:T(8,128)(2,1)S(1)}, bf16[128,512]{1,0:T(8,128)(2,1)S(1)}, u32[]{:S(2)}, u32[]{:S(2)}) collective-permute-start(bf16[128,512]{1,0:T(8,128)(2,1)S(1)} %get-tuple-element.27), channel_id=1, source_target_pairs={{0,32},{8,40},{16,48},{24,56},{32,64},{40,72},{48,80},{56,88},{64,... | collective-permute-start | bytes 393224 | tf_op jit(solution)/shard_map/ppermute | solution.py:209
  57.6 34.3 %copy-start.4 = (bf16[4,128,512]{2,1,0:T(8,128)(2,1)}, bf16[4,128,512]{2,1,0:T(8,128)(2,1)S(1)}, u32[]{:S(2)}) copy-start(bf16[4,128,512]{2,1,0:T(8,128)(2,1)S(1)} %pad_maximum_fusion.2.k0) | copy-start | bytes 1572868
  57.6 15.8 %collective-permute-start.3 = (bf16[4,128,512]{2,1,0:T(8,128)(2,1)S(1)}, bf16[4,128,512]{2,1,0:T(8,128)(2,1)}, u32[]{:S(2)}, u32[]{:S(2)}) collective-permute-start(bf16[4,128,512]{2,1,0:T(8,128)(2,1)S(1)} %pad_maximum_fusion.2.k0), channel_id=1, source_target_pairs={{0,32},{8,40},{16,48},{24,56},{32,64},{40,72},{48,80},{56,88},{64,... | collective-permute-start | bytes 1572872 | tf_op jit(solution)/shard_map/ppermute | solution.py:209
  61.6 30.3 %copy-start.5 = (bf16[4,128,512]{2,1,0:T(8,128)(2,1)}, bf16[4,128,512]{2,1,0:T(8,128)(2,1)S(1)}, u32[]{:S(2)}) copy-start(bf16[4,128,512]{2,1,0:T(8,128)(2,1)S(1)} %pad_maximum_fusion.3.v0) | copy-start | bytes 1572868
  61.6 16.1 %collective-permute-start.9 = (bf16[4,128,512]{2,1,0:T(8,128)(2,1)S(1)}, bf16[4,128,512]{2,1,0:T(8,128)(2,1)}, u32[]{:S(2)}, u32[]{:S(2)}) collective-permute-start(bf16[4,128,512]{2,1,0:T(8,128)(2,1)S(1)} %pad_maximum_fusion.3.v0), channel_id=1, source_target_pairs={{0,8},{8,16},{16,24},{24,0},{32,40},{40,48},{48,56},{56,32},{64,72... | collective-permute-start | bytes 1572872 | tf_op jit(solution)/shard_map/ppermute | solution.py:213
  64.6 15.6 %collective-permute-start.5 = (bf16[4,128,512]{2,1,0:T(8,128)(2,1)S(1)}, bf16[4,128,512]{2,1,0:T(8,128)(2,1)}, u32[]{:S(2)}, u32[]{:S(2)}) collective-permute-start(bf16[4,128,512]{2,1,0:T(8,128)(2,1)S(1)} %pad_maximum_fusion.2.k0), channel_id=1, source_target_pairs={{0,96},{8,104},{16,112},{24,120},{1,97},{9,105},{17,113},{25,121},... | collective-permute-start | bytes 1572872 | tf_op jit(solution)/shard_map/ppermute | solution.py:209
  66.1 14.2 %collective-permute-start.11 = (bf16[4,128,512]{2,1,0:T(8,128)(2,1)S(1)}, bf16[4,128,512]{2,1,0:T(8,128)(2,1)}, u32[]{:S(2)}, u32[]{:S(2)}) collective-permute-start(bf16[4,128,512]{2,1,0:T(8,128)(2,1)S(1)} %pad_maximum_fusion.3.v0), channel_id=1, source_target_pairs={{0,24},{8,0},{16,8},{24,16},{32,56},{40,32},{48,40},{56,48},{64,88... | collective-permute-start | bytes 1572872 | tf_op jit(solution)/shard_map/ppermute | solution.py:213
  73.5 14.2 %collective-permute-start.4 = (bf16[4,128,512]{2,1,0:T(8,128)(2,1)}, bf16[4,128,512]{2,1,0:T(8,128)(2,1)}, u32[]{:S(2)}, u32[]{:S(2)}) collective-permute-start(bf16[4,128,512]{2,1,0:T(8,128)(2,1)} %collective-permute-done.3.k1), channel_id=1, source_target_pairs={{32,64},{40,72},{48,80},{56,88},{64,96},{72,104},{80,112},{88,120}... | collective-permute-start | bytes 1572872 | tf_op jit(solution)/shard_map/ppermute | solution.py:209
  77.7 14.2 %collective-permute-start.10 = (bf16[4,128,512]{2,1,0:T(8,128)(2,1)}, bf16[4,128,512]{2,1,0:T(8,128)(2,1)}, u32[]{:S(2)}, u32[]{:S(2)}) collective-permute-start(bf16[4,128,512]{2,1,0:T(8,128)(2,1)} %collective-permute-done.9.v1), channel_id=1, source_target_pairs={{0,8},{8,16},{16,24},{24,0},{32,40},{40,48},{48,56},{56,32},{64,72... | collective-permute-start | bytes 1572872 | tf_op jit(solution)/shard_map/ppermute | solution.py:213
  139.9 24.1 %collective-permute-start.12 = (bf16[4,128,512]{2,1,0:T(8,128)(2,1)S(1)}, bf16[4,128,512]{2,1,0:T(8,128)(2,1)S(1)}, u32[]{:S(2)}, u32[]{:S(2)}) collective-permute-start(bf16[4,128,512]{2,1,0:T(8,128)(2,1)S(1)} %get-tuple-element.20), channel_id=1, source_target_pairs={{96,64},{104,72},{112,80},{120,88},{64,32},{72,40},{80,48},{88,56}... | collective-permute-start | bytes 1572872 | tf_op jit(solution)/shard_map/ppermute | solution.py:209
  142.3 29.6 %collective-permute-start.18 = (bf16[4,128,512]{2,1,0:T(8,128)(2,1)}, bf16[4,128,512]{2,1,0:T(8,128)(2,1)S(1)}, u32[]{:S(2)}, u32[]{:S(2)}) collective-permute-start(bf16[4,128,512]{2,1,0:T(8,128)(2,1)} %get-tuple-element.22), channel_id=1, source_target_pairs={{0,24},{8,0},{16,8},{24,16},{32,56},{40,32},{48,40},{56,48},{64,88... | collective-permute-start | bytes 1572872 | tf_op jit(solution)/shard_map/ppermute | solution.py:213
  142.8 33.3 %collective-permute-start.14 = (bf16[4,128,512]{2,1,0:T(8,128)(2,1)}, bf16[4,128,512]{2,1,0:T(8,128)(2,1)}, u32[]{:S(2)}, u32[]{:S(2)}) collective-permute-start(bf16[4,128,512]{2,1,0:T(8,128)(2,1)} %get-tuple-element.21), channel_id=1, source_target_pairs={{96,0},{104,8},{112,16},{120,24},{97,1},{105,9},{113,17},{121,25},... | collective-permute-start | bytes 1572872 | tf_op jit(solution)/shard_map/ppermute | solution.py:209
  165.2 21.4 %collective-permute-start.13 = (bf16[4,128,512]{2,1,0:T(8,128)(2,1)S(1)}, bf16[4,128,512]{2,1,0:T(8,128)(2,1)}, u32[]{:S(2)}, u32[]{:S(2)}) collective-permute-start(bf16[4,128,512]{2,1,0:T(8,128)(2,1)S(1)} %fusion.3), channel_id=1, source_target_pairs={{32,0},{40,8},{48,16},{56,24},{64,32},{72,40},{80,48},{88,56},{96,... | collective-permute-start | bytes 1572872 | tf_op jit(solution)/shard_map/ppermute | solution.py:209
  167.2 44.2 %all-to-all-start.2 = ((bf16[8,2,128,512]{3,2,1,0:T(8,128)(2,1)}), bf16[8,2,128,512]{3,2,1,0:T(8,128)(2,1)S(1)}, u32[]{:S(2)}, u32[]{:S(2)}) async-start(bf16[8,2,128,512]{3,2,1,0:T(8,128)(2,1)} %get-tuple-element.9), calls=%async_computation.2 | async-start | bytes 4194304 | tf_op jit(solution)/shard_map/all_to_all | solution.py:256
  171.6 23.1 %collective-permute-start.20 = (bf16[4,128,512]{2,1,0:T(8,128)(2,1)}, bf16[4,128,512]{2,1,0:T(8,128)(2,1)S(1)}, u32[]{:S(2)}, u32[]{:S(2)}) collective-permute-start(bf16[4,128,512]{2,1,0:T(8,128)(2,1)} %get-tuple-element.23), channel_id=1, source_target_pairs={{0,8},{8,16},{16,24},{24,0},{32,40},{40,48},{48,56},{56,32},{64,72... | collective-permute-start | bytes 1572872 | tf_op jit(solution)/shard_map/ppermute | solution.py:213
  173.1 21.6 %collective-permute-start.19 = (bf16[4,128,512]{2,1,0:T(8,128)(2,1)S(1)}, bf16[4,128,512]{2,1,0:T(8,128)(2,1)S(1)}, u32[]{:S(2)}, u32[]{:S(2)}) collective-permute-start(bf16[4,128,512]{2,1,0:T(8,128)(2,1)S(1)} %fusion), channel_id=1, source_target_pairs={{0,24},{8,0},{16,8},{24,16},{32,56},{40,32},{48,40},{56,48},{64,88... | collective-permute-start | bytes 1572872 | tf_op jit(solution)/shard_map/ppermute | solution.py:213
  188.2 10.4 %collective-permute-start.15 = (bf16[128,512]{1,0:T(8,128)(2,1)S(1)}, bf16[128,512]{1,0:T(8,128)(2,1)S(1)}, u32[]{:S(2)}, u32[]{:S(2)}) collective-permute-start(bf16[128,512]{1,0:T(8,128)(2,1)S(1)} %get-tuple-element.30), channel_id=1, source_target_pairs={{0,24},{8,0},{16,8},{24,16},{32,56},{40,32},{48,40},{56,48},{64,88... | collective-permute-start | bytes 393224 | tf_op jit(solution)/shard_map/ppermute | solution.py:213
  191.7 8.3 %collective-permute-start.17 = (bf16[128,512]{1,0:T(8,128)(2,1)S(1)}, bf16[128,512]{1,0:T(8,128)(2,1)S(1)}, u32[]{:S(2)}, u32[]{:S(2)}) collective-permute-start(bf16[128,512]{1,0:T(8,128)(2,1)S(1)} %get-tuple-element.31), channel_id=1, source_target_pairs={{0,8},{8,16},{16,24},{24,0},{32,40},{40,48},{48,56},{56,32},{64,72... | collective-permute-start | bytes 393224 | tf_op jit(solution)/shard_map/ppermute | solution.py:213
  192.7 17.8 %copy-start.3 = (f32[2,128,512]{2,1,0:T(8,128)S(1)}, f32[2,128,512]{2,1,0:T(8,128)}, u32[]{:S(2)}) copy-start(f32[2,128,512]{2,1,0:T(8,128)} %get-tuple-element.11) | copy-start | bytes 1572868
  192.7 7.2 %collective-permute-start.16 = (bf16[128,512]{1,0:T(8,128)(2,1)S(1)}, bf16[128,512]{1,0:T(8,128)(2,1)S(1)}, u32[]{:S(2)}, u32[]{:S(2)}) collective-permute-start(bf16[128,512]{1,0:T(8,128)(2,1)S(1)} %get-tuple-element.32), channel_id=1, source_target_pairs={{0,16},{8,24},{16,0},{24,8},{32,48},{40,56},{48,32},{56,40},{64,80... | collective-permute-start | bytes 393224 | tf_op jit(solution)/shard_map/ppermute | solution.py:213
  196.0 9.8 %collective-permute-start.21 = (bf16[128,512]{1,0:T(8,128)(2,1)S(1)}, bf16[128,512]{1,0:T(8,128)(2,1)S(1)}, u32[]{:S(2)}, u32[]{:S(2)}) collective-permute-start(bf16[128,512]{1,0:T(8,128)(2,1)S(1)} %get-tuple-element.33), channel_id=1, source_target_pairs={{32,0},{40,8},{48,16},{56,24},{64,32},{72,40},{80,48},{88,56},{96,... | collective-permute-start | bytes 393224 | tf_op jit(solution)/shard_map/ppermute | solution.py:209
  198.0 7.8 %collective-permute-start.23 = (bf16[128,512]{1,0:T(8,128)(2,1)S(1)}, bf16[128,512]{1,0:T(8,128)(2,1)S(1)}, u32[]{:S(2)}, u32[]{:S(2)}) collective-permute-start(bf16[128,512]{1,0:T(8,128)(2,1)S(1)} %get-tuple-element.34), channel_id=1, source_target_pairs={{96,0},{104,8},{112,16},{120,24},{97,1},{105,9},{113,17},{121,25},... | collective-permute-start | bytes 393224 | tf_op jit(solution)/shard_map/ppermute | solution.py:209
  198.6 11.8 %collective-permute-start.22 = (bf16[128,512]{1,0:T(8,128)(2,1)S(1)}, bf16[128,512]{1,0:T(8,128)(2,1)S(1)}, u32[]{:S(2)}, u32[]{:S(2)}) collective-permute-start(bf16[128,512]{1,0:T(8,128)(2,1)S(1)} %get-tuple-element.35), channel_id=1, source_target_pairs={{64,0},{72,8},{80,16},{88,24},{96,32},{104,40},{112,48},{120,56},{... | collective-permute-start | bytes 393224 | tf_op jit(solution)/shard_map/ppermute | solution.py:209
  211.4 31.8 %all-to-all-start.3 = ((bf16[8,2,128,512]{3,2,1,0:T(8,128)(2,1)}), bf16[8,2,128,512]{3,2,1,0:T(8,128)(2,1)}, u32[]{:S(2)}, u32[]{:S(2)}) async-start(bf16[8,2,128,512]{3,2,1,0:T(8,128)(2,1)} %fusion.8), calls=%async_computation.3 | async-start | bytes 4194304 | tf_op jit(solution)/shard_map/all_to_all | solution.py:256
  (3 other events, 20.7 us)

commit v2 on v1

v2 whole, which is shorter than its diff:
```python
import jax
import jax.numpy as jnp
from jax import lax
from jax.experimental import pallas as pl
from jax.experimental.pallas import tpu as pltpu
from jax.sharding import PartitionSpec as P

BLK = 128
NB = 8
SPAN = 1024
SCALE = 128 ** -0.5
LOG2E = 1.4426950408889634
NEG = -1e30
QT = 256
bf16 = jnp.bfloat16
f32 = jnp.float32


def dot_nt(a, b):
    return lax.dot_general(a, b, (((1,), (1,)), ((), ())), preferred_element_type=f32)


def dot_nn(a, b):
    return lax.dot_general(a, b, (((1,), (0,)), ((), ())), preferred_element_type=f32)


def fold_max(s):
    return s.reshape(s.shape[0] // 8, 8, s.shape[1]).max(0)


def fold_sum(s):
    return s.reshape(s.shape[0] // 8, 8, s.shape[1]).sum(0)


def attention_kernel(
    local, summary, kv, qg, k0, k1, k2a, k2b, k3, v0, v1, v2a, v2b, v3,
    ao, dl, dsum, gk0, gk1, gk2a, gk2b, gk3, gv0, gv1, gv2a, gv2b, gv3,
    kf, vf, kt, vt, kl, vl, klt, vlt, s_ref, dp_ref, p_ref, d_ref, mx, sm, ot, dqt, dk_acc, dv_acc, gs, qs, fk, fv,
):
    span = lax.axis_index("ctx")
    x, y, sb = lax.div(span, 4), lax.rem(span, 4), summary[0, 0]
    for a in range(4):
        for c in range(4):
            rows = slice(c * BLK, (c + 1) * BLK)
            kf[a, rows, :] = ((k0, k1, k2a, k3)[a][c] if a != 2 or c < 2 else k2b[c - 2])
            rows = slice(a * BLK, (a + 1) * BLK)
            vf[c, rows, :] = ((v0, v1, v2a, v3)[a][c] if a != 2 or c < 2 else v2b[c - 2])
    fk[...] = jnp.zeros_like(fk)
    fv[...] = jnp.zeros_like(fv)
    mx[...] = jnp.full_like(mx, NEG)
    sm[...] = jnp.zeros_like(sm)
    ot[...] = jnp.zeros_like(ot)
    dqt[...] = jnp.zeros_like(dqt)
    dk_acc[...] = jnp.zeros_like(dk_acc)
    dv_acc[...] = jnp.zeros_like(dv_acc)

    def queries(t, n=2):
        return qg[t * n:(t + 1) * n, 0].reshape(n * BLK, BLK)

    def cots(t, n=2):
        return qg[t * n:(t + 1) * n, 1].reshape(n * BLK, BLK)

    def score_far(sx, first):
        kt[sx] = kf[sx].T
        vt[sx] = vf[sx].T
        for t in range(4):
            cols = slice(t * QT, (t + 1) * QT)
            lo = BLK if first else 0
            s = dot_nt(kf[sx, lo:], queries(t))
            s_ref[sx, lo:, cols] = s
            if first:
                top = jnp.full((8, QT), NEG, f32)
                for sy in range(1, 4):
                    top = jnp.maximum(top, jnp.where(sy <= y, fold_max(s[sy * BLK - lo:(sy + 1) * BLK - lo]), NEG))
            else:
                top = fold_max(s)
            mx[:, cols] = jnp.maximum(mx[:, cols], top)

    score_far(0, True)
    pl.loop(1, x + 1)(lambda sx: score_far(sx, False))

    def local_scores(b):
        for i in range(4):
            idx = local[b, i]
            kl[b, i * BLK:(i + 1) * BLK, :] = kv[idx, 0]
            vl[b, i * BLK:(i + 1) * BLK, :] = kv[idx, 1]
        klt[b] = kl[b].T
        vlt[b] = vl[b].T
        cols = slice(b * BLK, (b + 1) * BLK)
        s = dot_nt(kl[b], qg[b, 0])
        s_ref[4, :, cols] = s
        mx[:, cols] = jnp.maximum(mx[:, cols], fold_max(s))

    for b in range(NB):
        local_scores(b)

    mc = mx[...].max(0, keepdims=True) * (SCALE * LOG2E)

    def prob_far(sx, first):
        for t in range(4):
            cols = slice(t * QT, (t + 1) * QT)
            total = sm[:, cols]
            lo = BLK if first else 0
            dp_ref[sx, lo:, cols] = dot_nt(vf[sx, lo:], cots(t))
            for sy in range(lo // BLK, 4):
                rows = slice(sy * BLK, (sy + 1) * BLK)
                shift = mc[:, cols]
                if first:
                    shift = jnp.where((sy >= 1) & (sy <= y), shift, -NEG)
                p = jnp.exp2(s_ref[sx, rows, cols] * (SCALE * LOG2E) - shift)
                total = total + fold_sum(p)
                p_ref[sx, rows, cols] = p.astype(bf16)
            sm[:, cols] = total
            ot[:, cols] += dot_nn(vt[sx, :, lo:], p_ref[sx, lo:, cols])

    prob_far(0, True)
    pl.loop(1, x + 1)(lambda sx: prob_far(sx, False))
    for b in range(NB):
        cols = slice(b * BLK, (b + 1) * BLK)
        p = jnp.exp2(s_ref[4, :, cols] * (SCALE * LOG2E) - mc[:, cols])
        sm[:, cols] += fold_sum(p)
        p_ref[4, :, cols] = p.astype(bf16)
        ot[:, cols] += dot_nn(vlt[b], p_ref[4, :, cols])

    inv = 1.0 / sm[...].sum(0, keepdims=True)
    deltas = []
    for b in range(NB):
        cols = slice(b * BLK, (b + 1) * BLK)
        o = (ot[:, cols] * inv[:, cols]).T.astype(bf16)
        ao[b, 0] = o
        g = qg[b, 1].astype(f32)
        column = jnp.broadcast_to(inv[:, cols], (BLK, BLK)).T
        gs[cols, :] = (g * column).astype(bf16)
        qs[cols, :] = (qg[b, 0].astype(f32) * (column * SCALE)).astype(bf16)
        deltas.append((g * o.astype(f32)).T.sum(0, keepdims=True))
    delta = jnp.concatenate(deltas, 1)

    def grad_far(sx, first=False):
        lo = BLK if first else 0
        for t in range(4):
            cols = slice(t * QT, (t + 1) * QT)
            for sy in range(lo // BLK, 4):
                rows = slice(sy * BLK, (sy + 1) * BLK)
                d_ref[sx, rows, cols] = p_ref[sx, rows, cols] * (dp_ref[sx, rows, cols] - delta[:, cols]).astype(bf16)
        dqt[...] += dot_nn(kt[sx, :, lo:], d_ref[sx, lo:])
        fv[lo // BLK:, sx] = dot_nn(p_ref[sx, lo:], gs[...]).reshape(4 - lo // BLK, BLK, BLK).astype(bf16)
        fk[sx, lo // BLK:] = dot_nn(d_ref[sx, lo:], qs[...]).reshape(4 - lo // BLK, BLK, BLK).astype(bf16)

    grad_far(0, True)
    pl.loop(1, x + 1)(grad_far)
    for out, far in (((gk0, gk1, gk2a, gk2b, gk3), fk), ((gv0, gv1, gv2a, gv2b, gv3), fv)):
        out[0][...] = far[0]
        out[1][...] = far[1]
        out[2][...] = far[2, :2]
        out[3][...] = far[2, 2:]
        out[4][...] = far[3]
    for b in range(NB):
        cols = slice(b * BLK, (b + 1) * BLK)
        dp = dot_nt(vl[b], qg[b, 1])
        d_ref[4, :, cols] = p_ref[4, :, cols] * (dp - delta[:, cols]).astype(bf16)
        dqt[:, cols] += dot_nn(klt[b], d_ref[4, :, cols])
        dv = dot_nn(p_ref[4, :, cols], gs[cols, :])
        dk = dot_nn(d_ref[4, :, cols], qs[cols, :])
        for i in range(4):
            idx = local[b, i]
            dk_acc[idx] += dk[i * BLK:(i + 1) * BLK]
            dv_acc[idx] += dv[i * BLK:(i + 1) * BLK]
        ao[b, 1] = (dqt[:, cols] * (inv[:, cols] * SCALE)).T.astype(bf16)
    dl[:, 0] = dk_acc[...].astype(bf16)
    dl[:, 1] = dv_acc[...].astype(bf16)
    dsum[0] = dk_acc[sb]
    dsum[1] = dv_acc[sb]


def attention(local, summary, kv, qg, ks, vs):
    width = kv.shape[-1]
    heads = width // BLK

    def block(*lead):
        return pl.BlockSpec((*lead, BLK, BLK), lambda h: (0,) * (len(lead) + 1) + (h,))

    def shape(kind, *lead):
        return jax.ShapeDtypeStruct((*lead, BLK, width), kind)

    smem = pl.BlockSpec(memory_space=pltpu.SMEM)
    counts = [4, 4, 2, 2, 4]
    far = [block(n) for n in counts]
    made = [shape(bf16, n) for n in counts]
    out = pl.pallas_call(
        attention_kernel,
        grid=(heads,),
        in_specs=[smem, smem, block(NB, 2), block(NB, 2)] + far + far,
        out_specs=[block(NB, 2), block(NB, 2), block(2)] + far + far,
        out_shape=[shape(bf16, NB, 2), shape(bf16, NB, 2), shape(f32, 2)] + made + made,
        scratch_shapes=[
            pltpu.VMEM((4, 512, BLK), bf16), pltpu.VMEM((4, 512, BLK), bf16),
            pltpu.VMEM((4, BLK, 512), bf16), pltpu.VMEM((4, BLK, 512), bf16),
            pltpu.VMEM((NB, 512, BLK), bf16), pltpu.VMEM((NB, 512, BLK), bf16),
            pltpu.VMEM((NB, BLK, 512), bf16), pltpu.VMEM((NB, BLK, 512), bf16),
            pltpu.VMEM((5, 512, SPAN), f32), pltpu.VMEM((4, 512, SPAN), f32), pltpu.VMEM((5, 512, SPAN), bf16), pltpu.VMEM((5, 512, SPAN), bf16),
            pltpu.VMEM((8, SPAN), f32), pltpu.VMEM((8, SPAN), f32),
            pltpu.VMEM((BLK, SPAN), f32), pltpu.VMEM((BLK, SPAN), f32),
            pltpu.VMEM((NB, BLK, BLK), f32), pltpu.VMEM((NB, BLK, BLK), f32),
            pltpu.VMEM((SPAN, BLK), bf16), pltpu.VMEM((SPAN, BLK), bf16),
            pltpu.VMEM((4, 4, BLK, BLK), bf16), pltpu.VMEM((4, 4, BLK, BLK), bf16),
        ],
        compiler_params=pltpu.CompilerParams(vmem_limit_bytes=56 << 20),
        cost_estimate=pl.CostEstimate(
            flops=heads * 12 * SPAN * 2432 * BLK, bytes_accessed=heads * (4 << 20), transcendentals=heads * SPAN * 2432
        ),
    )(local, summary, kv, qg, *ks, *vs)
    return out[:3], out[3:8], out[8:]


def through(pairs, held, arrive, leave):
    into = [pltpu.make_async_copy(a, held.at[n], arrive.at[n]) for n, (a, _) in enumerate(pairs)]
    out = [pltpu.make_async_copy(held.at[n], b, leave.at[n]) for n, (_, b) in enumerate(pairs)]
    for copy in into:
        copy.start()
    for before, after in zip(into, out):
        before.wait()
        after.start()
    for copy in out:
        copy.wait()


def pack_kernel(*refs):
    *arrays, out, held, arrive, leave = refs
    width = out.shape[-1]
    through(
        [
            (a.at[:, pl.ds(g * width, width)], out.at[g, i] if len(arrays) > 1 else out.at[g])
            for g in range(NB) for i, a in enumerate(arrays)
        ],
        held, arrive, leave,
    )


def held_blocks(count, width, kind):
    return [pltpu.VMEM((count, BLK, width), kind), pltpu.SemaphoreType.DMA((count,)), pltpu.SemaphoreType.DMA((count,))]


def pack(*arrays):
    width = arrays[0].shape[1] // NB
    lead = (NB, len(arrays)) if len(arrays) > 1 else (NB,)
    return pl.pallas_call(
        pack_kernel,
        in_specs=[pl.BlockSpec(memory_space=pl.ANY)] * len(arrays),
        out_specs=pl.BlockSpec(memory_space=pl.ANY),
        out_shape=jax.ShapeDtypeStruct((*lead, BLK, width), arrays[0].dtype),
        scratch_shapes=held_blocks(NB * len(arrays), width, arrays[0].dtype),
        cost_estimate=pl.CostEstimate(flops=0, bytes_accessed=len(arrays) << 21, transcendentals=0),
    )(*arrays)


def unpack_kernel(got, *refs):
    *arrays, held, arrive, leave = refs
    width = got.shape[-1]
    through(
        [
            (got.at[g, i] if len(arrays) > 1 else got.at[g], a.at[:, pl.ds(g * width, width)])
            for g in range(NB) for i, a in enumerate(arrays)
        ],
        held, arrive, leave,
    )


def unpack(got):
    count, width = (got.shape[1] if got.ndim == 4 else 1), got.shape[-1]
    out = pl.pallas_call(
        unpack_kernel,
        in_specs=[pl.BlockSpec(memory_space=pl.ANY)],
        out_specs=[pl.BlockSpec(memory_space=pl.ANY)] * count,
        out_shape=[jax.ShapeDtypeStruct((BLK, NB * width), got.dtype)] * count,
        scratch_shapes=held_blocks(NB * count, width, got.dtype),
        cost_estimate=pl.CostEstimate(flops=0, bytes_accessed=count << 21, transcendentals=0),
    )(got)
    return out if count > 1 else out[0]


SIDE = 4


def along_x(array, step):
    return lax.ppermute(
        array, "ctx", [(x * SIDE + y, (x + step) % SIDE * SIDE + y) for x in range(SIDE) for y in range(SIDE)]
    )


def along_y(array, step):
    return lax.ppermute(
        array, "ctx", [(x * SIDE + y, x * SIDE + (y + step) % SIDE) for x in range(SIDE) for y in range(SIDE)]
    )


def gather(own, first, second):
    line = jnp.stack([own] + [first(own, s) for s in (1, 2, 3)])
    near = second(line, 1)
    last = second(line, -1)
    return line, near, second(near[:2], 1), second(last[2:], -1), last


def plus(*terms):
    total = terms[0].astype(f32)
    for term in terms[1:]:
        total = total + term.astype(f32)
    return total


def scatter(parts, first, second):
    own, near, low, high, last = parts
    low = second(low, -1)
    high = second(high, 1)
    near = jnp.concatenate([plus(near[:2], low).astype(bf16), near[2:]])
    last = jnp.concatenate([last[:2], plus(last[2:], high).astype(bf16)])
    line = plus(own, second(near, -1), second(last, 1)).astype(bf16)
    return plus(line[0], *[first(line[s], -s) for s in (1, 2, 3)])


def exchange(array):
    return lax.all_to_all(array, "head", split_axis=0, concat_axis=0, tiled=True)


def device_step(queries, keys, values, grad_out, local_blocks, summary_blocks):
    sb = summary_blocks[0, 0]
    kv = exchange(pack(keys, values))
    qg = exchange(pack(queries, grad_out))
    own = lax.dynamic_index_in_dim(kv, sb, 0, keepdims=False)
    ks = gather(own[0], along_y, along_x)
    vs = gather(own[1], along_x, along_y)
    (ao, dl, dsum), fk, fv = attention(local_blocks, summary_blocks, kv, qg, ks, vs)
    attended, grad_q = unpack(exchange(ao))
    far = jnp.stack([scatter(fk, along_y, along_x), scatter(fv, along_x, along_y)])
    dl = lax.dynamic_update_slice(dl, (dsum + far).astype(bf16)[None], (sb, 0, 0, 0))
    grad_k, grad_v = unpack(exchange(dl))
    return attended, grad_q, grad_k, grad_v


def solution(mesh):
    tokens = P(("ctx", "head"), None)
    return jax.shard_map(
        device_step,
        mesh=mesh,
        in_specs=(tokens,) * 4 + (P("ctx", None),) * 2,
        out_specs=(tokens,) * 4,
        check_vma=False,
    )
```

time: 251 us -> 219 us (0.87)
  waiting for transfers between devices: 104 us -> 84.5 us
  local copies, waits for them, and re-layouts: 24.5 us -> 5.14 us
  starting transfers between devices: 63.1 us -> 81.8 us
  other arithmetic: 9.85 us -> 1.95 us
  Pallas kernels: 45.7 us -> 42.8 us
    ppermute x12 -> x14, waiting for transfers between devices: 55.7 us -> 16.7 us  [along_x(): lax.ppermute(array, 'ctx', [(x * SIDE + y, (x + step) % SIDE * SIDE + y)...]
    ppermute x12 -> x14, starting transfers between devices: 25.5 us -> 39.6 us  [along_x(): lax.ppermute(array, 'ctx', [(x * SIDE + y, (x + step) % SIDE * SIDE + y)...]
    ppermute x12 -> x14, waiting for transfers between devices: 4.57 us -> 18.6 us  [along_y(): lax.ppermute(array, 'ctx', [(x * SIDE + y, x * SIDE + (y + step) % SIDE)...]
    unnamed x23 -> x41, local copies, waits for them, and re-layouts: 10.9 us -> 2.88 us
    transpose x6 -> x0, local copies, waits for them, and re-layouts: 6.47 us -> none  [to_tokens(): got[:, i].transpose(1, 0, 2).reshape(BLK, -1)]
    all_to_all x4, waiting for transfers between devices: 43.7 us -> 49.2 us  [exchange(): lax.all_to_all(array, 'head', split_axis=0, concat_axis=0, tiled=True)]
    convert_element_type x4 -> x6, other arithmetic: 5.16 us -> 0.68 us  [the longest x2 0.41 us: scatter(): line = plus(own, second(near, -1), second(last, 1)).astype(bf16)]
    ppermute x12 -> x14, starting transfers between devices: 19.6 us -> 23.7 us  [along_y(): lax.ppermute(array, 'ctx', [(x * SIDE + y, x * SIDE + (y + step) % SIDE)...]
  transfers between devices with their start and end apart: 28 -> 32, of which waited for: 11 -> 14; matrix products, arithmetic and copies ran while one was open for 8% -> 2% of each run, Pallas kernels for 0% -> 2%
where the time goes in v2:
time: 219 us; the launch traced here: 218 us
  waiting for transfers between devices  84.5 us (39%)
  starting transfers between devices  81.8 us (37%)
  Pallas kernels  42.8 us (20%)
  local copies, waits for them, and re-layouts  5.14 us (2%)
    all_to_all x4, waiting for transfers between devices, exchange(): lax.all_to_all(array, 'head', split_axis=0, concat_axis=0, tiled=True)  49.2 us
    ppermute x14, starting transfers between devices, along_x(): lax.ppermute(array, 'ctx', [(x * SIDE + y, (x + step) % SIDE * SIDE + y)...  39.6 us
    pallas_call x1, Pallas kernels, attention(): pl.pallas_call(attention_kernel, grid=(heads,), in_specs=[smem, smem, blo...  32.5 us
    ppermute x14, starting transfers between devices, along_y(): lax.ppermute(array, 'ctx', [(x * SIDE + y, x * SIDE + (y + step) % SIDE)...  23.7 us
    ppermute x14, waiting for transfers between devices, along_y(): lax.ppermute(array, 'ctx', [(x * SIDE + y, x * SIDE + (y + step) % SIDE)...  18.6 us
    all_to_all x4, starting transfers between devices, exchange(): lax.all_to_all(array, 'head', split_axis=0, concat_axis=0, tiled=True)  18.4 us
    ppermute x14, waiting for transfers between devices, along_x(): lax.ppermute(array, 'ctx', [(x * SIDE + y, (x + step) % SIDE * SIDE + y)...  16.7 us
    pallas_call x2, Pallas kernels, pack(): pl.pallas_call(pack_kernel, in_specs=[pl.BlockSpec(memory_space=pl.ANY)]...  5.24 us
  transfers between devices with their start and end apart: 32, of which 14 were waited for; matrix products, arithmetic and copies ran while one was open for 2% of the time, Pallas kernels for 2%

profile of v2, /device:TPU:2, one launch (start us, length us, event | category | flops | bytes accessed | tf_op | source)
XLA Modules:
  0.0 218.1 jit_solution(13887051808055233537)
XLA Ops:
  0.6 2.6 %shard_map.93 = bf16[8,2,128,512]{3,2,1,0:T(8,128)(2,1)} custom-call(bf16[128,4096]{1,0:T(8,128)(2,1)} %refs_0_.2, bf16[128,4096]{1,0:T(8,128)(2,1)} %refs_1_.2), custom_call_target="tpu_custom_call" | custom-call | bytes 4194304 | tf_op jit(solution)/shard_map/pallas_call | solution.py:246
  3.2 5.3 %all-to-all-start = ((bf16[8,2,128,512]{3,2,1,0:T(8,128)(2,1)}), bf16[8,2,128,512]{3,2,1,0:T(8,128)(2,1)S(1)}, u32[]{:S(2)}, u32[]{:S(2)}) async-start(bf16[8,2,128,512]{3,2,1,0:T(8,128)(2,1)} %shard_map.93), calls=%async_computation | async-start | bytes 4194304 | tf_op jit(solution)/shard_map/all_to_all | solution.py:321
  8.6 2.6 %shard_map.94 = bf16[8,2,128,512]{3,2,1,0:T(8,128)(2,1)} custom-call(bf16[128,4096]{1,0:T(8,128)(2,1)} %refs_0_.3, bf16[128,4096]{1,0:T(8,128)(2,1)} %refs_1_.3), custom_call_target="tpu_custom_call" | custom-call | bytes 4194304 | tf_op jit(solution)/shard_map/pallas_call | solution.py:246
  11.2 24.6 %all-to-all-done.kv = bf16[8,2,128,512]{3,2,1,0:T(8,128)(2,1)S(1)} async-done(((bf16[8,2,128,512]{3,2,1,0:T(8,128)(2,1)}), bf16[8,2,128,512]{3,2,1,0:T(8,128)(2,1)S(1)}, u32[]{:S(2)}, u32[]{:S(2)}) %all-to-all-start) | async-done | bytes 2097184 | tf_op jit(solution)/shard_map/all_to_all | solution.py:321
  35.8 4.4 %all-to-all-start.1 = ((bf16[8,2,128,512]{3,2,1,0:T(8,128)(2,1)}), bf16[8,2,128,512]{3,2,1,0:T(8,128)(2,1)}, u32[]{:S(2)}, u32[]{:S(2)}) async-start(bf16[8,2,128,512]{3,2,1,0:T(8,128)(2,1)} %shard_map.94), calls=%async_computation.1 | async-start | bytes 4194304 | tf_op jit(solution)/shard_map/all_to_all | solution.py:321
  40.9 3.1 %collective-permute-start.2 = (bf16[128,512]{1,0:T(8,128)(2,1)S(1)}, bf16[128,512]{1,0:T(8,128)(2,1)S(1)}, u32[]{:S(2)}, u32[]{:S(2)}) collective-permute-start(bf16[128,512]{1,0:T(8,128)(2,1)S(1)} %get-tuple-element.40), channel_id=1, source_target_pairs={{0,24},{8,0},{16,8},{24,16},{32,56},{40,32},{48,40},{56,48},{64,88... | collective-permute-start | bytes 393224 | tf_op jit(solution)/shard_map/ppermute | solution.py:291
  46.1 2.4 %collective-permute-start.8 = (bf16[128,512]{1,0:T(8,128)(2,1)S(1)}, bf16[128,512]{1,0:T(8,128)(2,1)S(1)}, u32[]{:S(2)}, u32[]{:S(2)}) collective-permute-start(bf16[128,512]{1,0:T(8,128)(2,1)S(1)} %get-tuple-element.39), channel_id=1, source_target_pairs={{0,64},{8,72},{16,80},{24,88},{32,96},{40,104},{48,112},{56,120},{... | collective-permute-start | bytes 393224 | tf_op jit(solution)/shard_map/ppermute | solution.py:285
  48.5 1.5 collective-permute-done.2
  51.9 1.9 collective-permute-done
  56.0 3.9 %collective-permute-start.12 = (bf16[4,128,512]{2,1,0:T(8,128)(2,1)S(1)}, bf16[4,128,512]{2,1,0:T(8,128)(2,1)S(1)}, u32[]{:S(2)}, u32[]{:S(2)}) collective-permute-start(bf16[4,128,512]{2,1,0:T(8,128)(2,1)S(1)} %pad_maximum_fusion.1.v0), channel_id=1, source_target_pairs={{0,24},{8,0},{16,8},{24,16},{32,56},{40,32},{48,40},{56,48},{64,88... | collective-permute-start | bytes 1572872 | tf_op jit(solution)/shard_map/ppermute | solution.py:291
  59.9 7.9 %collective-permute-done.5.k3 = bf16[4,128,512]{2,1,0:T(8,128)(2,1)S(1)} collective-permute-done((bf16[4,128,512]{2,1,0:T(8,128)(2,1)S(1)}, bf16[4,128,512]{2,1,0:T(8,128)(2,1)S(1)}, u32[]{:S(2)}, u32[]{:S(2)}) %collective-permute-start.5) | collective-permute-done | bytes 524320 | tf_op jit(solution)/shard_map/ppermute | solution.py:285
  70.1 2.7 %collective-permute-start.13 = (bf16[2,128,512]{2,1,0:T(8,128)(2,1)S(1)}, bf16[2,128,512]{2,1,0:T(8,128)(2,1)}, u32[]{:S(2)}, u32[]{:S(2)}) collective-permute-start(bf16[2,128,512]{2,1,0:T(8,128)(2,1)S(1)} %slice.99), channel_id=1, source_target_pairs={{0,24},{8,0},{16,8},{24,16},{32,56},{40,32},{48,40},{56,48},{64,88... | collective-permute-start | bytes 786440 | tf_op jit(solution)/shard_map/ppermute | solution.py:291
  75.6 2.6 %collective-permute-done.4.k2a = bf16[2,128,512]{2,1,0:T(8,128)(2,1)} collective-permute-done((bf16[2,128,512]{2,1,0:T(8,128)(2,1)S(1)}, bf16[2,128,512]{2,1,0:T(8,128)(2,1)}, u32[]{:S(2)}, u32[]{:S(2)}) %collective-permute-start.4) | collective-permute-done | bytes 262176 | tf_op jit(solution)/shard_map/ppermute | solution.py:285
  78.1 3.2 %collective-permute-done.11.v2a = bf16[2,128,512]{2,1,0:T(8,128)(2,1)} collective-permute-done((bf16[2,128,512]{2,1,0:T(8,128)(2,1)S(1)}, bf16[2,128,512]{2,1,0:T(8,128)(2,1)}, u32[]{:S(2)}, u32[]{:S(2)}) %collective-permute-start.11) | collective-permute-done | bytes 262176 | tf_op jit(solution)/shard_map/ppermute | solution.py:291
  81.3 32.5 %shard_map.95 = (bf16[8,2,128,512]{3,2,1,0:T(8,128)(2,1)}, bf16[8,2,128,512]{3,2,1,0:T(8,128)(2,1)}, f32[2,128,512]{2,1,0:T(8,128)}, bf16[4,128,512]{2,1,0:T(8,1...) custom-call(s32[8,4]{1,0:T(8,128)} %copy.10.local, ...), custom_call_target="tpu_custom_call" | custom-call | flops 15300820992 | bytes 16777216 | tf_op jit(solution)/shard_map/pallas_call | solution.py:189
  113.9 4.4 %all-to-all-start.2 = ((bf16[8,2,128,512]{3,2,1,0:T(8,128)(2,1)}), bf16[8,2,128,512]{3,2,1,0:T(8,128)(2,1)S(1)}, u32[]{:S(2)}, u32[]{:S(2)}) async-start(bf16[8,2,128,512]{3,2,1,0:T(8,128)(2,1)} %get-tuple-element.21), calls=%async_computation.2 | async-start | bytes 4194304 | tf_op jit(solution)/shard_map/all_to_all | solution.py:321
  120.5 9.6 %collective-permute-start.16 = (bf16[2,128,512]{2,1,0:T(8,128)(2,1)S(1)}, bf16[2,128,512]{2,1,0:T(8,128)(2,1)S(1)}, u32[]{:S(2)}, u32[]{:S(2)}) collective-permute-start(bf16[2,128,512]{2,1,0:T(8,128)(2,1)S(1)} %copy-done.17), channel_id=1, source_target_pairs={{0,32},{8,40},{16,48},{24,56},{32,64},{40,72},{48,80},{56,88},{64,... | collective-permute-start | bytes 786440 | tf_op jit(solution)/shard_map/ppermute | solution.py:285
  130.2 3.2 %collective-permute-start.21 = (bf16[2,128,512]{2,1,0:T(8,128)(2,1)S(1)}, bf16[2,128,512]{2,1,0:T(8,128)(2,1)S(1)}, u32[]{:S(2)}, u32[]{:S(2)}) collective-permute-start(bf16[2,128,512]{2,1,0:T(8,128)(2,1)S(1)} %copy-done.19), channel_id=1, source_target_pairs={{0,24},{8,0},{16,8},{24,16},{32,56},{40,32},{48,40},{56,48},{64,88... | collective-permute-start | bytes 786440 | tf_op jit(solution)/shard_map/ppermute | solution.py:291
  133.6 5.7 %collective-permute-done.21 = bf16[2,128,512]{2,1,0:T(8,128)(2,1)S(1)} collective-permute-done((bf16[2,128,512]{2,1,0:T(8,128)(2,1)S(1)}, bf16[2,128,512]{2,1,0:T(8,128)(2,1)S(1)}, u32[]{:S(2)}, u32[]{:S(2)}) %collective-permute-start.21) | collective-permute-done | bytes 262176 | tf_op jit(solution)/shard_map/ppermute | solution.py:291
  139.5 3.8 %collective-permute-start.22 = (bf16[4,128,512]{2,1,0:T(8,128)(2,1)S(1)}, bf16[4,128,512]{2,1,0:T(8,128)(2,1)S(1)}, u32[]{:S(2)}, u32[]{:S(2)}) collective-permute-start(bf16[4,128,512]{2,1,0:T(8,128)(2,1)S(1)} %pad_maximum_fusion.4), channel_id=1, source_target_pairs={{0,24},{8,0},{16,8},{24,16},{32,56},{40,32},{48,40},{56,48},{64,88... | collective-permute-start | bytes 1572872 | tf_op jit(solution)/shard_map/ppermute | solution.py:291
  143.2 4.5 %collective-permute-done.16 = bf16[2,128,512]{2,1,0:T(8,128)(2,1)S(1)} collective-permute-done((bf16[2,128,512]{2,1,0:T(8,128)(2,1)S(1)}, bf16[2,128,512]{2,1,0:T(8,128)(2,1)S(1)}, u32[]{:S(2)}, u32[]{:S(2)}) %collective-permute-start.16) | collective-permute-done | bytes 262176 | tf_op jit(solution)/shard_map/ppermute | solution.py:285
  147.9 5.9 %collective-permute-start.17 = (bf16[4,128,512]{2,1,0:T(8,128)(2,1)S(1)}, bf16[4,128,512]{2,1,0:T(8,128)(2,1)S(1)}, u32[]{:S(2)}, u32[]{:S(2)}) collective-permute-start(bf16[4,128,512]{2,1,0:T(8,128)(2,1)S(1)} %pad_maximum_fusion.3), channel_id=1, source_target_pairs={{0,32},{8,40},{16,48},{24,56},{32,64},{40,72},{48,80},{56,88},{64,... | collective-permute-start | bytes 1572872 | tf_op jit(solution)/shard_map/ppermute | solution.py:285
  154.9 10.4 %collective-permute-start.25 = (bf16[128,512]{1,0:T(8,128)(2,1)S(1)}, bf16[128,512]{1,0:T(8,128)(2,1)S(1)}, u32[]{:S(2)}, u32[]{:S(2)}) collective-permute-start(bf16[128,512]{1,0:T(8,128)(2,1)S(1)} %get-tuple-element.45), channel_id=1, source_target_pairs={{0,96},{8,104},{16,112},{24,120},{32,0},{40,8},{48,16},{56,24},{64... | collective-permute-start | bytes 393224 | tf_op jit(solution)/shard_map/ppermute | solution.py:285
  165.3 4.6 %collective-permute-start.26 = (bf16[128,512]{1,0:T(8,128)(2,1)S(1)}, bf16[128,512]{1,0:T(8,128)(2,1)S(1)}, u32[]{:S(2)}, u32[]{:S(2)}) collective-permute-start(bf16[128,512]{1,0:T(8,128)(2,1)S(1)} %get-tuple-element.47), channel_id=1, source_target_pairs={{0,64},{8,72},{16,80},{24,88},{32,96},{40,104},{48,112},{56,120},{... | collective-permute-start | bytes 393224 | tf_op jit(solution)/shard_map/ppermute | solution.py:285
  170.2 3.8 %collective-permute-start.18 = (bf16[128,512]{1,0:T(8,128)(2,1)S(1)}, bf16[128,512]{1,0:T(8,128)(2,1)S(1)}, u32[]{:S(2)}, u32[]{:S(2)}) collective-permute-start(bf16[128,512]{1,0:T(8,128)(2,1)S(1)} %get-tuple-element.42), channel_id=1, source_target_pairs={{0,24},{8,0},{16,8},{24,16},{32,56},{40,32},{48,40},{56,48},{64,88... | collective-permute-start | bytes 393224 | tf_op jit(solution)/shard_map/ppermute | solution.py:291
  173.9 1.5 collective-permute-start.19
  175.5 1.6 collective-permute-done.18
  177.1 4.4 %collective-permute-done.20 = bf16[128,512]{1,0:T(8,128)(2,1)S(1)} collective-permute-done((bf16[128,512]{1,0:T(8,128)(2,1)S(1)}, bf16[128,512]{1,0:T(8,128)(2,1)S(1)}, u32[]{:S(2)}, u32[]{:S(2)}) %collective-permute-start.20) | collective-permute-done | bytes 131104 | tf_op jit(solution)/shard_map/ppermute | solution.py:291
  183.8 4.4 %all-to-all-start.3 = ((bf16[8,2,128,512]{3,2,1,0:T(8,128)(2,1)}), bf16[8,2,128,512]{3,2,1,0:T(8,128)(2,1)}, u32[]{:S(2)}, u32[]{:S(2)}) async-start(bf16[8,2,128,512]{3,2,1,0:T(8,128)(2,1)} %fusion.2), calls=%async_computation.3 | async-start | bytes 4194304 | tf_op jit(solution)/shard_map/all_to_all | solution.py:321
  188.1 2.6 %shard_map.96 = (bf16[128,4096]{1,0:T(8,128)(2,1)}, bf16[128,4096]{1,0:T(8,128)(2,1)}) custom-call(bf16[8,2,128,512]{3,2,1,0:T(8,128)(2,1)} %copy-done), custom_call_target="tpu_custom_call" | custom-call | bytes 4194304 | tf_op jit(solution)/shard_map/pallas_call | solution.py:270
  190.7 24.6 %all-to-all-done.3.got = bf16[8,2,128,512]{3,2,1,0:T(8,128)(2,1)} async-done(((bf16[8,2,128,512]{3,2,1,0:T(8,128)(2,1)}), bf16[8,2,128,512]{3,2,1,0:T(8,128)(2,1)}, u32[]{:S(2)}, u32[]{:S(2)}) %all-to-all-start.3) | async-done | bytes 2097184 | tf_op jit(solution)/shard_map/all_to_all | solution.py:321
  215.3 2.6 %shard_map.97 = (bf16[128,4096]{1,0:T(8,128)(2,1)}, bf16[128,4096]{1,0:T(8,128)(2,1)}) custom-call(bf16[8,2,128,512]{3,2,1,0:T(8,128)(2,1)} %all-to-all-done.3.got), custom_call_target="tpu_custom_call" | custom-call | bytes 4194304 | tf_op jit(solution)/shard_map/pallas_call | solution.py:270
  (104 shorter events, 17.5 us)
Async XLA Ops:
  3.2 32.5 %all-to-all-start = ((bf16[8,2,128,512]{3,2,1,0:T(8,128)(2,1)}), bf16[8,2,128,512]{3,2,1,0:T(8,128)(2,1)S(1)}, u32[]{:S(2)}, u32[]{:S(2)}) async-start(bf16[8,2,128,512]{3,2,1,0:T(8,128)(2,1)} %shard_map.93), calls=%async_computation | async-start | bytes 4194304 | tf_op jit(solution)/shard_map/all_to_all | solution.py:321
  35.8 38.5 %all-to-all-start.1 = ((bf16[8,2,128,512]{3,2,1,0:T(8,128)(2,1)}), bf16[8,2,128,512]{3,2,1,0:T(8,128)(2,1)}, u32[]{:S(2)}, u32[]{:S(2)}) async-start(bf16[8,2,128,512]{3,2,1,0:T(8,128)(2,1)} %shard_map.94), calls=%async_computation.1 | async-start | bytes 4194304 | tf_op jit(solution)/shard_map/all_to_all | solution.py:321
  40.9 9.2 %collective-permute-start.2 = (bf16[128,512]{1,0:T(8,128)(2,1)S(1)}, bf16[128,512]{1,0:T(8,128)(2,1)S(1)}, u32[]{:S(2)}, u32[]{:S(2)}) collective-permute-start(bf16[128,512]{1,0:T(8,128)(2,1)S(1)} %get-tuple-element.40), channel_id=1, source_target_pairs={{0,24},{8,0},{16,8},{24,16},{32,56},{40,32},{48,40},{56,48},{64,88... | collective-permute-start | bytes 393224 | tf_op jit(solution)/shard_map/ppermute | solution.py:291
  44.0 7.9 %collective-permute-start.1 = (bf16[128,512]{1,0:T(8,128)(2,1)S(1)}, bf16[128,512]{1,0:T(8,128)(2,1)S(1)}, u32[]{:S(2)}, u32[]{:S(2)}) collective-permute-start(bf16[128,512]{1,0:T(8,128)(2,1)S(1)} %get-tuple-element.40), channel_id=1, source_target_pairs={{0,16},{8,24},{16,0},{24,8},{32,48},{40,56},{48,32},{56,40},{64,80... | collective-permute-start | bytes 393224 | tf_op jit(solution)/shard_map/ppermute | solution.py:291
  44.6 9.2 %collective-permute-start = (bf16[128,512]{1,0:T(8,128)(2,1)S(1)}, bf16[128,512]{1,0:T(8,128)(2,1)S(1)}, u32[]{:S(2)}, u32[]{:S(2)}) collective-permute-start(bf16[128,512]{1,0:T(8,128)(2,1)S(1)} %get-tuple-element.40), channel_id=1, source_target_pairs={{0,8},{8,16},{16,24},{24,0},{32,40},{40,48},{48,56},{56,32},{64,72... | collective-permute-start | bytes 393224 | tf_op jit(solution)/shard_map/ppermute | solution.py:291
  45.6 10.4 %collective-permute-start.9 = (bf16[128,512]{1,0:T(8,128)(2,1)S(1)}, bf16[128,512]{1,0:T(8,128)(2,1)S(1)}, u32[]{:S(2)}, u32[]{:S(2)}) collective-permute-start(bf16[128,512]{1,0:T(8,128)(2,1)S(1)} %get-tuple-element.39), channel_id=1, source_target_pairs={{0,96},{8,104},{16,112},{24,120},{32,0},{40,8},{48,16},{56,24},{64... | collective-permute-start | bytes 393224 | tf_op jit(solution)/shard_map/ppermute | solution.py:285
  46.1 9.8 %collective-permute-start.8 = (bf16[128,512]{1,0:T(8,128)(2,1)S(1)}, bf16[128,512]{1,0:T(8,128)(2,1)S(1)}, u32[]{:S(2)}, u32[]{:S(2)}) collective-permute-start(bf16[128,512]{1,0:T(8,128)(2,1)S(1)} %get-tuple-element.39), channel_id=1, source_target_pairs={{0,64},{8,72},{16,80},{24,88},{32,96},{40,104},{48,112},{56,120},{... | collective-permute-start | bytes 393224 | tf_op jit(solution)/shard_map/ppermute | solution.py:285
  50.1 5.9 %collective-permute-start.7 = (bf16[128,512]{1,0:T(8,128)(2,1)S(1)}, bf16[128,512]{1,0:T(8,128)(2,1)S(1)}, u32[]{:S(2)}, u32[]{:S(2)}) collective-permute-start(bf16[128,512]{1,0:T(8,128)(2,1)S(1)} %get-tuple-element.39), channel_id=1, source_target_pairs={{0,32},{8,40},{16,48},{24,56},{32,64},{40,72},{48,80},{56,88},{64,... | collective-permute-start | bytes 393224 | tf_op jit(solution)/shard_map/ppermute | solution.py:285
  53.8 14.0 %collective-permute-start.5 = (bf16[4,128,512]{2,1,0:T(8,128)(2,1)S(1)}, bf16[4,128,512]{2,1,0:T(8,128)(2,1)S(1)}, u32[]{:S(2)}, u32[]{:S(2)}) collective-permute-start(bf16[4,128,512]{2,1,0:T(8,128)(2,1)S(1)} %pad_maximum_fusion.k0), channel_id=1, source_target_pairs={{0,96},{8,104},{16,112},{24,120},{32,0},{40,8},{48,16},{56,24},{64... | collective-permute-start | bytes 1572872 | tf_op jit(solution)/shard_map/ppermute | solution.py:285
  54.4 14.7 %collective-permute-start.3 = (bf16[4,128,512]{2,1,0:T(8,128)(2,1)S(1)}, bf16[4,128,512]{2,1,0:T(8,128)(2,1)S(1)}, u32[]{:S(2)}, u32[]{:S(2)}) collective-permute-start(bf16[4,128,512]{2,1,0:T(8,128)(2,1)S(1)} %pad_maximum_fusion.k0), channel_id=1, source_target_pairs={{0,32},{8,40},{16,48},{24,56},{32,64},{40,72},{48,80},{56,88},{64,... | collective-permute-start | bytes 1572872 | tf_op jit(solution)/shard_map/ppermute | solution.py:285
  56.0 14.0 %collective-permute-start.12 = (bf16[4,128,512]{2,1,0:T(8,128)(2,1)S(1)}, bf16[4,128,512]{2,1,0:T(8,128)(2,1)S(1)}, u32[]{:S(2)}, u32[]{:S(2)}) collective-permute-start(bf16[4,128,512]{2,1,0:T(8,128)(2,1)S(1)} %pad_maximum_fusion.1.v0), channel_id=1, source_target_pairs={{0,24},{8,0},{16,8},{24,16},{32,56},{40,32},{48,40},{56,48},{64,88... | collective-permute-start | bytes 1572872 | tf_op jit(solution)/shard_map/ppermute | solution.py:291
  59.9 12.9 %collective-permute-start.10 = (bf16[4,128,512]{2,1,0:T(8,128)(2,1)S(1)}, bf16[4,128,512]{2,1,0:T(8,128)(2,1)S(1)}, u32[]{:S(2)}, u32[]{:S(2)}) collective-permute-start(bf16[4,128,512]{2,1,0:T(8,128)(2,1)S(1)} %pad_maximum_fusion.1.v0), channel_id=1, source_target_pairs={{0,8},{8,16},{16,24},{24,0},{32,40},{40,48},{48,56},{56,32},{64,72... | collective-permute-start | bytes 1572872 | tf_op jit(solution)/shard_map/ppermute | solution.py:291
  67.9 7.7 %collective-permute-start.6 = (bf16[2,128,512]{2,1,0:T(8,128)(2,1)S(1)}, bf16[2,128,512]{2,1,0:T(8,128)(2,1)S(1)}, u32[]{:S(2)}, u32[]{:S(2)}) collective-permute-start(bf16[2,128,512]{2,1,0:T(8,128)(2,1)S(1)} %slice.97), channel_id=1, source_target_pairs={{0,96},{8,104},{16,112},{24,120},{32,0},{40,8},{48,16},{56,24},{64... | collective-permute-start | bytes 786440 | tf_op jit(solution)/shard_map/ppermute | solution.py:285
  69.2 9.0 %collective-permute-start.4 = (bf16[2,128,512]{2,1,0:T(8,128)(2,1)S(1)}, bf16[2,128,512]{2,1,0:T(8,128)(2,1)}, u32[]{:S(2)}, u32[]{:S(2)}) collective-permute-start(bf16[2,128,512]{2,1,0:T(8,128)(2,1)S(1)} %slice.96), channel_id=1, source_target_pairs={{0,32},{8,40},{16,48},{24,56},{32,64},{40,72},{48,80},{56,88},{64,... | collective-permute-start | bytes 786440 | tf_op jit(solution)/shard_map/ppermute | solution.py:285
  70.1 8.0 %collective-permute-start.13 = (bf16[2,128,512]{2,1,0:T(8,128)(2,1)S(1)}, bf16[2,128,512]{2,1,0:T(8,128)(2,1)}, u32[]{:S(2)}, u32[]{:S(2)}) collective-permute-start(bf16[2,128,512]{2,1,0:T(8,128)(2,1)S(1)} %slice.99), channel_id=1, source_target_pairs={{0,24},{8,0},{16,8},{24,16},{32,56},{40,32},{48,40},{56,48},{64,88... | collective-permute-start | bytes 786440 | tf_op jit(solution)/shard_map/ppermute | solution.py:291
  73.6 7.7 %collective-permute-start.11 = (bf16[2,128,512]{2,1,0:T(8,128)(2,1)S(1)}, bf16[2,128,512]{2,1,0:T(8,128)(2,1)}, u32[]{:S(2)}, u32[]{:S(2)}) collective-permute-start(bf16[2,128,512]{2,1,0:T(8,128)(2,1)S(1)} %slice.98), channel_id=1, source_target_pairs={{0,8},{8,16},{16,24},{24,0},{32,40},{40,48},{48,56},{56,32},{64,72... | collective-permute-start | bytes 786440 | tf_op jit(solution)/shard_map/ppermute | solution.py:291
  113.8 19.6 %collective-permute-start.23 = (bf16[2,128,512]{2,1,0:T(8,128)(2,1)}, bf16[2,128,512]{2,1,0:T(8,128)(2,1)S(1)}, u32[]{:S(2)}, u32[]{:S(2)}) collective-permute-start(bf16[2,128,512]{2,1,0:T(8,128)(2,1)} %get-tuple-element.35), channel_id=1, source_target_pairs={{0,8},{8,16},{16,24},{24,0},{32,40},{40,48},{48,56},{56,32},{64,72... | collective-permute-start | bytes 786440 | tf_op jit(solution)/shard_map/ppermute | solution.py:291
  113.9 68.5 %all-to-all-start.2 = ((bf16[8,2,128,512]{3,2,1,0:T(8,128)(2,1)}), bf16[8,2,128,512]{3,2,1,0:T(8,128)(2,1)S(1)}, u32[]{:S(2)}, u32[]{:S(2)}) async-start(bf16[8,2,128,512]{3,2,1,0:T(8,128)(2,1)} %get-tuple-element.21), calls=%async_computation.2 | async-start | bytes 4194304 | tf_op jit(solution)/shard_map/all_to_all | solution.py:321
  120.5 33.4 %collective-permute-start.14 = (bf16[2,128,512]{2,1,0:T(8,128)(2,1)S(1)}, bf16[2,128,512]{2,1,0:T(8,128)(2,1)S(1)}, u32[]{:S(2)}, u32[]{:S(2)}) collective-permute-start(bf16[2,128,512]{2,1,0:T(8,128)(2,1)S(1)} %copy-done.16), channel_id=1, source_target_pairs={{0,96},{8,104},{16,112},{24,120},{32,0},{40,8},{48,16},{56,24},{64... | collective-permute-start | bytes 786440 | tf_op jit(solution)/shard_map/ppermute | solution.py:285
  120.5 27.2 %collective-permute-start.16 = (bf16[2,128,512]{2,1,0:T(8,128)(2,1)S(1)}, bf16[2,128,512]{2,1,0:T(8,128)(2,1)S(1)}, u32[]{:S(2)}, u32[]{:S(2)}) collective-permute-start(bf16[2,128,512]{2,1,0:T(8,128)(2,1)S(1)} %copy-done.17), channel_id=1, source_target_pairs={{0,32},{8,40},{16,48},{24,56},{32,64},{40,72},{48,80},{56,88},{64,... | collective-permute-start | bytes 786440 | tf_op jit(solution)/shard_map/ppermute | solution.py:285
  130.2 9.1 %collective-permute-start.21 = (bf16[2,128,512]{2,1,0:T(8,128)(2,1)S(1)}, bf16[2,128,512]{2,1,0:T(8,128)(2,1)S(1)}, u32[]{:S(2)}, u32[]{:S(2)}) collective-permute-start(bf16[2,128,512]{2,1,0:T(8,128)(2,1)S(1)} %copy-done.19), channel_id=1, source_target_pairs={{0,24},{8,0},{16,8},{24,16},{32,56},{40,32},{48,40},{56,48},{64,88... | collective-permute-start | bytes 786440 | tf_op jit(solution)/shard_map/ppermute | solution.py:291
  133.5 21.1 %collective-permute-start.24 = (bf16[4,128,512]{2,1,0:T(8,128)(2,1)S(1)}, bf16[4,128,512]{2,1,0:T(8,128)(2,1)S(1)}, u32[]{:S(2)}, u32[]{:S(2)}) collective-permute-start(bf16[4,128,512]{2,1,0:T(8,128)(2,1)S(1)} %pad_maximum_fusion.5), channel_id=1, source_target_pairs={{0,8},{8,16},{16,24},{24,0},{32,40},{40,48},{48,56},{56,32},{64,72... | collective-permute-start | bytes 1572872 | tf_op jit(solution)/shard_map/ppermute | solution.py:291
  139.5 15.2 %collective-permute-start.22 = (bf16[4,128,512]{2,1,0:T(8,128)(2,1)S(1)}, bf16[4,128,512]{2,1,0:T(8,128)(2,1)S(1)}, u32[]{:S(2)}, u32[]{:S(2)}) collective-permute-start(bf16[4,128,512]{2,1,0:T(8,128)(2,1)S(1)} %pad_maximum_fusion.4), channel_id=1, source_target_pairs={{0,24},{8,0},{16,8},{24,16},{32,56},{40,32},{48,40},{56,48},{64,88... | collective-permute-start | bytes 1572872 | tf_op jit(solution)/shard_map/ppermute | solution.py:291
  147.9 22.0 %collective-permute-start.17 = (bf16[4,128,512]{2,1,0:T(8,128)(2,1)S(1)}, bf16[4,128,512]{2,1,0:T(8,128)(2,1)S(1)}, u32[]{:S(2)}, u32[]{:S(2)}) collective-permute-start(bf16[4,128,512]{2,1,0:T(8,128)(2,1)S(1)} %pad_maximum_fusion.3), channel_id=1, source_target_pairs={{0,32},{8,40},{16,48},{24,56},{32,64},{40,72},{48,80},{56,88},{64,... | collective-permute-start | bytes 1572872 | tf_op jit(solution)/shard_map/ppermute | solution.py:285
  154.0 15.9 %collective-permute-start.15 = (bf16[4,128,512]{2,1,0:T(8,128)(2,1)S(1)}, bf16[4,128,512]{2,1,0:T(8,128)(2,1)S(1)}, u32[]{:S(2)}, u32[]{:S(2)}) collective-permute-start(bf16[4,128,512]{2,1,0:T(8,128)(2,1)S(1)} %pad_maximum_fusion.2), channel_id=1, source_target_pairs={{0,96},{8,104},{16,112},{24,120},{32,0},{40,8},{48,16},{56,24},{64... | collective-permute-start | bytes 1572872 | tf_op jit(solution)/shard_map/ppermute | solution.py:285
  154.9 19.0 %collective-permute-start.25 = (bf16[128,512]{1,0:T(8,128)(2,1)S(1)}, bf16[128,512]{1,0:T(8,128)(2,1)S(1)}, u32[]{:S(2)}, u32[]{:S(2)}) collective-permute-start(bf16[128,512]{1,0:T(8,128)(2,1)S(1)} %get-tuple-element.45), channel_id=1, source_target_pairs={{0,96},{8,104},{16,112},{24,120},{32,0},{40,8},{48,16},{56,24},{64... | collective-permute-start | bytes 393224 | tf_op jit(solution)/shard_map/ppermute | solution.py:285
  165.3 10.2 %collective-permute-start.27 = (bf16[128,512]{1,0:T(8,128)(2,1)S(1)}, bf16[128,512]{1,0:T(8,128)(2,1)S(1)}, u32[]{:S(2)}, u32[]{:S(2)}) collective-permute-start(bf16[128,512]{1,0:T(8,128)(2,1)S(1)} %get-tuple-element.46), channel_id=1, source_target_pairs={{0,32},{8,40},{16,48},{24,56},{32,64},{40,72},{48,80},{56,88},{64,... | collective-permute-start | bytes 393224 | tf_op jit(solution)/shard_map/ppermute | solution.py:285
  165.3 10.2 %collective-permute-start.26 = (bf16[128,512]{1,0:T(8,128)(2,1)S(1)}, bf16[128,512]{1,0:T(8,128)(2,1)S(1)}, u32[]{:S(2)}, u32[]{:S(2)}) collective-permute-start(bf16[128,512]{1,0:T(8,128)(2,1)S(1)} %get-tuple-element.47), channel_id=1, source_target_pairs={{0,64},{8,72},{16,80},{24,88},{32,96},{40,104},{48,112},{56,120},{... | collective-permute-start | bytes 393224 | tf_op jit(solution)/shard_map/ppermute | solution.py:285
  170.2 7.0 %collective-permute-start.18 = (bf16[128,512]{1,0:T(8,128)(2,1)S(1)}, bf16[128,512]{1,0:T(8,128)(2,1)S(1)}, u32[]{:S(2)}, u32[]{:S(2)}) collective-permute-start(bf16[128,512]{1,0:T(8,128)(2,1)S(1)} %get-tuple-element.42), channel_id=1, source_target_pairs={{0,24},{8,0},{16,8},{24,16},{32,56},{40,32},{48,40},{56,48},{64,88... | collective-permute-start | bytes 393224 | tf_op jit(solution)/shard_map/ppermute | solution.py:291
  173.9 7.6 %collective-permute-start.20 = (bf16[128,512]{1,0:T(8,128)(2,1)S(1)}, bf16[128,512]{1,0:T(8,128)(2,1)S(1)}, u32[]{:S(2)}, u32[]{:S(2)}) collective-permute-start(bf16[128,512]{1,0:T(8,128)(2,1)S(1)} %get-tuple-element.43), channel_id=1, source_target_pairs={{0,8},{8,16},{16,24},{24,0},{32,40},{40,48},{48,56},{56,32},{64,72... | collective-permute-start | bytes 393224 | tf_op jit(solution)/shard_map/ppermute | solution.py:291
  173.9 7.6 %collective-permute-start.19 = (bf16[128,512]{1,0:T(8,128)(2,1)S(1)}, bf16[128,512]{1,0:T(8,128)(2,1)S(1)}, u32[]{:S(2)}, u32[]{:S(2)}) collective-permute-start(bf16[128,512]{1,0:T(8,128)(2,1)S(1)} %get-tuple-element.44), channel_id=1, source_target_pairs={{0,16},{8,24},{16,0},{24,8},{32,48},{40,56},{48,32},{56,40},{64,80... | collective-permute-start | bytes 393224 | tf_op jit(solution)/shard_map/ppermute | solution.py:291
  183.8 31.6 %all-to-all-start.3 = ((bf16[8,2,128,512]{3,2,1,0:T(8,128)(2,1)}), bf16[8,2,128,512]{3,2,1,0:T(8,128)(2,1)}, u32[]{:S(2)}, u32[]{:S(2)}) async-start(bf16[8,2,128,512]{3,2,1,0:T(8,128)(2,1)} %fusion.2), calls=%async_computation.3 | async-start | bytes 4194304 | tf_op jit(solution)/shard_map/all_to_all | solution.py:321
  (20 other events, 218.1 us)

commit v3 on v2

--- a/solution.py
+++ b/solution.py
@@ -117,6 +117,7 @@
     pl.loop(1, x + 1)(lambda sx: prob_far(sx, False))
     for b in range(NB):
         cols = slice(b * BLK, (b + 1) * BLK)
+        dp_ref[4, :, cols] = dot_nt(vl[b], qg[b, 1])
         p = jnp.exp2(s_ref[4, :, cols] * (SCALE * LOG2E) - mc[:, cols])
         sm[:, cols] += fold_sum(p)
         p_ref[4, :, cols] = p.astype(bf16)
@@ -137,13 +138,13 @@
 
     def grad_far(sx, first=False):
         lo = BLK if first else 0
+        fv[lo // BLK:, sx] = dot_nn(p_ref[sx, lo:], gs[...]).reshape(4 - lo // BLK, BLK, BLK).astype(bf16)
         for t in range(4):
             cols = slice(t * QT, (t + 1) * QT)
             for sy in range(lo // BLK, 4):
                 rows = slice(sy * BLK, (sy + 1) * BLK)
                 d_ref[sx, rows, cols] = p_ref[sx, rows, cols] * (dp_ref[sx, rows, cols] - delta[:, cols]).astype(bf16)
         dqt[...] += dot_nn(kt[sx, :, lo:], d_ref[sx, lo:])
-        fv[lo // BLK:, sx] = dot_nn(p_ref[sx, lo:], gs[...]).reshape(4 - lo // BLK, BLK, BLK).astype(bf16)
         fk[sx, lo // BLK:] = dot_nn(d_ref[sx, lo:], qs[...]).reshape(4 - lo // BLK, BLK, BLK).astype(bf16)
 
     grad_far(0, True)
@@ -156,10 +157,10 @@
         out[4][...] = far[3]
     for b in range(NB):
         cols = slice(b * BLK, (b + 1) * BLK)
-        dp = dot_nt(vl[b], qg[b, 1])
+        dv = dot_nn(p_ref[4, :, cols], gs[cols, :])
+        dp = dp_ref[4, :, cols]
         d_ref[4, :, cols] = p_ref[4, :, cols] * (dp - delta[:, cols]).astype(bf16)
         dqt[:, cols] += dot_nn(klt[b], d_ref[4, :, cols])
-        dv = dot_nn(p_ref[4, :, cols], gs[cols, :])
         dk = dot_nn(d_ref[4, :, cols], qs[cols, :])
         for i in range(4):
             idx = local[b, i]
@@ -197,7 +198,7 @@
             pltpu.VMEM((4, BLK, 512), bf16), pltpu.VMEM((4, BLK, 512), bf16),
             pltpu.VMEM((NB, 512, BLK), bf16), pltpu.VMEM((NB, 512, BLK), bf16),
             pltpu.VMEM((NB, BLK, 512), bf16), pltpu.VMEM((NB, BLK, 512), bf16),
-            pltpu.VMEM((5, 512, SPAN), f32), pltpu.VMEM((4, 512, SPAN), f32), pltpu.VMEM((5, 512, SPAN), bf16), pltpu.VMEM((5, 512, SPAN), bf16),
+            pltpu.VMEM((5, 512, SPAN), f32), pltpu.VMEM((5, 512, SPAN), f32), pltpu.VMEM((5, 512, SPAN), bf16), pltpu.VMEM((5, 512, SPAN), bf16),
             pltpu.VMEM((8, SPAN), f32), pltpu.VMEM((8, SPAN), f32),
             pltpu.VMEM((BLK, SPAN), f32), pltpu.VMEM((BLK, SPAN), f32),
             pltpu.VMEM((NB, BLK, BLK), f32), pltpu.VMEM((NB, BLK, BLK), f32),

time: 219 us -> 217 us (level)
  no operation moved by 1% of the time
where the time goes in v3:
time: 217 us; the launch traced here: 216 us
  waiting for transfers between devices  84.3 us (39%)
  starting transfers between devices  81.7 us (38%)
  Pallas kernels  41.1 us (19%)
  local copies, waits for them, and re-layouts  5.14 us (2%)
    all_to_all x4, waiting for transfers between devices, exchange(): lax.all_to_all(array, 'head', split_axis=0, concat_axis=0, tiled=True)  49.2 us
    ppermute x14, starting transfers between devices, along_x(): lax.ppermute(array, 'ctx', [(x * SIDE + y, (x + step) % SIDE * SIDE + y)...  39.5 us
    pallas_call x1, Pallas kernels, attention(): pl.pallas_call(attention_kernel, grid=(heads,), in_specs=[smem, smem, blo...  30.8 us
    ppermute x14, starting transfers between devices, along_y(): lax.ppermute(array, 'ctx', [(x * SIDE + y, x * SIDE + (y + step) % SIDE)...  23.7 us
    ppermute x14, waiting for transfers between devices, along_y(): lax.ppermute(array, 'ctx', [(x * SIDE + y, x * SIDE + (y + step) % SIDE)...  18.6 us
    all_to_all x4, starting transfers between devices, exchange(): lax.all_to_all(array, 'head', split_axis=0, concat_axis=0, tiled=True)  18.4 us
    ppermute x14, waiting for transfers between devices, along_x(): lax.ppermute(array, 'ctx', [(x * SIDE + y, (x + step) % SIDE * SIDE + y)...  16.5 us
    pallas_call x2, Pallas kernels, pack(): pl.pallas_call(pack_kernel, in_specs=[pl.BlockSpec(memory_space=pl.ANY)]...  5.24 us
  transfers between devices with their start and end apart: 32, of which 14 were waited for; matrix products, arithmetic and copies ran while one was open for 2% of the time, Pallas kernels for 2%

profile of v3, /device:TPU:2, one launch (start us, length us, event | category | flops | bytes accessed | tf_op | source)
XLA Modules:
  0.0 216.1 jit_solution(442860348090356422)
XLA Ops:
  0.6 2.6 %shard_map.93 = bf16[8,2,128,512]{3,2,1,0:T(8,128)(2,1)} custom-call(bf16[128,4096]{1,0:T(8,128)(2,1)} %refs_0_.2, bf16[128,4096]{1,0:T(8,128)(2,1)} %refs_1_.2), custom_call_target="tpu_custom_call" | custom-call | bytes 4194304 | tf_op jit(solution)/shard_map/pallas_call | solution.py:247
  3.2 5.3 %all-to-all-start = ((bf16[8,2,128,512]{3,2,1,0:T(8,128)(2,1)}), bf16[8,2,128,512]{3,2,1,0:T(8,128)(2,1)S(1)}, u32[]{:S(2)}, u32[]{:S(2)}) async-start(bf16[8,2,128,512]{3,2,1,0:T(8,128)(2,1)} %shard_map.93), calls=%async_computation | async-start | bytes 4194304 | tf_op jit(solution)/shard_map/all_to_all | solution.py:322
  8.6 2.6 %shard_map.94 = bf16[8,2,128,512]{3,2,1,0:T(8,128)(2,1)} custom-call(bf16[128,4096]{1,0:T(8,128)(2,1)} %refs_0_.3, bf16[128,4096]{1,0:T(8,128)(2,1)} %refs_1_.3), custom_call_target="tpu_custom_call" | custom-call | bytes 4194304 | tf_op jit(solution)/shard_map/pallas_call | solution.py:247
  11.2 24.6 %all-to-all-done.kv = bf16[8,2,128,512]{3,2,1,0:T(8,128)(2,1)S(1)} async-done(((bf16[8,2,128,512]{3,2,1,0:T(8,128)(2,1)}), bf16[8,2,128,512]{3,2,1,0:T(8,128)(2,1)S(1)}, u32[]{:S(2)}, u32[]{:S(2)}) %all-to-all-start) | async-done | bytes 2097184 | tf_op jit(solution)/shard_map/all_to_all | solution.py:322
  35.8 4.4 %all-to-all-start.1 = ((bf16[8,2,128,512]{3,2,1,0:T(8,128)(2,1)}), bf16[8,2,128,512]{3,2,1,0:T(8,128)(2,1)}, u32[]{:S(2)}, u32[]{:S(2)}) async-start(bf16[8,2,128,512]{3,2,1,0:T(8,128)(2,1)} %shard_map.94), calls=%async_computation.1 | async-start | bytes 4194304 | tf_op jit(solution)/shard_map/all_to_all | solution.py:322
  40.9 3.1 %collective-permute-start.2 = (bf16[128,512]{1,0:T(8,128)(2,1)S(1)}, bf16[128,512]{1,0:T(8,128)(2,1)S(1)}, u32[]{:S(2)}, u32[]{:S(2)}) collective-permute-start(bf16[128,512]{1,0:T(8,128)(2,1)S(1)} %get-tuple-element.40), channel_id=1, source_target_pairs={{0,24},{8,0},{16,8},{24,16},{32,56},{40,32},{48,40},{56,48},{64,88... | collective-permute-start | bytes 393224 | tf_op jit(solution)/shard_map/ppermute | solution.py:292
  46.1 2.4 %collective-permute-start.8 = (bf16[128,512]{1,0:T(8,128)(2,1)S(1)}, bf16[128,512]{1,0:T(8,128)(2,1)S(1)}, u32[]{:S(2)}, u32[]{:S(2)}) collective-permute-start(bf16[128,512]{1,0:T(8,128)(2,1)S(1)} %get-tuple-element.39), channel_id=1, source_target_pairs={{0,64},{8,72},{16,80},{24,88},{32,96},{40,104},{48,112},{56,120},{... | collective-permute-start | bytes 393224 | tf_op jit(solution)/shard_map/ppermute | solution.py:286
  48.5 1.5 collective-permute-done.2
  51.9 1.9 collective-permute-done
  56.0 3.9 %collective-permute-start.12 = (bf16[4,128,512]{2,1,0:T(8,128)(2,1)S(1)}, bf16[4,128,512]{2,1,0:T(8,128)(2,1)S(1)}, u32[]{:S(2)}, u32[]{:S(2)}) collective-permute-start(bf16[4,128,512]{2,1,0:T(8,128)(2,1)S(1)} %pad_maximum_fusion.1.v0), channel_id=1, source_target_pairs={{0,24},{8,0},{16,8},{24,16},{32,56},{40,32},{48,40},{56,48},{64,88... | collective-permute-start | bytes 1572872 | tf_op jit(solution)/shard_map/ppermute | solution.py:292
  59.9 7.9 %collective-permute-done.5.k3 = bf16[4,128,512]{2,1,0:T(8,128)(2,1)S(1)} collective-permute-done((bf16[4,128,512]{2,1,0:T(8,128)(2,1)S(1)}, bf16[4,128,512]{2,1,0:T(8,128)(2,1)S(1)}, u32[]{:S(2)}, u32[]{:S(2)}) %collective-permute-start.5) | collective-permute-done | bytes 524320 | tf_op jit(solution)/shard_map/ppermute | solution.py:286
  70.1 2.7 %collective-permute-start.13 = (bf16[2,128,512]{2,1,0:T(8,128)(2,1)S(1)}, bf16[2,128,512]{2,1,0:T(8,128)(2,1)}, u32[]{:S(2)}, u32[]{:S(2)}) collective-permute-start(bf16[2,128,512]{2,1,0:T(8,128)(2,1)S(1)} %slice.99), channel_id=1, source_target_pairs={{0,24},{8,0},{16,8},{24,16},{32,56},{40,32},{48,40},{56,48},{64,88... | collective-permute-start | bytes 786440 | tf_op jit(solution)/shard_map/ppermute | solution.py:292
  75.6 2.6 %collective-permute-done.4.k2a = bf16[2,128,512]{2,1,0:T(8,128)(2,1)} collective-permute-done((bf16[2,128,512]{2,1,0:T(8,128)(2,1)S(1)}, bf16[2,128,512]{2,1,0:T(8,128)(2,1)}, u32[]{:S(2)}, u32[]{:S(2)}) %collective-permute-start.4) | collective-permute-done | bytes 262176 | tf_op jit(solution)/shard_map/ppermute | solution.py:286
  78.1 3.2 %collective-permute-done.11.v2a = bf16[2,128,512]{2,1,0:T(8,128)(2,1)} collective-permute-done((bf16[2,128,512]{2,1,0:T(8,128)(2,1)S(1)}, bf16[2,128,512]{2,1,0:T(8,128)(2,1)}, u32[]{:S(2)}, u32[]{:S(2)}) %collective-permute-start.11) | collective-permute-done | bytes 262176 | tf_op jit(solution)/shard_map/ppermute | solution.py:292
  81.3 30.8 %shard_map.95 = (bf16[8,2,128,512]{3,2,1,0:T(8,128)(2,1)}, bf16[8,2,128,512]{3,2,1,0:T(8,128)(2,1)}, f32[2,128,512]{2,1,0:T(8,128)}, bf16[4,128,512]{2,1,0:T(8,1...) custom-call(s32[8,4]{1,0:T(8,128)} %copy.10.local, ...), custom_call_target="tpu_custom_call" | custom-call | flops 15300820992 | bytes 16777216 | tf_op jit(solution)/shard_map/pallas_call | solution.py:190
  112.2 4.4 %all-to-all-start.2 = ((bf16[8,2,128,512]{3,2,1,0:T(8,128)(2,1)}), bf16[8,2,128,512]{3,2,1,0:T(8,128)(2,1)S(1)}, u32[]{:S(2)}, u32[]{:S(2)}) async-start(bf16[8,2,128,512]{3,2,1,0:T(8,128)(2,1)} %get-tuple-element.21), calls=%async_computation.2 | async-start | bytes 4194304 | tf_op jit(solution)/shard_map/all_to_all | solution.py:322
  118.8 9.5 %collective-permute-start.16 = (bf16[2,128,512]{2,1,0:T(8,128)(2,1)S(1)}, bf16[2,128,512]{2,1,0:T(8,128)(2,1)S(1)}, u32[]{:S(2)}, u32[]{:S(2)}) collective-permute-start(bf16[2,128,512]{2,1,0:T(8,128)(2,1)S(1)} %copy-done.17), channel_id=1, source_target_pairs={{0,32},{8,40},{16,48},{24,56},{32,64},{40,72},{48,80},{56,88},{64,... | collective-permute-start | bytes 786440 | tf_op jit(solution)/shard_map/ppermute | solution.py:286
  128.4 3.2 %collective-permute-start.21 = (bf16[2,128,512]{2,1,0:T(8,128)(2,1)S(1)}, bf16[2,128,512]{2,1,0:T(8,128)(2,1)S(1)}, u32[]{:S(2)}, u32[]{:S(2)}) collective-permute-start(bf16[2,128,512]{2,1,0:T(8,128)(2,1)S(1)} %copy-done.19), channel_id=1, source_target_pairs={{0,24},{8,0},{16,8},{24,16},{32,56},{40,32},{48,40},{56,48},{64,88... | collective-permute-start | bytes 786440 | tf_op jit(solution)/shard_map/ppermute | solution.py:292
  131.8 5.7 %collective-permute-done.21 = bf16[2,128,512]{2,1,0:T(8,128)(2,1)S(1)} collective-permute-done((bf16[2,128,512]{2,1,0:T(8,128)(2,1)S(1)}, bf16[2,128,512]{2,1,0:T(8,128)(2,1)S(1)}, u32[]{:S(2)}, u32[]{:S(2)}) %collective-permute-start.21) | collective-permute-done | bytes 262176 | tf_op jit(solution)/shard_map/ppermute | solution.py:292
  137.7 3.8 %collective-permute-start.22 = (bf16[4,128,512]{2,1,0:T(8,128)(2,1)S(1)}, bf16[4,128,512]{2,1,0:T(8,128)(2,1)S(1)}, u32[]{:S(2)}, u32[]{:S(2)}) collective-permute-start(bf16[4,128,512]{2,1,0:T(8,128)(2,1)S(1)} %pad_maximum_fusion.4), channel_id=1, source_target_pairs={{0,24},{8,0},{16,8},{24,16},{32,56},{40,32},{48,40},{56,48},{64,88... | collective-permute-start | bytes 1572872 | tf_op jit(solution)/shard_map/ppermute | solution.py:292
  141.4 4.4 %collective-permute-done.16 = bf16[2,128,512]{2,1,0:T(8,128)(2,1)S(1)} collective-permute-done((bf16[2,128,512]{2,1,0:T(8,128)(2,1)S(1)}, bf16[2,128,512]{2,1,0:T(8,128)(2,1)S(1)}, u32[]{:S(2)}, u32[]{:S(2)}) %collective-permute-start.16) | collective-permute-done | bytes 262176 | tf_op jit(solution)/shard_map/ppermute | solution.py:286
  145.9 5.9 %collective-permute-start.17 = (bf16[4,128,512]{2,1,0:T(8,128)(2,1)S(1)}, bf16[4,128,512]{2,1,0:T(8,128)(2,1)S(1)}, u32[]{:S(2)}, u32[]{:S(2)}) collective-permute-start(bf16[4,128,512]{2,1,0:T(8,128)(2,1)S(1)} %pad_maximum_fusion.3), channel_id=1, source_target_pairs={{0,32},{8,40},{16,48},{24,56},{32,64},{40,72},{48,80},{56,88},{64,... | collective-permute-start | bytes 1572872 | tf_op jit(solution)/shard_map/ppermute | solution.py:286
  152.9 10.4 %collective-permute-start.25 = (bf16[128,512]{1,0:T(8,128)(2,1)S(1)}, bf16[128,512]{1,0:T(8,128)(2,1)S(1)}, u32[]{:S(2)}, u32[]{:S(2)}) collective-permute-start(bf16[128,512]{1,0:T(8,128)(2,1)S(1)} %get-tuple-element.45), channel_id=1, source_target_pairs={{0,96},{8,104},{16,112},{24,120},{32,0},{40,8},{48,16},{56,24},{64... | collective-permute-start | bytes 393224 | tf_op jit(solution)/shard_map/ppermute | solution.py:286
  163.3 4.6 %collective-permute-start.26 = (bf16[128,512]{1,0:T(8,128)(2,1)S(1)}, bf16[128,512]{1,0:T(8,128)(2,1)S(1)}, u32[]{:S(2)}, u32[]{:S(2)}) collective-permute-start(bf16[128,512]{1,0:T(8,128)(2,1)S(1)} %get-tuple-element.47), channel_id=1, source_target_pairs={{0,64},{8,72},{16,80},{24,88},{32,96},{40,104},{48,112},{56,120},{... | collective-permute-start | bytes 393224 | tf_op jit(solution)/shard_map/ppermute | solution.py:286
  168.2 3.8 %collective-permute-start.18 = (bf16[128,512]{1,0:T(8,128)(2,1)S(1)}, bf16[128,512]{1,0:T(8,128)(2,1)S(1)}, u32[]{:S(2)}, u32[]{:S(2)}) collective-permute-start(bf16[128,512]{1,0:T(8,128)(2,1)S(1)} %get-tuple-element.42), channel_id=1, source_target_pairs={{0,24},{8,0},{16,8},{24,16},{32,56},{40,32},{48,40},{56,48},{64,88... | collective-permute-start | bytes 393224 | tf_op jit(solution)/shard_map/ppermute | solution.py:292
  172.0 1.5 collective-permute-start.19
  173.6 1.6 collective-permute-done.18
  175.1 4.4 %collective-permute-done.20 = bf16[128,512]{1,0:T(8,128)(2,1)S(1)} collective-permute-done((bf16[128,512]{1,0:T(8,128)(2,1)S(1)}, bf16[128,512]{1,0:T(8,128)(2,1)S(1)}, u32[]{:S(2)}, u32[]{:S(2)}) %collective-permute-start.20) | collective-permute-done | bytes 131104 | tf_op jit(solution)/shard_map/ppermute | solution.py:292
  181.8 4.4 %all-to-all-start.3 = ((bf16[8,2,128,512]{3,2,1,0:T(8,128)(2,1)}), bf16[8,2,128,512]{3,2,1,0:T(8,128)(2,1)}, u32[]{:S(2)}, u32[]{:S(2)}) async-start(bf16[8,2,128,512]{3,2,1,0:T(8,128)(2,1)} %fusion.2), calls=%async_computation.3 | async-start | bytes 4194304 | tf_op jit(solution)/shard_map/all_to_all | solution.py:322
  186.2 2.6 %shard_map.96 = (bf16[128,4096]{1,0:T(8,128)(2,1)}, bf16[128,4096]{1,0:T(8,128)(2,1)}) custom-call(bf16[8,2,128,512]{3,2,1,0:T(8,128)(2,1)} %copy-done), custom_call_target="tpu_custom_call" | custom-call | bytes 4194304 | tf_op jit(solution)/shard_map/pallas_call | solution.py:271
  188.7 24.6 %all-to-all-done.3.got = bf16[8,2,128,512]{3,2,1,0:T(8,128)(2,1)} async-done(((bf16[8,2,128,512]{3,2,1,0:T(8,128)(2,1)}), bf16[8,2,128,512]{3,2,1,0:T(8,128)(2,1)}, u32[]{:S(2)}, u32[]{:S(2)}) %all-to-all-start.3) | async-done | bytes 2097184 | tf_op jit(solution)/shard_map/all_to_all | solution.py:322
  213.3 2.6 %shard_map.97 = (bf16[128,4096]{1,0:T(8,128)(2,1)}, bf16[128,4096]{1,0:T(8,128)(2,1)}) custom-call(bf16[8,2,128,512]{3,2,1,0:T(8,128)(2,1)} %all-to-all-done.3.got), custom_call_target="tpu_custom_call" | custom-call | bytes 4194304 | tf_op jit(solution)/shard_map/pallas_call | solution.py:271
  (104 shorter events, 17.5 us)
Async XLA Ops:
  3.2 32.5 %all-to-all-start = ((bf16[8,2,128,512]{3,2,1,0:T(8,128)(2,1)}), bf16[8,2,128,512]{3,2,1,0:T(8,128)(2,1)S(1)}, u32[]{:S(2)}, u32[]{:S(2)}) async-start(bf16[8,2,128,512]{3,2,1,0:T(8,128)(2,1)} %shard_map.93), calls=%async_computation | async-start | bytes 4194304 | tf_op jit(solution)/shard_map/all_to_all | solution.py:322
  35.8 38.5 %all-to-all-start.1 = ((bf16[8,2,128,512]{3,2,1,0:T(8,128)(2,1)}), bf16[8,2,128,512]{3,2,1,0:T(8,128)(2,1)}, u32[]{:S(2)}, u32[]{:S(2)}) async-start(bf16[8,2,128,512]{3,2,1,0:T(8,128)(2,1)} %shard_map.94), calls=%async_computation.1 | async-start | bytes 4194304 | tf_op jit(solution)/shard_map/all_to_all | solution.py:322
  40.9 9.2 %collective-permute-start.2 = (bf16[128,512]{1,0:T(8,128)(2,1)S(1)}, bf16[128,512]{1,0:T(8,128)(2,1)S(1)}, u32[]{:S(2)}, u32[]{:S(2)}) collective-permute-start(bf16[128,512]{1,0:T(8,128)(2,1)S(1)} %get-tuple-element.40), channel_id=1, source_target_pairs={{0,24},{8,0},{16,8},{24,16},{32,56},{40,32},{48,40},{56,48},{64,88... | collective-permute-start | bytes 393224 | tf_op jit(solution)/shard_map/ppermute | solution.py:292
  44.0 7.9 %collective-permute-start.1 = (bf16[128,512]{1,0:T(8,128)(2,1)S(1)}, bf16[128,512]{1,0:T(8,128)(2,1)S(1)}, u32[]{:S(2)}, u32[]{:S(2)}) collective-permute-start(bf16[128,512]{1,0:T(8,128)(2,1)S(1)} %get-tuple-element.40), channel_id=1, source_target_pairs={{0,16},{8,24},{16,0},{24,8},{32,48},{40,56},{48,32},{56,40},{64,80... | collective-permute-start | bytes 393224 | tf_op jit(solution)/shard_map/ppermute | solution.py:292
  44.6 9.2 %collective-permute-start = (bf16[128,512]{1,0:T(8,128)(2,1)S(1)}, bf16[128,512]{1,0:T(8,128)(2,1)S(1)}, u32[]{:S(2)}, u32[]{:S(2)}) collective-permute-start(bf16[128,512]{1,0:T(8,128)(2,1)S(1)} %get-tuple-element.40), channel_id=1, source_target_pairs={{0,8},{8,16},{16,24},{24,0},{32,40},{40,48},{48,56},{56,32},{64,72... | collective-permute-start | bytes 393224 | tf_op jit(solution)/shard_map/ppermute | solution.py:292
  45.6 10.4 %collective-permute-start.9 = (bf16[128,512]{1,0:T(8,128)(2,1)S(1)}, bf16[128,512]{1,0:T(8,128)(2,1)S(1)}, u32[]{:S(2)}, u32[]{:S(2)}) collective-permute-start(bf16[128,512]{1,0:T(8,128)(2,1)S(1)} %get-tuple-element.39), channel_id=1, source_target_pairs={{0,96},{8,104},{16,112},{24,120},{32,0},{40,8},{48,16},{56,24},{64... | collective-permute-start | bytes 393224 | tf_op jit(solution)/shard_map/ppermute | solution.py:286
  46.1 9.8 %collective-permute-start.8 = (bf16[128,512]{1,0:T(8,128)(2,1)S(1)}, bf16[128,512]{1,0:T(8,128)(2,1)S(1)}, u32[]{:S(2)}, u32[]{:S(2)}) collective-permute-start(bf16[128,512]{1,0:T(8,128)(2,1)S(1)} %get-tuple-element.39), channel_id=1, source_target_pairs={{0,64},{8,72},{16,80},{24,88},{32,96},{40,104},{48,112},{56,120},{... | collective-permute-start | bytes 393224 | tf_op jit(solution)/shard_map/ppermute | solution.py:286
  50.1 5.9 %collective-permute-start.7 = (bf16[128,512]{1,0:T(8,128)(2,1)S(1)}, bf16[128,512]{1,0:T(8,128)(2,1)S(1)}, u32[]{:S(2)}, u32[]{:S(2)}) collective-permute-start(bf16[128,512]{1,0:T(8,128)(2,1)S(1)} %get-tuple-element.39), channel_id=1, source_target_pairs={{0,32},{8,40},{16,48},{24,56},{32,64},{40,72},{48,80},{56,88},{64,... | collective-permute-start | bytes 393224 | tf_op jit(solution)/shard_map/ppermute | solution.py:286
  53.8 14.0 %collective-permute-start.5 = (bf16[4,128,512]{2,1,0:T(8,128)(2,1)S(1)}, bf16[4,128,512]{2,1,0:T(8,128)(2,1)S(1)}, u32[]{:S(2)}, u32[]{:S(2)}) collective-permute-start(bf16[4,128,512]{2,1,0:T(8,128)(2,1)S(1)} %pad_maximum_fusion.k0), channel_id=1, source_target_pairs={{0,96},{8,104},{16,112},{24,120},{32,0},{40,8},{48,16},{56,24},{64... | collective-permute-start | bytes 1572872 | tf_op jit(solution)/shard_map/ppermute | solution.py:286
  54.4 14.7 %collective-permute-start.3 = (bf16[4,128,512]{2,1,0:T(8,128)(2,1)S(1)}, bf16[4,128,512]{2,1,0:T(8,128)(2,1)S(1)}, u32[]{:S(2)}, u32[]{:S(2)}) collective-permute-start(bf16[4,128,512]{2,1,0:T(8,128)(2,1)S(1)} %pad_maximum_fusion.k0), channel_id=1, source_target_pairs={{0,32},{8,40},{16,48},{24,56},{32,64},{40,72},{48,80},{56,88},{64,... | collective-permute-start | bytes 1572872 | tf_op jit(solution)/shard_map/ppermute | solution.py:286
  56.0 14.0 %collective-permute-start.12 = (bf16[4,128,512]{2,1,0:T(8,128)(2,1)S(1)}, bf16[4,128,512]{2,1,0:T(8,128)(2,1)S(1)}, u32[]{:S(2)}, u32[]{:S(2)}) collective-permute-start(bf16[4,128,512]{2,1,0:T(8,128)(2,1)S(1)} %pad_maximum_fusion.1.v0), channel_id=1, source_target_pairs={{0,24},{8,0},{16,8},{24,16},{32,56},{40,32},{48,40},{56,48},{64,88... | collective-permute-start | bytes 1572872 | tf_op jit(solution)/shard_map/ppermute | solution.py:292
  59.9 12.9 %collective-permute-start.10 = (bf16[4,128,512]{2,1,0:T(8,128)(2,1)S(1)}, bf16[4,128,512]{2,1,0:T(8,128)(2,1)S(1)}, u32[]{:S(2)}, u32[]{:S(2)}) collective-permute-start(bf16[4,128,512]{2,1,0:T(8,128)(2,1)S(1)} %pad_maximum_fusion.1.v0), channel_id=1, source_target_pairs={{0,8},{8,16},{16,24},{24,0},{32,40},{40,48},{48,56},{56,32},{64,72... | collective-permute-start | bytes 1572872 | tf_op jit(solution)/shard_map/ppermute | solution.py:292
  67.9 7.7 %collective-permute-start.6 = (bf16[2,128,512]{2,1,0:T(8,128)(2,1)S(1)}, bf16[2,128,512]{2,1,0:T(8,128)(2,1)S(1)}, u32[]{:S(2)}, u32[]{:S(2)}) collective-permute-start(bf16[2,128,512]{2,1,0:T(8,128)(2,1)S(1)} %slice.97), channel_id=1, source_target_pairs={{0,96},{8,104},{16,112},{24,120},{32,0},{40,8},{48,16},{56,24},{64... | collective-permute-start | bytes 786440 | tf_op jit(solution)/shard_map/ppermute | solution.py:286
  69.2 9.0 %collective-permute-start.4 = (bf16[2,128,512]{2,1,0:T(8,128)(2,1)S(1)}, bf16[2,128,512]{2,1,0:T(8,128)(2,1)}, u32[]{:S(2)}, u32[]{:S(2)}) collective-permute-start(bf16[2,128,512]{2,1,0:T(8,128)(2,1)S(1)} %slice.96), channel_id=1, source_target_pairs={{0,32},{8,40},{16,48},{24,56},{32,64},{40,72},{48,80},{56,88},{64,... | collective-permute-start | bytes 786440 | tf_op jit(solution)/shard_map/ppermute | solution.py:286
  70.1 8.0 %collective-permute-start.13 = (bf16[2,128,512]{2,1,0:T(8,128)(2,1)S(1)}, bf16[2,128,512]{2,1,0:T(8,128)(2,1)}, u32[]{:S(2)}, u32[]{:S(2)}) collective-permute-start(bf16[2,128,512]{2,1,0:T(8,128)(2,1)S(1)} %slice.99), channel_id=1, source_target_pairs={{0,24},{8,0},{16,8},{24,16},{32,56},{40,32},{48,40},{56,48},{64,88... | collective-permute-start | bytes 786440 | tf_op jit(solution)/shard_map/ppermute | solution.py:292
  73.6 7.7 %collective-permute-start.11 = (bf16[2,128,512]{2,1,0:T(8,128)(2,1)S(1)}, bf16[2,128,512]{2,1,0:T(8,128)(2,1)}, u32[]{:S(2)}, u32[]{:S(2)}) collective-permute-start(bf16[2,128,512]{2,1,0:T(8,128)(2,1)S(1)} %slice.98), channel_id=1, source_target_pairs={{0,8},{8,16},{16,24},{24,0},{32,40},{40,48},{48,56},{56,32},{64,72... | collective-permute-start | bytes 786440 | tf_op jit(solution)/shard_map/ppermute | solution.py:292
  112.1 19.5 %collective-permute-start.23 = (bf16[2,128,512]{2,1,0:T(8,128)(2,1)}, bf16[2,128,512]{2,1,0:T(8,128)(2,1)S(1)}, u32[]{:S(2)}, u32[]{:S(2)}) collective-permute-start(bf16[2,128,512]{2,1,0:T(8,128)(2,1)} %get-tuple-element.35), channel_id=1, source_target_pairs={{0,8},{8,16},{16,24},{24,0},{32,40},{40,48},{48,56},{56,32},{64,72... | collective-permute-start | bytes 786440 | tf_op jit(solution)/shard_map/ppermute | solution.py:292
  112.2 68.2 %all-to-all-start.2 = ((bf16[8,2,128,512]{3,2,1,0:T(8,128)(2,1)}), bf16[8,2,128,512]{3,2,1,0:T(8,128)(2,1)S(1)}, u32[]{:S(2)}, u32[]{:S(2)}) async-start(bf16[8,2,128,512]{3,2,1,0:T(8,128)(2,1)} %get-tuple-element.21), calls=%async_computation.2 | async-start | bytes 4194304 | tf_op jit(solution)/shard_map/all_to_all | solution.py:322
  118.8 33.1 %collective-permute-start.14 = (bf16[2,128,512]{2,1,0:T(8,128)(2,1)S(1)}, bf16[2,128,512]{2,1,0:T(8,128)(2,1)S(1)}, u32[]{:S(2)}, u32[]{:S(2)}) collective-permute-start(bf16[2,128,512]{2,1,0:T(8,128)(2,1)S(1)} %copy-done.16), channel_id=1, source_target_pairs={{0,96},{8,104},{16,112},{24,120},{32,0},{40,8},{48,16},{56,24},{64... | collective-permute-start | bytes 786440 | tf_op jit(solution)/shard_map/ppermute | solution.py:286
  118.8 27.0 %collective-permute-start.16 = (bf16[2,128,512]{2,1,0:T(8,128)(2,1)S(1)}, bf16[2,128,512]{2,1,0:T(8,128)(2,1)S(1)}, u32[]{:S(2)}, u32[]{:S(2)}) collective-permute-start(bf16[2,128,512]{2,1,0:T(8,128)(2,1)S(1)} %copy-done.17), channel_id=1, source_target_pairs={{0,32},{8,40},{16,48},{24,56},{32,64},{40,72},{48,80},{56,88},{64,... | collective-permute-start | bytes 786440 | tf_op jit(solution)/shard_map/ppermute | solution.py:286
  128.4 9.1 %collective-permute-start.21 = (bf16[2,128,512]{2,1,0:T(8,128)(2,1)S(1)}, bf16[2,128,512]{2,1,0:T(8,128)(2,1)S(1)}, u32[]{:S(2)}, u32[]{:S(2)}) collective-permute-start(bf16[2,128,512]{2,1,0:T(8,128)(2,1)S(1)} %copy-done.19), channel_id=1, source_target_pairs={{0,24},{8,0},{16,8},{24,16},{32,56},{40,32},{48,40},{56,48},{64,88... | collective-permute-start | bytes 786440 | tf_op jit(solution)/shard_map/ppermute | solution.py:292
  131.7 20.9 %collective-permute-start.24 = (bf16[4,128,512]{2,1,0:T(8,128)(2,1)S(1)}, bf16[4,128,512]{2,1,0:T(8,128)(2,1)S(1)}, u32[]{:S(2)}, u32[]{:S(2)}) collective-permute-start(bf16[4,128,512]{2,1,0:T(8,128)(2,1)S(1)} %pad_maximum_fusion.5), channel_id=1, source_target_pairs={{0,8},{8,16},{16,24},{24,0},{32,40},{40,48},{48,56},{56,32},{64,72... | collective-permute-start | bytes 1572872 | tf_op jit(solution)/shard_map/ppermute | solution.py:292
  137.7 15.0 %collective-permute-start.22 = (bf16[4,128,512]{2,1,0:T(8,128)(2,1)S(1)}, bf16[4,128,512]{2,1,0:T(8,128)(2,1)S(1)}, u32[]{:S(2)}, u32[]{:S(2)}) collective-permute-start(bf16[4,128,512]{2,1,0:T(8,128)(2,1)S(1)} %pad_maximum_fusion.4), channel_id=1, source_target_pairs={{0,24},{8,0},{16,8},{24,16},{32,56},{40,32},{48,40},{56,48},{64,88... | collective-permute-start | bytes 1572872 | tf_op jit(solution)/shard_map/ppermute | solution.py:292
  145.9 22.0 %collective-permute-start.17 = (bf16[4,128,512]{2,1,0:T(8,128)(2,1)S(1)}, bf16[4,128,512]{2,1,0:T(8,128)(2,1)S(1)}, u32[]{:S(2)}, u32[]{:S(2)}) collective-permute-start(bf16[4,128,512]{2,1,0:T(8,128)(2,1)S(1)} %pad_maximum_fusion.3), channel_id=1, source_target_pairs={{0,32},{8,40},{16,48},{24,56},{32,64},{40,72},{48,80},{56,88},{64,... | collective-permute-start | bytes 1572872 | tf_op jit(solution)/shard_map/ppermute | solution.py:286
  152.0 15.9 %collective-permute-start.15 = (bf16[4,128,512]{2,1,0:T(8,128)(2,1)S(1)}, bf16[4,128,512]{2,1,0:T(8,128)(2,1)S(1)}, u32[]{:S(2)}, u32[]{:S(2)}) collective-permute-start(bf16[4,128,512]{2,1,0:T(8,128)(2,1)S(1)} %pad_maximum_fusion.2), channel_id=1, source_target_pairs={{0,96},{8,104},{16,112},{24,120},{32,0},{40,8},{48,16},{56,24},{64... | collective-permute-start | bytes 1572872 | tf_op jit(solution)/shard_map/ppermute | solution.py:286
  152.9 19.0 %collective-permute-start.25 = (bf16[128,512]{1,0:T(8,128)(2,1)S(1)}, bf16[128,512]{1,0:T(8,128)(2,1)S(1)}, u32[]{:S(2)}, u32[]{:S(2)}) collective-permute-start(bf16[128,512]{1,0:T(8,128)(2,1)S(1)} %get-tuple-element.45), channel_id=1, source_target_pairs={{0,96},{8,104},{16,112},{24,120},{32,0},{40,8},{48,16},{56,24},{64... | collective-permute-start | bytes 393224 | tf_op jit(solution)/shard_map/ppermute | solution.py:286
  163.3 10.2 %collective-permute-start.27 = (bf16[128,512]{1,0:T(8,128)(2,1)S(1)}, bf16[128,512]{1,0:T(8,128)(2,1)S(1)}, u32[]{:S(2)}, u32[]{:S(2)}) collective-permute-start(bf16[128,512]{1,0:T(8,128)(2,1)S(1)} %get-tuple-element.46), channel_id=1, source_target_pairs={{0,32},{8,40},{16,48},{24,56},{32,64},{40,72},{48,80},{56,88},{64,... | collective-permute-start | bytes 393224 | tf_op jit(solution)/shard_map/ppermute | solution.py:286
  163.3 10.2 %collective-permute-start.26 = (bf16[128,512]{1,0:T(8,128)(2,1)S(1)}, bf16[128,512]{1,0:T(8,128)(2,1)S(1)}, u32[]{:S(2)}, u32[]{:S(2)}) collective-permute-start(bf16[128,512]{1,0:T(8,128)(2,1)S(1)} %get-tuple-element.47), channel_id=1, source_target_pairs={{0,64},{8,72},{16,80},{24,88},{32,96},{40,104},{48,112},{56,120},{... | collective-permute-start | bytes 393224 | tf_op jit(solution)/shard_map/ppermute | solution.py:286
  168.2 7.0 %collective-permute-start.18 = (bf16[128,512]{1,0:T(8,128)(2,1)S(1)}, bf16[128,512]{1,0:T(8,128)(2,1)S(1)}, u32[]{:S(2)}, u32[]{:S(2)}) collective-permute-start(bf16[128,512]{1,0:T(8,128)(2,1)S(1)} %get-tuple-element.42), channel_id=1, source_target_pairs={{0,24},{8,0},{16,8},{24,16},{32,56},{40,32},{48,40},{56,48},{64,88... | collective-permute-start | bytes 393224 | tf_op jit(solution)/shard_map/ppermute | solution.py:292
  171.9 7.6 %collective-permute-start.20 = (bf16[128,512]{1,0:T(8,128)(2,1)S(1)}, bf16[128,512]{1,0:T(8,128)(2,1)S(1)}, u32[]{:S(2)}, u32[]{:S(2)}) collective-permute-start(bf16[128,512]{1,0:T(8,128)(2,1)S(1)} %get-tuple-element.43), channel_id=1, source_target_pairs={{0,8},{8,16},{16,24},{24,0},{32,40},{40,48},{48,56},{56,32},{64,72... | collective-permute-start | bytes 393224 | tf_op jit(solution)/shard_map/ppermute | solution.py:292
  172.0 7.6 %collective-permute-start.19 = (bf16[128,512]{1,0:T(8,128)(2,1)S(1)}, bf16[128,512]{1,0:T(8,128)(2,1)S(1)}, u32[]{:S(2)}, u32[]{:S(2)}) collective-permute-start(bf16[128,512]{1,0:T(8,128)(2,1)S(1)} %get-tuple-element.44), channel_id=1, source_target_pairs={{0,16},{8,24},{16,0},{24,8},{32,48},{40,56},{48,32},{56,40},{64,80... | collective-permute-start | bytes 393224 | tf_op jit(solution)/shard_map/ppermute | solution.py:292
  181.8 31.6 %all-to-all-start.3 = ((bf16[8,2,128,512]{3,2,1,0:T(8,128)(2,1)}), bf16[8,2,128,512]{3,2,1,0:T(8,128)(2,1)}, u32[]{:S(2)}, u32[]{:S(2)}) async-start(bf16[8,2,128,512]{3,2,1,0:T(8,128)(2,1)} %fusion.2), calls=%async_computation.3 | async-start | bytes 4194304 | tf_op jit(solution)/shard_map/all_to_all | solution.py:322
  (20 other events, 217.7 us)

commit v4 on v3

--- a/solution.py
+++ b/solution.py
@@ -76,8 +76,6 @@
                 top = fold_max(s)
             mx[:, cols] = jnp.maximum(mx[:, cols], top)
 
-    score_far(0, True)
-    pl.loop(1, x + 1)(lambda sx: score_far(sx, False))
 
     def local_scores(b):
         for i in range(4):
@@ -91,8 +89,10 @@
         s_ref[4, :, cols] = s
         mx[:, cols] = jnp.maximum(mx[:, cols], fold_max(s))
 
+    score_far(0, True)
     for b in range(NB):
         local_scores(b)
+    pl.loop(1, x + 1)(lambda sx: score_far(sx, False))
 
     mc = mx[...].max(0, keepdims=True) * (SCALE * LOG2E)
 
@@ -114,7 +114,6 @@
             ot[:, cols] += dot_nn(vt[sx, :, lo:], p_ref[sx, lo:, cols])
 
     prob_far(0, True)
-    pl.loop(1, x + 1)(lambda sx: prob_far(sx, False))
     for b in range(NB):
         cols = slice(b * BLK, (b + 1) * BLK)
         dp_ref[4, :, cols] = dot_nt(vl[b], qg[b, 1])
@@ -122,6 +121,7 @@
         sm[:, cols] += fold_sum(p)
         p_ref[4, :, cols] = p.astype(bf16)
         ot[:, cols] += dot_nn(vlt[b], p_ref[4, :, cols])
+    pl.loop(1, x + 1)(lambda sx: prob_far(sx, False))
 
     inv = 1.0 / sm[...].sum(0, keepdims=True)
     deltas = []
@@ -148,13 +148,6 @@
         fk[sx, lo // BLK:] = dot_nn(d_ref[sx, lo:], qs[...]).reshape(4 - lo // BLK, BLK, BLK).astype(bf16)
 
     grad_far(0, True)
-    pl.loop(1, x + 1)(grad_far)
-    for out, far in (((gk0, gk1, gk2a, gk2b, gk3), fk), ((gv0, gv1, gv2a, gv2b, gv3), fv)):
-        out[0][...] = far[0]
-        out[1][...] = far[1]
-        out[2][...] = far[2, :2]
-        out[3][...] = far[2, 2:]
-        out[4][...] = far[3]
     for b in range(NB):
         cols = slice(b * BLK, (b + 1) * BLK)
         dv = dot_nn(p_ref[4, :, cols], gs[cols, :])
@@ -166,6 +159,15 @@
             idx = local[b, i]
             dk_acc[idx] += dk[i * BLK:(i + 1) * BLK]
             dv_acc[idx] += dv[i * BLK:(i + 1) * BLK]
+    pl.loop(1, x + 1)(grad_far)
+    for out, far in (((gk0, gk1, gk2a, gk2b, gk3), fk), ((gv0, gv1, gv2a, gv2b, gv3), fv)):
+        out[0][...] = far[0]
+        out[1][...] = far[1]
+        out[2][...] = far[2, :2]
+        out[3][...] = far[2, 2:]
+        out[4][...] = far[3]
+    for b in range(NB):
+        cols = slice(b * BLK, (b + 1) * BLK)
         ao[b, 1] = (dqt[:, cols] * (inv[:, cols] * SCALE)).T.astype(bf16)
     dl[:, 0] = dk_acc[...].astype(bf16)
     dl[:, 1] = dv_acc[...].astype(bf16)

time: 217 us -> 216 us (level)
  no operation moved by 1% of the time
where the time goes in v4:
time: 216 us; the launch traced here: 215 us
  waiting for transfers between devices  84.5 us (39%)
  starting transfers between devices  81.7 us (38%)
  Pallas kernels  40.2 us (19%)
  local copies, waits for them, and re-layouts  5.14 us (2%)
    all_to_all x4, waiting for transfers between devices, exchange(): lax.all_to_all(array, 'head', split_axis=0, concat_axis=0, tiled=True)  49.2 us
    ppermute x14, starting transfers between devices, along_x(): lax.ppermute(array, 'ctx', [(x * SIDE + y, (x + step) % SIDE * SIDE + y)...  39.6 us
    pallas_call x1, Pallas kernels, attention(): pl.pallas_call(attention_kernel, grid=(heads,), in_specs=[smem, smem, blo...  29.8 us
    ppermute x14, starting transfers between devices, along_y(): lax.ppermute(array, 'ctx', [(x * SIDE + y, x * SIDE + (y + step) % SIDE)...  23.7 us
    ppermute x14, waiting for transfers between devices, along_y(): lax.ppermute(array, 'ctx', [(x * SIDE + y, x * SIDE + (y + step) % SIDE)...  18.6 us
    all_to_all x4, starting transfers between devices, exchange(): lax.all_to_all(array, 'head', split_axis=0, concat_axis=0, tiled=True)  18.4 us
    ppermute x14, waiting for transfers between devices, along_x(): lax.ppermute(array, 'ctx', [(x * SIDE + y, (x + step) % SIDE * SIDE + y)...  16.7 us
    pallas_call x2, Pallas kernels, pack(): pl.pallas_call(pack_kernel, in_specs=[pl.BlockSpec(memory_space=pl.ANY)]...  5.24 us
  transfers between devices with their start and end apart: 32, of which 14 were waited for; matrix products, arithmetic and copies ran while one was open for 2% of the time, Pallas kernels for 2%

profile of v4, /device:TPU:2, one launch (start us, length us, event | category | flops | bytes accessed | tf_op | source)
XLA Modules:
  0.0 215.3 jit_solution(8848446942161492586)
XLA Ops:
  0.6 2.6 %shard_map.93 = bf16[8,2,128,512]{3,2,1,0:T(8,128)(2,1)} custom-call(bf16[128,4096]{1,0:T(8,128)(2,1)} %refs_0_.2, bf16[128,4096]{1,0:T(8,128)(2,1)} %refs_1_.2), custom_call_target="tpu_custom_call" | custom-call | bytes 4194304 | tf_op jit(solution)/shard_map/pallas_call | solution.py:249
  3.2 5.3 %all-to-all-start = ((bf16[8,2,128,512]{3,2,1,0:T(8,128)(2,1)}), bf16[8,2,128,512]{3,2,1,0:T(8,128)(2,1)S(1)}, u32[]{:S(2)}, u32[]{:S(2)}) async-start(bf16[8,2,128,512]{3,2,1,0:T(8,128)(2,1)} %shard_map.93), calls=%async_computation | async-start | bytes 4194304 | tf_op jit(solution)/shard_map/all_to_all | solution.py:324
  8.6 2.6 %shard_map.94 = bf16[8,2,128,512]{3,2,1,0:T(8,128)(2,1)} custom-call(bf16[128,4096]{1,0:T(8,128)(2,1)} %refs_0_.3, bf16[128,4096]{1,0:T(8,128)(2,1)} %refs_1_.3), custom_call_target="tpu_custom_call" | custom-call | bytes 4194304 | tf_op jit(solution)/shard_map/pallas_call | solution.py:249
  11.2 24.6 %all-to-all-done.kv = bf16[8,2,128,512]{3,2,1,0:T(8,128)(2,1)S(1)} async-done(((bf16[8,2,128,512]{3,2,1,0:T(8,128)(2,1)}), bf16[8,2,128,512]{3,2,1,0:T(8,128)(2,1)S(1)}, u32[]{:S(2)}, u32[]{:S(2)}) %all-to-all-start) | async-done | bytes 2097184 | tf_op jit(solution)/shard_map/all_to_all | solution.py:324
  35.8 4.4 %all-to-all-start.1 = ((bf16[8,2,128,512]{3,2,1,0:T(8,128)(2,1)}), bf16[8,2,128,512]{3,2,1,0:T(8,128)(2,1)}, u32[]{:S(2)}, u32[]{:S(2)}) async-start(bf16[8,2,128,512]{3,2,1,0:T(8,128)(2,1)} %shard_map.94), calls=%async_computation.1 | async-start | bytes 4194304 | tf_op jit(solution)/shard_map/all_to_all | solution.py:324
  40.9 3.1 %collective-permute-start.2 = (bf16[128,512]{1,0:T(8,128)(2,1)S(1)}, bf16[128,512]{1,0:T(8,128)(2,1)S(1)}, u32[]{:S(2)}, u32[]{:S(2)}) collective-permute-start(bf16[128,512]{1,0:T(8,128)(2,1)S(1)} %get-tuple-element.40), channel_id=1, source_target_pairs={{0,24},{8,0},{16,8},{24,16},{32,56},{40,32},{48,40},{56,48},{64,88... | collective-permute-start | bytes 393224 | tf_op jit(solution)/shard_map/ppermute | solution.py:294
  46.1 2.4 %collective-permute-start.8 = (bf16[128,512]{1,0:T(8,128)(2,1)S(1)}, bf16[128,512]{1,0:T(8,128)(2,1)S(1)}, u32[]{:S(2)}, u32[]{:S(2)}) collective-permute-start(bf16[128,512]{1,0:T(8,128)(2,1)S(1)} %get-tuple-element.39), channel_id=1, source_target_pairs={{0,64},{8,72},{16,80},{24,88},{32,96},{40,104},{48,112},{56,120},{... | collective-permute-start | bytes 393224 | tf_op jit(solution)/shard_map/ppermute | solution.py:288
  48.5 1.5 collective-permute-done.2
  51.9 1.9 collective-permute-done
  56.0 3.9 %collective-permute-start.12 = (bf16[4,128,512]{2,1,0:T(8,128)(2,1)S(1)}, bf16[4,128,512]{2,1,0:T(8,128)(2,1)S(1)}, u32[]{:S(2)}, u32[]{:S(2)}) collective-permute-start(bf16[4,128,512]{2,1,0:T(8,128)(2,1)S(1)} %pad_maximum_fusion.1.v0), channel_id=1, source_target_pairs={{0,24},{8,0},{16,8},{24,16},{32,56},{40,32},{48,40},{56,48},{64,88... | collective-permute-start | bytes 1572872 | tf_op jit(solution)/shard_map/ppermute | solution.py:294
  59.9 7.9 %collective-permute-done.5.k3 = bf16[4,128,512]{2,1,0:T(8,128)(2,1)S(1)} collective-permute-done((bf16[4,128,512]{2,1,0:T(8,128)(2,1)S(1)}, bf16[4,128,512]{2,1,0:T(8,128)(2,1)S(1)}, u32[]{:S(2)}, u32[]{:S(2)}) %collective-permute-start.5) | collective-permute-done | bytes 524320 | tf_op jit(solution)/shard_map/ppermute | solution.py:288
  70.1 2.7 %collective-permute-start.13 = (bf16[2,128,512]{2,1,0:T(8,128)(2,1)S(1)}, bf16[2,128,512]{2,1,0:T(8,128)(2,1)}, u32[]{:S(2)}, u32[]{:S(2)}) collective-permute-start(bf16[2,128,512]{2,1,0:T(8,128)(2,1)S(1)} %slice.99), channel_id=1, source_target_pairs={{0,24},{8,0},{16,8},{24,16},{32,56},{40,32},{48,40},{56,48},{64,88... | collective-permute-start | bytes 786440 | tf_op jit(solution)/shard_map/ppermute | solution.py:294
  75.6 2.6 %collective-permute-done.4.k2a = bf16[2,128,512]{2,1,0:T(8,128)(2,1)} collective-permute-done((bf16[2,128,512]{2,1,0:T(8,128)(2,1)S(1)}, bf16[2,128,512]{2,1,0:T(8,128)(2,1)}, u32[]{:S(2)}, u32[]{:S(2)}) %collective-permute-start.4) | collective-permute-done | bytes 262176 | tf_op jit(solution)/shard_map/ppermute | solution.py:288
  78.1 3.2 %collective-permute-done.11.v2a = bf16[2,128,512]{2,1,0:T(8,128)(2,1)} collective-permute-done((bf16[2,128,512]{2,1,0:T(8,128)(2,1)S(1)}, bf16[2,128,512]{2,1,0:T(8,128)(2,1)}, u32[]{:S(2)}, u32[]{:S(2)}) %collective-permute-start.11) | collective-permute-done | bytes 262176 | tf_op jit(solution)/shard_map/ppermute | solution.py:294
  81.3 29.8 %shard_map.95 = (bf16[8,2,128,512]{3,2,1,0:T(8,128)(2,1)}, bf16[8,2,128,512]{3,2,1,0:T(8,128)(2,1)}, f32[2,128,512]{2,1,0:T(8,128)}, bf16[4,128,512]{2,1,0:T(8,1...) custom-call(s32[8,4]{1,0:T(8,128)} %copy.10.local, ...), custom_call_target="tpu_custom_call" | custom-call | flops 15300820992 | bytes 16777216 | tf_op jit(solution)/shard_map/pallas_call | solution.py:192
  111.3 4.4 %all-to-all-start.2 = ((bf16[8,2,128,512]{3,2,1,0:T(8,128)(2,1)}), bf16[8,2,128,512]{3,2,1,0:T(8,128)(2,1)S(1)}, u32[]{:S(2)}, u32[]{:S(2)}) async-start(bf16[8,2,128,512]{3,2,1,0:T(8,128)(2,1)} %get-tuple-element.21), calls=%async_computation.2 | async-start | bytes 4194304 | tf_op jit(solution)/shard_map/all_to_all | solution.py:324
  117.9 9.6 %collective-permute-start.16 = (bf16[2,128,512]{2,1,0:T(8,128)(2,1)S(1)}, bf16[2,128,512]{2,1,0:T(8,128)(2,1)S(1)}, u32[]{:S(2)}, u32[]{:S(2)}) collective-permute-start(bf16[2,128,512]{2,1,0:T(8,128)(2,1)S(1)} %copy-done.17), channel_id=1, source_target_pairs={{0,32},{8,40},{16,48},{24,56},{32,64},{40,72},{48,80},{56,88},{64,... | collective-permute-start | bytes 786440 | tf_op jit(solution)/shard_map/ppermute | solution.py:288
  127.5 3.2 %collective-permute-start.21 = (bf16[2,128,512]{2,1,0:T(8,128)(2,1)S(1)}, bf16[2,128,512]{2,1,0:T(8,128)(2,1)S(1)}, u32[]{:S(2)}, u32[]{:S(2)}) collective-permute-start(bf16[2,128,512]{2,1,0:T(8,128)(2,1)S(1)} %copy-done.19), channel_id=1, source_target_pairs={{0,24},{8,0},{16,8},{24,16},{32,56},{40,32},{48,40},{56,48},{64,88... | collective-permute-start | bytes 786440 | tf_op jit(solution)/shard_map/ppermute | solution.py:294
  130.9 5.7 %collective-permute-done.21 = bf16[2,128,512]{2,1,0:T(8,128)(2,1)S(1)} collective-permute-done((bf16[2,128,512]{2,1,0:T(8,128)(2,1)S(1)}, bf16[2,128,512]{2,1,0:T(8,128)(2,1)S(1)}, u32[]{:S(2)}, u32[]{:S(2)}) %collective-permute-start.21) | collective-permute-done | bytes 262176 | tf_op jit(solution)/shard_map/ppermute | solution.py:294
  136.8 3.8 %collective-permute-start.22 = (bf16[4,128,512]{2,1,0:T(8,128)(2,1)S(1)}, bf16[4,128,512]{2,1,0:T(8,128)(2,1)S(1)}, u32[]{:S(2)}, u32[]{:S(2)}) collective-permute-start(bf16[4,128,512]{2,1,0:T(8,128)(2,1)S(1)} %pad_maximum_fusion.4), channel_id=1, source_target_pairs={{0,24},{8,0},{16,8},{24,16},{32,56},{40,32},{48,40},{56,48},{64,88... | collective-permute-start | bytes 1572872 | tf_op jit(solution)/shard_map/ppermute | solution.py:294
  140.6 4.5 %collective-permute-done.16 = bf16[2,128,512]{2,1,0:T(8,128)(2,1)S(1)} collective-permute-done((bf16[2,128,512]{2,1,0:T(8,128)(2,1)S(1)}, bf16[2,128,512]{2,1,0:T(8,128)(2,1)S(1)}, u32[]{:S(2)}, u32[]{:S(2)}) %collective-permute-start.16) | collective-permute-done | bytes 262176 | tf_op jit(solution)/shard_map/ppermute | solution.py:288
  145.2 5.9 %collective-permute-start.17 = (bf16[4,128,512]{2,1,0:T(8,128)(2,1)S(1)}, bf16[4,128,512]{2,1,0:T(8,128)(2,1)S(1)}, u32[]{:S(2)}, u32[]{:S(2)}) collective-permute-start(bf16[4,128,512]{2,1,0:T(8,128)(2,1)S(1)} %pad_maximum_fusion.3), channel_id=1, source_target_pairs={{0,32},{8,40},{16,48},{24,56},{32,64},{40,72},{48,80},{56,88},{64,... | collective-permute-start | bytes 1572872 | tf_op jit(solution)/shard_map/ppermute | solution.py:288
  152.2 10.4 %collective-permute-start.25 = (bf16[128,512]{1,0:T(8,128)(2,1)S(1)}, bf16[128,512]{1,0:T(8,128)(2,1)S(1)}, u32[]{:S(2)}, u32[]{:S(2)}) collective-permute-start(bf16[128,512]{1,0:T(8,128)(2,1)S(1)} %get-tuple-element.45), channel_id=1, source_target_pairs={{0,96},{8,104},{16,112},{24,120},{32,0},{40,8},{48,16},{56,24},{64... | collective-permute-start | bytes 393224 | tf_op jit(solution)/shard_map/ppermute | solution.py:288
  162.5 4.6 %collective-permute-start.26 = (bf16[128,512]{1,0:T(8,128)(2,1)S(1)}, bf16[128,512]{1,0:T(8,128)(2,1)S(1)}, u32[]{:S(2)}, u32[]{:S(2)}) collective-permute-start(bf16[128,512]{1,0:T(8,128)(2,1)S(1)} %get-tuple-element.47), channel_id=1, source_target_pairs={{0,64},{8,72},{16,80},{24,88},{32,96},{40,104},{48,112},{56,120},{... | collective-permute-start | bytes 393224 | tf_op jit(solution)/shard_map/ppermute | solution.py:288
  167.4 3.8 %collective-permute-start.18 = (bf16[128,512]{1,0:T(8,128)(2,1)S(1)}, bf16[128,512]{1,0:T(8,128)(2,1)S(1)}, u32[]{:S(2)}, u32[]{:S(2)}) collective-permute-start(bf16[128,512]{1,0:T(8,128)(2,1)S(1)} %get-tuple-element.42), channel_id=1, source_target_pairs={{0,24},{8,0},{16,8},{24,16},{32,56},{40,32},{48,40},{56,48},{64,88... | collective-permute-start | bytes 393224 | tf_op jit(solution)/shard_map/ppermute | solution.py:294
  171.2 1.5 collective-permute-start.19
  172.8 1.6 collective-permute-done.18
  174.4 4.4 %collective-permute-done.20 = bf16[128,512]{1,0:T(8,128)(2,1)S(1)} collective-permute-done((bf16[128,512]{1,0:T(8,128)(2,1)S(1)}, bf16[128,512]{1,0:T(8,128)(2,1)S(1)}, u32[]{:S(2)}, u32[]{:S(2)}) %collective-permute-start.20) | collective-permute-done | bytes 131104 | tf_op jit(solution)/shard_map/ppermute | solution.py:294
  181.0 4.4 %all-to-all-start.3 = ((bf16[8,2,128,512]{3,2,1,0:T(8,128)(2,1)}), bf16[8,2,128,512]{3,2,1,0:T(8,128)(2,1)}, u32[]{:S(2)}, u32[]{:S(2)}) async-start(bf16[8,2,128,512]{3,2,1,0:T(8,128)(2,1)} %fusion.2), calls=%async_computation.3 | async-start | bytes 4194304 | tf_op jit(solution)/shard_map/all_to_all | solution.py:324
  185.4 2.6 %shard_map.96 = (bf16[128,4096]{1,0:T(8,128)(2,1)}, bf16[128,4096]{1,0:T(8,128)(2,1)}) custom-call(bf16[8,2,128,512]{3,2,1,0:T(8,128)(2,1)} %copy-done), custom_call_target="tpu_custom_call" | custom-call | bytes 4194304 | tf_op jit(solution)/shard_map/pallas_call | solution.py:273
  188.0 24.6 %all-to-all-done.3.got = bf16[8,2,128,512]{3,2,1,0:T(8,128)(2,1)} async-done(((bf16[8,2,128,512]{3,2,1,0:T(8,128)(2,1)}), bf16[8,2,128,512]{3,2,1,0:T(8,128)(2,1)}, u32[]{:S(2)}, u32[]{:S(2)}) %all-to-all-start.3) | async-done | bytes 2097184 | tf_op jit(solution)/shard_map/all_to_all | solution.py:324
  212.6 2.6 %shard_map.97 = (bf16[128,4096]{1,0:T(8,128)(2,1)}, bf16[128,4096]{1,0:T(8,128)(2,1)}) custom-call(bf16[8,2,128,512]{3,2,1,0:T(8,128)(2,1)} %all-to-all-done.3.got), custom_call_target="tpu_custom_call" | custom-call | bytes 4194304 | tf_op jit(solution)/shard_map/pallas_call | solution.py:273
  (104 shorter events, 17.5 us)
Async XLA Ops:
  3.2 32.5 %all-to-all-start = ((bf16[8,2,128,512]{3,2,1,0:T(8,128)(2,1)}), bf16[8,2,128,512]{3,2,1,0:T(8,128)(2,1)S(1)}, u32[]{:S(2)}, u32[]{:S(2)}) async-start(bf16[8,2,128,512]{3,2,1,0:T(8,128)(2,1)} %shard_map.93), calls=%async_computation | async-start | bytes 4194304 | tf_op jit(solution)/shard_map/all_to_all | solution.py:324
  35.8 38.5 %all-to-all-start.1 = ((bf16[8,2,128,512]{3,2,1,0:T(8,128)(2,1)}), bf16[8,2,128,512]{3,2,1,0:T(8,128)(2,1)}, u32[]{:S(2)}, u32[]{:S(2)}) async-start(bf16[8,2,128,512]{3,2,1,0:T(8,128)(2,1)} %shard_map.94), calls=%async_computation.1 | async-start | bytes 4194304 | tf_op jit(solution)/shard_map/all_to_all | solution.py:324
  40.9 9.2 %collective-permute-start.2 = (bf16[128,512]{1,0:T(8,128)(2,1)S(1)}, bf16[128,512]{1,0:T(8,128)(2,1)S(1)}, u32[]{:S(2)}, u32[]{:S(2)}) collective-permute-start(bf16[128,512]{1,0:T(8,128)(2,1)S(1)} %get-tuple-element.40), channel_id=1, source_target_pairs={{0,24},{8,0},{16,8},{24,16},{32,56},{40,32},{48,40},{56,48},{64,88... | collective-permute-start | bytes 393224 | tf_op jit(solution)/shard_map/ppermute | solution.py:294
  44.0 7.9 %collective-permute-start.1 = (bf16[128,512]{1,0:T(8,128)(2,1)S(1)}, bf16[128,512]{1,0:T(8,128)(2,1)S(1)}, u32[]{:S(2)}, u32[]{:S(2)}) collective-permute-start(bf16[128,512]{1,0:T(8,128)(2,1)S(1)} %get-tuple-element.40), channel_id=1, source_target_pairs={{0,16},{8,24},{16,0},{24,8},{32,48},{40,56},{48,32},{56,40},{64,80... | collective-permute-start | bytes 393224 | tf_op jit(solution)/shard_map/ppermute | solution.py:294
  44.6 9.2 %collective-permute-start = (bf16[128,512]{1,0:T(8,128)(2,1)S(1)}, bf16[128,512]{1,0:T(8,128)(2,1)S(1)}, u32[]{:S(2)}, u32[]{:S(2)}) collective-permute-start(bf16[128,512]{1,0:T(8,128)(2,1)S(1)} %get-tuple-element.40), channel_id=1, source_target_pairs={{0,8},{8,16},{16,24},{24,0},{32,40},{40,48},{48,56},{56,32},{64,72... | collective-permute-start | bytes 393224 | tf_op jit(solution)/shard_map/ppermute | solution.py:294
  45.6 10.4 %collective-permute-start.9 = (bf16[128,512]{1,0:T(8,128)(2,1)S(1)}, bf16[128,512]{1,0:T(8,128)(2,1)S(1)}, u32[]{:S(2)}, u32[]{:S(2)}) collective-permute-start(bf16[128,512]{1,0:T(8,128)(2,1)S(1)} %get-tuple-element.39), channel_id=1, source_target_pairs={{0,96},{8,104},{16,112},{24,120},{32,0},{40,8},{48,16},{56,24},{64... | collective-permute-start | bytes 393224 | tf_op jit(solution)/shard_map/ppermute | solution.py:288
  46.1 9.8 %collective-permute-start.8 = (bf16[128,512]{1,0:T(8,128)(2,1)S(1)}, bf16[128,512]{1,0:T(8,128)(2,1)S(1)}, u32[]{:S(2)}, u32[]{:S(2)}) collective-permute-start(bf16[128,512]{1,0:T(8,128)(2,1)S(1)} %get-tuple-element.39), channel_id=1, source_target_pairs={{0,64},{8,72},{16,80},{24,88},{32,96},{40,104},{48,112},{56,120},{... | collective-permute-start | bytes 393224 | tf_op jit(solution)/shard_map/ppermute | solution.py:288
  50.1 5.9 %collective-permute-start.7 = (bf16[128,512]{1,0:T(8,128)(2,1)S(1)}, bf16[128,512]{1,0:T(8,128)(2,1)S(1)}, u32[]{:S(2)}, u32[]{:S(2)}) collective-permute-start(bf16[128,512]{1,0:T(8,128)(2,1)S(1)} %get-tuple-element.39), channel_id=1, source_target_pairs={{0,32},{8,40},{16,48},{24,56},{32,64},{40,72},{48,80},{56,88},{64,... | collective-permute-start | bytes 393224 | tf_op jit(solution)/shard_map/ppermute | solution.py:288
  53.8 14.0 %collective-permute-start.5 = (bf16[4,128,512]{2,1,0:T(8,128)(2,1)S(1)}, bf16[4,128,512]{2,1,0:T(8,128)(2,1)S(1)}, u32[]{:S(2)}, u32[]{:S(2)}) collective-permute-start(bf16[4,128,512]{2,1,0:T(8,128)(2,1)S(1)} %pad_maximum_fusion.k0), channel_id=1, source_target_pairs={{0,96},{8,104},{16,112},{24,120},{32,0},{40,8},{48,16},{56,24},{64... | collective-permute-start | bytes 1572872 | tf_op jit(solution)/shard_map/ppermute | solution.py:288
  54.4 14.7 %collective-permute-start.3 = (bf16[4,128,512]{2,1,0:T(8,128)(2,1)S(1)}, bf16[4,128,512]{2,1,0:T(8,128)(2,1)S(1)}, u32[]{:S(2)}, u32[]{:S(2)}) collective-permute-start(bf16[4,128,512]{2,1,0:T(8,128)(2,1)S(1)} %pad_maximum_fusion.k0), channel_id=1, source_target_pairs={{0,32},{8,40},{16,48},{24,56},{32,64},{40,72},{48,80},{56,88},{64,... | collective-permute-start | bytes 1572872 | tf_op jit(solution)/shard_map/ppermute | solution.py:288
  56.0 14.0 %collective-permute-start.12 = (bf16[4,128,512]{2,1,0:T(8,128)(2,1)S(1)}, bf16[4,128,512]{2,1,0:T(8,128)(2,1)S(1)}, u32[]{:S(2)}, u32[]{:S(2)}) collective-permute-start(bf16[4,128,512]{2,1,0:T(8,128)(2,1)S(1)} %pad_maximum_fusion.1.v0), channel_id=1, source_target_pairs={{0,24},{8,0},{16,8},{24,16},{32,56},{40,32},{48,40},{56,48},{64,88... | collective-permute-start | bytes 1572872 | tf_op jit(solution)/shard_map/ppermute | solution.py:294
  59.9 12.9 %collective-permute-start.10 = (bf16[4,128,512]{2,1,0:T(8,128)(2,1)S(1)}, bf16[4,128,512]{2,1,0:T(8,128)(2,1)S(1)}, u32[]{:S(2)}, u32[]{:S(2)}) collective-permute-start(bf16[4,128,512]{2,1,0:T(8,128)(2,1)S(1)} %pad_maximum_fusion.1.v0), channel_id=1, source_target_pairs={{0,8},{8,16},{16,24},{24,0},{32,40},{40,48},{48,56},{56,32},{64,72... | collective-permute-start | bytes 1572872 | tf_op jit(solution)/shard_map/ppermute | solution.py:294
  67.9 7.7 %collective-permute-start.6 = (bf16[2,128,512]{2,1,0:T(8,128)(2,1)S(1)}, bf16[2,128,512]{2,1,0:T(8,128)(2,1)S(1)}, u32[]{:S(2)}, u32[]{:S(2)}) collective-permute-start(bf16[2,128,512]{2,1,0:T(8,128)(2,1)S(1)} %slice.97), channel_id=1, source_target_pairs={{0,96},{8,104},{16,112},{24,120},{32,0},{40,8},{48,16},{56,24},{64... | collective-permute-start | bytes 786440 | tf_op jit(solution)/shard_map/ppermute | solution.py:288
  69.2 9.0 %collective-permute-start.4 = (bf16[2,128,512]{2,1,0:T(8,128)(2,1)S(1)}, bf16[2,128,512]{2,1,0:T(8,128)(2,1)}, u32[]{:S(2)}, u32[]{:S(2)}) collective-permute-start(bf16[2,128,512]{2,1,0:T(8,128)(2,1)S(1)} %slice.96), channel_id=1, source_target_pairs={{0,32},{8,40},{16,48},{24,56},{32,64},{40,72},{48,80},{56,88},{64,... | collective-permute-start | bytes 786440 | tf_op jit(solution)/shard_map/ppermute | solution.py:288
  70.1 8.0 %collective-permute-start.13 = (bf16[2,128,512]{2,1,0:T(8,128)(2,1)S(1)}, bf16[2,128,512]{2,1,0:T(8,128)(2,1)}, u32[]{:S(2)}, u32[]{:S(2)}) collective-permute-start(bf16[2,128,512]{2,1,0:T(8,128)(2,1)S(1)} %slice.99), channel_id=1, source_target_pairs={{0,24},{8,0},{16,8},{24,16},{32,56},{40,32},{48,40},{56,48},{64,88... | collective-permute-start | bytes 786440 | tf_op jit(solution)/shard_map/ppermute | solution.py:294
  73.6 7.7 %collective-permute-start.11 = (bf16[2,128,512]{2,1,0:T(8,128)(2,1)S(1)}, bf16[2,128,512]{2,1,0:T(8,128)(2,1)}, u32[]{:S(2)}, u32[]{:S(2)}) collective-permute-start(bf16[2,128,512]{2,1,0:T(8,128)(2,1)S(1)} %slice.98), channel_id=1, source_target_pairs={{0,8},{8,16},{16,24},{24,0},{32,40},{40,48},{48,56},{56,32},{64,72... | collective-permute-start | bytes 786440 | tf_op jit(solution)/shard_map/ppermute | solution.py:294
  111.2 19.6 %collective-permute-start.23 = (bf16[2,128,512]{2,1,0:T(8,128)(2,1)}, bf16[2,128,512]{2,1,0:T(8,128)(2,1)S(1)}, u32[]{:S(2)}, u32[]{:S(2)}) collective-permute-start(bf16[2,128,512]{2,1,0:T(8,128)(2,1)} %get-tuple-element.35), channel_id=1, source_target_pairs={{0,8},{8,16},{16,24},{24,0},{32,40},{40,48},{48,56},{56,32},{64,72... | collective-permute-start | bytes 786440 | tf_op jit(solution)/shard_map/ppermute | solution.py:294
  111.3 68.4 %all-to-all-start.2 = ((bf16[8,2,128,512]{3,2,1,0:T(8,128)(2,1)}), bf16[8,2,128,512]{3,2,1,0:T(8,128)(2,1)S(1)}, u32[]{:S(2)}, u32[]{:S(2)}) async-start(bf16[8,2,128,512]{3,2,1,0:T(8,128)(2,1)} %get-tuple-element.21), calls=%async_computation.2 | async-start | bytes 4194304 | tf_op jit(solution)/shard_map/all_to_all | solution.py:324
  117.8 33.3 %collective-permute-start.14 = (bf16[2,128,512]{2,1,0:T(8,128)(2,1)S(1)}, bf16[2,128,512]{2,1,0:T(8,128)(2,1)S(1)}, u32[]{:S(2)}, u32[]{:S(2)}) collective-permute-start(bf16[2,128,512]{2,1,0:T(8,128)(2,1)S(1)} %copy-done.16), channel_id=1, source_target_pairs={{0,96},{8,104},{16,112},{24,120},{32,0},{40,8},{48,16},{56,24},{64... | collective-permute-start | bytes 786440 | tf_op jit(solution)/shard_map/ppermute | solution.py:288
  117.9 27.2 %collective-permute-start.16 = (bf16[2,128,512]{2,1,0:T(8,128)(2,1)S(1)}, bf16[2,128,512]{2,1,0:T(8,128)(2,1)S(1)}, u32[]{:S(2)}, u32[]{:S(2)}) collective-permute-start(bf16[2,128,512]{2,1,0:T(8,128)(2,1)S(1)} %copy-done.17), channel_id=1, source_target_pairs={{0,32},{8,40},{16,48},{24,56},{32,64},{40,72},{48,80},{56,88},{64,... | collective-permute-start | bytes 786440 | tf_op jit(solution)/shard_map/ppermute | solution.py:288
  127.5 9.1 %collective-permute-start.21 = (bf16[2,128,512]{2,1,0:T(8,128)(2,1)S(1)}, bf16[2,128,512]{2,1,0:T(8,128)(2,1)S(1)}, u32[]{:S(2)}, u32[]{:S(2)}) collective-permute-start(bf16[2,128,512]{2,1,0:T(8,128)(2,1)S(1)} %copy-done.19), channel_id=1, source_target_pairs={{0,24},{8,0},{16,8},{24,16},{32,56},{40,32},{48,40},{56,48},{64,88... | collective-permute-start | bytes 786440 | tf_op jit(solution)/shard_map/ppermute | solution.py:294
  130.8 21.1 %collective-permute-start.24 = (bf16[4,128,512]{2,1,0:T(8,128)(2,1)S(1)}, bf16[4,128,512]{2,1,0:T(8,128)(2,1)S(1)}, u32[]{:S(2)}, u32[]{:S(2)}) collective-permute-start(bf16[4,128,512]{2,1,0:T(8,128)(2,1)S(1)} %pad_maximum_fusion.5), channel_id=1, source_target_pairs={{0,8},{8,16},{16,24},{24,0},{32,40},{40,48},{48,56},{56,32},{64,72... | collective-permute-start | bytes 1572872 | tf_op jit(solution)/shard_map/ppermute | solution.py:294
  136.8 15.1 %collective-permute-start.22 = (bf16[4,128,512]{2,1,0:T(8,128)(2,1)S(1)}, bf16[4,128,512]{2,1,0:T(8,128)(2,1)S(1)}, u32[]{:S(2)}, u32[]{:S(2)}) collective-permute-start(bf16[4,128,512]{2,1,0:T(8,128)(2,1)S(1)} %pad_maximum_fusion.4), channel_id=1, source_target_pairs={{0,24},{8,0},{16,8},{24,16},{32,56},{40,32},{48,40},{56,48},{64,88... | collective-permute-start | bytes 1572872 | tf_op jit(solution)/shard_map/ppermute | solution.py:294
  145.2 22.0 %collective-permute-start.17 = (bf16[4,128,512]{2,1,0:T(8,128)(2,1)S(1)}, bf16[4,128,512]{2,1,0:T(8,128)(2,1)S(1)}, u32[]{:S(2)}, u32[]{:S(2)}) collective-permute-start(bf16[4,128,512]{2,1,0:T(8,128)(2,1)S(1)} %pad_maximum_fusion.3), channel_id=1, source_target_pairs={{0,32},{8,40},{16,48},{24,56},{32,64},{40,72},{48,80},{56,88},{64,... | collective-permute-start | bytes 1572872 | tf_op jit(solution)/shard_map/ppermute | solution.py:288
  151.2 15.9 %collective-permute-start.15 = (bf16[4,128,512]{2,1,0:T(8,128)(2,1)S(1)}, bf16[4,128,512]{2,1,0:T(8,128)(2,1)S(1)}, u32[]{:S(2)}, u32[]{:S(2)}) collective-permute-start(bf16[4,128,512]{2,1,0:T(8,128)(2,1)S(1)} %pad_maximum_fusion.2), channel_id=1, source_target_pairs={{0,96},{8,104},{16,112},{24,120},{32,0},{40,8},{48,16},{56,24},{64... | collective-permute-start | bytes 1572872 | tf_op jit(solution)/shard_map/ppermute | solution.py:288
  152.2 19.0 %collective-permute-start.25 = (bf16[128,512]{1,0:T(8,128)(2,1)S(1)}, bf16[128,512]{1,0:T(8,128)(2,1)S(1)}, u32[]{:S(2)}, u32[]{:S(2)}) collective-permute-start(bf16[128,512]{1,0:T(8,128)(2,1)S(1)} %get-tuple-element.45), channel_id=1, source_target_pairs={{0,96},{8,104},{16,112},{24,120},{32,0},{40,8},{48,16},{56,24},{64... | collective-permute-start | bytes 393224 | tf_op jit(solution)/shard_map/ppermute | solution.py:288
  162.5 10.2 %collective-permute-start.27 = (bf16[128,512]{1,0:T(8,128)(2,1)S(1)}, bf16[128,512]{1,0:T(8,128)(2,1)S(1)}, u32[]{:S(2)}, u32[]{:S(2)}) collective-permute-start(bf16[128,512]{1,0:T(8,128)(2,1)S(1)} %get-tuple-element.46), channel_id=1, source_target_pairs={{0,32},{8,40},{16,48},{24,56},{32,64},{40,72},{48,80},{56,88},{64,... | collective-permute-start | bytes 393224 | tf_op jit(solution)/shard_map/ppermute | solution.py:288
  162.5 10.2 %collective-permute-start.26 = (bf16[128,512]{1,0:T(8,128)(2,1)S(1)}, bf16[128,512]{1,0:T(8,128)(2,1)S(1)}, u32[]{:S(2)}, u32[]{:S(2)}) collective-permute-start(bf16[128,512]{1,0:T(8,128)(2,1)S(1)} %get-tuple-element.47), channel_id=1, source_target_pairs={{0,64},{8,72},{16,80},{24,88},{32,96},{40,104},{48,112},{56,120},{... | collective-permute-start | bytes 393224 | tf_op jit(solution)/shard_map/ppermute | solution.py:288
  167.4 7.0 %collective-permute-start.18 = (bf16[128,512]{1,0:T(8,128)(2,1)S(1)}, bf16[128,512]{1,0:T(8,128)(2,1)S(1)}, u32[]{:S(2)}, u32[]{:S(2)}) collective-permute-start(bf16[128,512]{1,0:T(8,128)(2,1)S(1)} %get-tuple-element.42), channel_id=1, source_target_pairs={{0,24},{8,0},{16,8},{24,16},{32,56},{40,32},{48,40},{56,48},{64,88... | collective-permute-start | bytes 393224 | tf_op jit(solution)/shard_map/ppermute | solution.py:294
  171.2 7.6 %collective-permute-start.20 = (bf16[128,512]{1,0:T(8,128)(2,1)S(1)}, bf16[128,512]{1,0:T(8,128)(2,1)S(1)}, u32[]{:S(2)}, u32[]{:S(2)}) collective-permute-start(bf16[128,512]{1,0:T(8,128)(2,1)S(1)} %get-tuple-element.43), channel_id=1, source_target_pairs={{0,8},{8,16},{16,24},{24,0},{32,40},{40,48},{48,56},{56,32},{64,72... | collective-permute-start | bytes 393224 | tf_op jit(solution)/shard_map/ppermute | solution.py:294
  171.2 7.6 %collective-permute-start.19 = (bf16[128,512]{1,0:T(8,128)(2,1)S(1)}, bf16[128,512]{1,0:T(8,128)(2,1)S(1)}, u32[]{:S(2)}, u32[]{:S(2)}) collective-permute-start(bf16[128,512]{1,0:T(8,128)(2,1)S(1)} %get-tuple-element.44), channel_id=1, source_target_pairs={{0,16},{8,24},{16,0},{24,8},{32,48},{40,56},{48,32},{56,40},{64,80... | collective-permute-start | bytes 393224 | tf_op jit(solution)/shard_map/ppermute | solution.py:294
  181.0 31.6 %all-to-all-start.3 = ((bf16[8,2,128,512]{3,2,1,0:T(8,128)(2,1)}), bf16[8,2,128,512]{3,2,1,0:T(8,128)(2,1)}, u32[]{:S(2)}, u32[]{:S(2)}) async-start(bf16[8,2,128,512]{3,2,1,0:T(8,128)(2,1)} %fusion.2), calls=%async_computation.3 | async-start | bytes 4194304 | tf_op jit(solution)/shard_map/all_to_all | solution.py:324
  (20 other events, 218.0 us)
